TPU v7x, 512 devices: a whole 4x4x16 slice. The times are simulated.
512 devices in a mesh: node: 32 (over x, z_lo, core), state: 16 (over y, z_hi).
Axes of the slice: x: 4, y: 4, z: 16 (z_hi: 4, z_lo: 4; z = z_hi * 4 + z_lo), core: 2. Of those that a mesh axis runs over, the one named last changes fastest.
Arguments:
- states: float32 [24576, 12288], P('node', 'state'), may hold values from -0.0390625 to 0.0390625
- coeffs: float32 [12288, 512], P('state'), may hold values from -6 to 6
- cell_matrix: float32 [384, 125, 125], P('node'), may hold values from -0.5 to 0.5
- connect: int32 [384, 125], P('node'), may hold values from 0 to 831, as said below
- face_list: int32 [2048], P('node'), may hold values from 0 to 767, as said below
- node_mass: float32 [24576], P('node'), may hold values from 0.25 to 4
Outputs:
- rotated: float32 [512, 24576], P('state', 'node')
- h_panel: float32 [512, 12288], P('node', 'state')
- m_panel: float32 [512, 12288], P('node', 'state')
Inputs may be any that keep to these rules, and one draw needn't show every extreme that they name: `connect`: within each partition the cells cover a periodic in-plane slab of hexahedral elements of order 4; indices 768 and above name ghosts, every ghost and every owned node is used by some cell. `face_list`: the 64 entries of one partition are distinct.
All inputs are finite; a program needn't handle non-finite values.
Results may differ from a plain program's by a relative error of at most 0.000084.
Values sent between devices are 32-bit elements; how exact they have to be, the bound alone decides.
No kernel may reach another device: no remote copies, remote signals or barrier semaphores. Data moves between devices by JAX's collectives and lax.ppermute only.
A program may use at most 64 MiB of HBM per device.

v0:
```python
import jax
import jax.numpy as jnp
from jax import lax
from jax.sharding import PartitionSpec as P


def shifted(shard, axis, by):
    length = lax.axis_size(axis)
    pairs = [(i, i + by) for i in range(length) if 0 <= i + by < length]
    return lax.ppermute(shard, axis, pairs)


def apply_cells(block_rows, cell_matrix, connect, face_list):
    height = block_rows.shape[0]
    owned_count = block_rows.shape[1]
    face_values = block_rows[:, face_list]
    ghosts = shifted(face_values, "node", -1)
    extended = jnp.concatenate([block_rows, ghosts], axis=1)
    cell_values = extended[:, connect]
    symmetric = 0.5 * (cell_matrix + jnp.swapaxes(cell_matrix, 1, 2))
    cell_output = jnp.einsum(
        "cab,rcb->rca", symmetric, cell_values, precision=lax.Precision.HIGHEST
    )
    assembled = (
        jnp.zeros(extended.shape, jnp.float32)
        .at[:, connect.reshape(-1)]
        .add(cell_output.reshape(height, -1))
    )
    returned = shifted(assembled[:, owned_count:], "node", 1)
    return assembled[:, :owned_count].at[:, face_list].add(returned)


def local(states, coeffs, cell_matrix, connect, face_list, node_mass):
    state_width = states.shape[1]
    rotated = lax.psum_scatter(
        lax.dot_general(
            coeffs,
            states,
            (((0,), (1,)), ((), ())),
            precision=lax.Precision.HIGHEST,
            preferred_element_type=jnp.float32,
        ),
        "state",
        scatter_dimension=0,
        tiled=True,
    )
    applied = apply_cells(rotated, cell_matrix, connect, face_list)
    stacked = jnp.stack([applied, rotated * node_mass[None, :]], 0)
    pieces = lax.all_gather(stacked, "state", axis=1, tiled=True)
    hamilton = jnp.dot(
        pieces[0], states, precision=lax.Precision.HIGHEST, preferred_element_type=jnp.float32
    )
    correlation = jnp.dot(
        pieces[1], states, precision=lax.Precision.HIGHEST, preferred_element_type=jnp.float32
    )
    partial_value = jnp.concatenate([hamilton, correlation], axis=1)
    own_rows = lax.psum_scatter(partial_value, "node", scatter_dimension=0, tiled=True)
    return (rotated, own_rows[:, :state_width], own_rows[:, state_width:])


def solution(mesh):
    return jax.shard_map(
        local,
        mesh=mesh,
        in_specs=(
            P("node", "state"),
            P("state", None),
            P("node", None, None),
            P("node", None),
            P("node"),
            P("node"),
        ),
        out_specs=(P("state", "node"), P("node", "state"), P("node", "state")),
        check_vma=False,
    )
```

profile of v0, /device:TPU:24, one launch (start us, length us, event | category | flops | bytes accessed | tf_op | source)
XLA Modules:
  0.0 458.6 jit_solution(17920757914317738274)
XLA Ops:
  7.2 1.6 copy-done
  8.8 10.0 %fusion.13 = f32[512,768]{1,0:T(8,128)} fusion(f32[768,512]{1,0:T(8,128)} %param.7, f32[768,768]{1,0:T(8,128)S(1)} %copy-done), kind=kOutput, calls=%fused_computation.29 | convolution fusion | flops 3623878656 | bytes 5505024 | tf_op jit(solution)/shard_map/dot_general | solution.py:36
  19.2 0.6 fusion.10
  19.8 119.4 %reduce-scatter.3.cloned.1.call-done = f32[32,768]{1,0:T(8,128)} async-done(((f32[512,768]{1,0:T(8,128)}), f32[32,768]{1,0:T(8,128)}) %reduce-scatter.3.cloned.1.call-update) | async-done | bytes 98320 | tf_op jit(solution)/shard_map/reduce_scatter | solution.py:35
  139.2 1.1 copy.15
  140.3 1.2 gather_fusion
  141.5 0.8 copy.16
  142.3 1.5 collective-permute-start
  143.8 0.6 pad_clamp_fusion
  144.4 1.2 copy.19
  145.6 0.9 pad_maximum_fusion.2
  146.5 0.2 copy.17
  146.7 3.2 gather_fusion.1
  149.9 0.9 copy.18
  150.8 1.2 reshape.56
  152.0 2.7 convolution_bitcast_fusion
  154.7 0.1 copy.21
  154.8 0.1 reshape.60
  154.9 1.2 copy.22
  156.1 9.2 %scatter_custom_fusion = f32[32,832]{0,1:T(8,128)S(1)} fusion(s32[1500]{0:T(1024)} %fusion.10, f32[1500,32]{1,0:T(8,128)} %copy.22, f32[]{:T(128)} %constant.5.clone.1), kind=kCustom, calls=%fused_computation.13 | custom fusion | flops 48000 | bytes 107008 | tf_op jit(solution)/shard_map/scatter-add | solution.py:27
  165.4 3.0 collective-permute-start.1
  168.5 0.8 collective-permute-done.1
  169.2 1.2 scatter_custom_fusion.1
  170.4 0.1 copy.23
  170.6 0.7 pad_maximum_fusion.1
  171.3 0.3 reduce-scatter.5.cloned.1.call-start
  171.6 116.3 %all-gather.2.cloned.1.call-done = f32[2,512,768]{2,1,0:T(8,128)} async-done(((f32[2,32,768]{2,1,0:T(8,128)}), f32[2,512,768]{2,1,0:T(8,128)}) %all-gather.2.cloned.1.call-update) | async-done | bytes 3145744 | tf_op jit(solution)/shard_map/all_gather | solution.py:49
  287.8 5.6 %fusion = f32[512,768]{1,0:T(8,128)S(1)} fusion(f32[768,768]{1,0:T(8,128)S(1)} %copy-done, f32[2,512,768]{2,1,0:T(8,128)} %all-gather.2.cloned.1.call-done), kind=kOutput, calls=%fused_computation.6 | convolution fusion | flops 3623878656 | bytes 5505024 | tf_op jit(solution)/shard_map/dot_general | solution.py:53
  293.4 4.0 fusion.1
  297.5 2.0 pad_maximum_fusion
  299.5 151.1 %reduce-scatter.5.cloned.1.call-done = f32[16,1536]{1,0:T(8,128)} async-done(((f32[512,1536]{1,0:T(8,128)}), f32[16,1536]{1,0:T(8,128)}) %reduce-scatter.5.cloned.1.call-update) | async-done | bytes 98320 | tf_op jit(solution)/shard_map/reduce_scatter | solution.py:57
  450.6 1.5 fusion.12
  (29 shorter events, 0.4 us)
Async XLA Ops:
  7.2 1.7 copy-start
  7.2 11.8 %copy-start.4 = (s32[12,125]{1,0:T(8,128)S(1)}, s32[12,125]{1,0:T(8,128)}, u32[]{:S(2)}) copy-start(s32[12,125]{1,0:T(8,128)} %param.9) | copy-start | bytes 18004
  7.2 12.0 %copy-start.7 = (s32[64]{0:T(128)S(1)}, s32[64]{0:T(128)}, u32[]{:S(2)}) copy-start(s32[64]{0:T(128)} %param.10) | copy-start | bytes 772
  7.2 132.0 %reduce-scatter.3.cloned.1.call-start = ((), (), s32[]{:S(2)}) async-start(), calls=%async_computation.2 | async-start | bytes 1671168 | tf_op jit(solution)/shard_map/reduce_scatter | solution.py:35
  18.9 125.5 %copy-start.1 = (f32[12,125,125]{2,1,0:T(8,128)S(1)}, f32[12,125,125]{2,1,0:T(8,128)}, u32[]{:S(2)}) copy-start(f32[12,125,125]{2,1,0:T(8,128)} %param.8) | copy-start | bytes 2250004
  18.9 268.9 %all-gather.2.cloned.1.call-start = ((), (), s32[]{:S(2)}) async-start(), calls=%async_computation.3 | async-start | bytes 3342336 | tf_op jit(solution)/shard_map/all_gather | solution.py:49
  19.2 0.6 copy-start.6
  142.3 3.3 collective-permute-start
  150.8 17.6 %copy-start.3 = (f32[32,768]{1,0:T(8,128)S(1)}, f32[32,768]{1,0:T(8,128)}, u32[]{:S(2)}) copy-start(f32[32,768]{1,0:T(8,128)} %reduce-scatter.3.cloned.1.call-done) | copy-start | bytes 294916
  150.8 17.6 %copy-start.5 = (f32[768]{0:T(1024)S(1)}, f32[768]{0:T(1024)}, u32[]{:S(2)}) copy-start(f32[768]{0:T(1024)} %param.11) | copy-start | bytes 9220
  165.4 3.9 collective-permute-start.1
  171.3 279.3 %reduce-scatter.5.cloned.1.call-start = ((), (), s32[]{:S(2)}) async-start(), calls=%async_computation.4 | async-start | bytes 3244032 | tf_op jit(solution)/shard_map/reduce_scatter | solution.py:57
  287.8 5.6 %copy-start.2 = (f32[2,512,768]{2,1,0:T(8,128)S(1)}, f32[2,512,768]{2,1,0:T(8,128)}, u32[]{:S(2)}) copy-start(f32[2,512,768]{2,1,0:T(8,128)} %all-gather.2.cloned.1.call-done) | copy-start | bytes 9437188
Sparse Core Ops, SparseCore 0:
  19.0 120.1 reduce-scatter.2
  171.4 116.3 all-gather.1
  299.7 150.9 reduce-scatter.4
where the time goes:
time: 459 us
  waiting for transfers between devices  388 us (85%)
  matrix products  22.3 us (5%)
  other arithmetic  15.3 us (3%)
  local copies, waits for them, and re-layouts  14.6 us (3%)
  between operations  14 us (3%)
  starting transfers between devices  4.85 us (1%)
    reduce_scatter x1, waiting for transfers between devices, local(): lax.psum_scatter(partial_value, 'node', scatter_dimension=0, tiled=True)  151 us
    reduce_scatter x1, waiting for transfers between devices, local(): lax.psum_scatter(lax.dot_general(coeffs, states, (((0,), (1,)), ((), ()))...  119 us
    all_gather x1, waiting for transfers between devices, local(): pieces = lax.all_gather(stacked, 'state', axis=1, tiled=True)  116 us
    dot_general x1, matrix products, local(): lax.dot_general(coeffs, states, (((0,), (1,)), ((), ())), precision=lax.P...  10 us
    scatter-add x1, other arithmetic, apply_cells(): assembled = jnp.zeros(extended.shape, jnp.float32).at[:, connect.reshape(...  9.24 us
  transfers between devices with their start and end apart: 5, of which 4 were waited for; matrix products, arithmetic and copies ran while one was open for 1% of the time, Pallas kernels for 0%

commit v1 on v0

v1 whole, which is shorter than its diff:
```python
import jax
import jax.numpy as jnp
from jax import lax
from jax.sharding import Mesh, PartitionSpec as P

FINE = ("x", "zl", "core", "y", "zh")
NODE = ("x", "zl", "core")
STATE = ("y", "zh")
HIGH = lax.Precision.HIGH


def node_shift(shard, by):
    length = lax.axis_size(NODE)
    pairs = [(i, i + by) for i in range(length) if 0 <= i + by < length]
    return lax.ppermute(shard, NODE, pairs)


def ring(shard, axis, by):
    length = lax.axis_size(axis)
    return lax.ppermute(shard, axis, [(i, (i + by) % length) for i in range(length)])


def halves(value):
    top = lax.reduce_precision(value, 8, 7)
    return top.astype(jnp.bfloat16), (value - top).astype(jnp.bfloat16)


def pick(table, value, dims):
    top, low = halves(value)
    dot = lambda part: lax.dot_general(
        table, part, (dims, ((), ())), preferred_element_type=jnp.float32
    )
    return dot(top) + dot(low)


def apply_cells(values, cell_matrix, connect, face_list):
    owned, width = values.shape
    cells, per_cell = connect.shape
    face = face_list.shape[0]
    face_table = (face_list[:, None] == jnp.arange(owned)[None, :]).astype(jnp.bfloat16)
    table = (
        connect.reshape(-1)[:, None] == jnp.arange(owned + face)[None, :]
    ).astype(jnp.bfloat16)
    ghosts = node_shift(pick(face_table, values, ((1,), (0,))), -1)
    extended = jnp.concatenate([values, ghosts], axis=0)
    cell_values = pick(table, extended, ((1,), (0,))).reshape(cells, per_cell, width)
    symmetric = 0.5 * (cell_matrix + jnp.swapaxes(cell_matrix, 1, 2))
    cell_output = jnp.einsum("cab,cbr->car", symmetric, cell_values, precision=HIGH)
    assembled = pick(table, cell_output.reshape(cells * per_cell, width), ((0,), (0,)))
    returned = node_shift(assembled[owned:], 1)
    return assembled[:owned] + pick(face_table, returned, ((0,), (0,)))


def spread_sum(pieces, axis):
    return jnp.sum(lax.all_to_all(pieces, axis, 0, 0, tiled=True), axis=0)


def gather_rows(rows, axis):
    length = lax.axis_size(axis)
    here = lax.axis_index(axis)
    out = jnp.zeros((length,) + rows.shape, rows.dtype)
    out = lax.dynamic_update_slice_in_dim(out, rows[None], here, 0)
    for by in (1, length - 1, 2):
        out = lax.dynamic_update_slice_in_dim(
            out, ring(rows, axis, by)[None], (here - by) % length, 0
        )
    return out


def local(states, coeffs, cell_matrix, connect, face_list, node_mass):
    owned, width = states.shape
    block = coeffs.shape[1]
    partial = lax.dot_general(
        coeffs,
        states,
        (((0,), (1,)), ((), ())),
        precision=HIGH,
        preferred_element_type=jnp.float32,
    )
    over_y = spread_sum(partial.reshape(4, block // 4, owned), "y")
    rotated = spread_sum(over_y.reshape(4, block // 16, owned), "zh")

    weighted = jnp.concatenate(
        [
            apply_cells(states, cell_matrix, connect, face_list),
            states * node_mass[:, None],
        ],
        axis=1,
    )

    group = lax.all_gather(rotated, "zh", axis=0, tiled=False)
    rows = gather_rows(group, "y")
    rows = rows.reshape(16, 2, block // 32, owned).swapaxes(0, 1).reshape(block, owned)
    panel = jnp.dot(rows, weighted, precision=HIGH, preferred_element_type=jnp.float32)
    panel = spread_sum(panel.reshape(2, block // 2, 2 * width), "core")
    panel = spread_sum(panel.reshape(4, block // 8, 2 * width), "x")
    panel = spread_sum(panel.reshape(4, block // 32, 2 * width), "zl")
    return rotated, panel[:, :width], panel[:, width:]


def solution(mesh):
    fine = Mesh(mesh.devices.reshape(4, 4, 2, 4, 4), FINE)
    return jax.shard_map(
        local,
        mesh=fine,
        in_specs=(
            P(NODE, STATE),
            P(STATE, None),
            P(NODE, None, None),
            P(NODE, None),
            P(NODE),
            P(NODE),
        ),
        out_specs=(P(STATE, NODE), P(NODE, STATE), P(NODE, STATE)),
        check_vma=False,
    )
```

time: 459 us -> 194 us (0.42)
  waiting for transfers between devices: 388 us -> 19.3 us
  blocking collectives: 0 us -> 71.5 us
  starting transfers between devices: 4.85 us -> 32.7 us
  matrix products: 22.3 us -> 41.7 us
  between operations: 14 us -> 0.99 us
  other arithmetic: 15.3 us -> 8.82 us
    reduce_scatter x2 -> x0, waiting for transfers between devices: 271 us -> none  [the longest x1 151 us: local(): lax.psum_scatter(partial_value, 'node', scatter_dimension=0, tiled=True)]
    all_gather x1 -> x0, waiting for transfers between devices: 116 us -> none  [local(): pieces = lax.all_gather(stacked, 'state', axis=1, tiled=True)]
    all_to_all x0 -> x3, blocking collectives: none -> 45.8 us  [spread_sum(): return jnp.sum(lax.all_to_all(pieces, axis, 0, 0, tiled=True), axis=0)]
    all_gather x0 -> x1, blocking collectives: none -> 25.7 us  [local(): group = lax.all_gather(rotated, 'zh', axis=0, tiled=False)]
    all_to_all x0 -> x2, starting transfers between devices: none -> 20 us  [spread_sum(): return jnp.sum(lax.all_to_all(pieces, axis, 0, 0, tiled=True), axis=0)]
    dot_general x4 -> x11, matrix products: 22.3 us -> 41.7 us  [the longest x8 25.3 us: pick(): lax.dot_general(table, part, (dims, ((), ())), preferred_element_type=jnp...]
    ppermute x2 -> x5, waiting for transfers between devices: 0.77 us -> 12.5 us  [the longest x3 11.5 us: ring(): lax.ppermute(shard, axis, [(i, (i + by) % length) for i in range(length)])]
    scatter-add x2 -> x0, other arithmetic: 10.4 us -> none  [the longest x1 9.24 us: apply_cells(): assembled = jnp.zeros(extended.shape, jnp.float32).at[:, connect.reshape(...]
  transfers between devices with their start and end apart: 5 -> 7, of which waited for: 4 -> 4; matrix products, arithmetic and copies ran while one was open for 1% -> 27% of each run, Pallas kernels for 0% -> 0%
where the time goes in v1:
time: 194 us; the launch traced here: 191 us
  blocking collectives  71.5 us (37%)
  matrix products  41.7 us (21%)
  starting transfers between devices  32.7 us (17%)
  waiting for transfers between devices  19.3 us (10%)
  local copies, waits for them, and re-layouts  16.1 us (8%)
  other arithmetic  8.82 us (5%)
    all_to_all x3, blocking collectives, spread_sum(): return jnp.sum(lax.all_to_all(pieces, axis, 0, 0, tiled=True), axis=0)  45.8 us
    all_gather x1, blocking collectives, local(): group = lax.all_gather(rotated, 'zh', axis=0, tiled=False)  25.7 us
    dot_general x8, matrix products, pick(): lax.dot_general(table, part, (dims, ((), ())), preferred_element_type=jnp...  25.3 us
    all_to_all x2, starting transfers between devices, spread_sum(): return jnp.sum(lax.all_to_all(pieces, axis, 0, 0, tiled=True), axis=0)  20 us
    ppermute x3, waiting for transfers between devices, ring(): lax.ppermute(shard, axis, [(i, (i + by) % length) for i in range(length)])  11.5 us
    ppermute x3, starting transfers between devices, ring(): lax.ppermute(shard, axis, [(i, (i + by) % length) for i in range(length)])  9.2 us
    dot_general x1, matrix products, apply_cells(): jnp.einsum('cab,cbr->car', symmetric, cell_values, precision=HIGH)  7.22 us
    all_to_all x2, waiting for transfers between devices, spread_sum(): return jnp.sum(lax.all_to_all(pieces, axis, 0, 0, tiled=True), axis=0)  6.84 us
  transfers between devices with their start and end apart: 7, of which 4 were waited for; matrix products, arithmetic and copies ran while one was open for 27% of the time, Pallas kernels for 0%

profile of v1, /device:TPU:24, one launch (start us, length us, event | category | flops | bytes accessed | tf_op | source)
XLA Modules:
  0.0 191.3 jit_solution(4113627333422660496)
XLA Ops:
  0.7 2.2 %fusion.18 = f32[64,768]{1,0:T(8,128)S(1)} fusion(f32[768,768]{1,0:T(8,128)} %param.6, s32[64]{0:T(128)} %param.10), kind=kOutput, calls=%fused_computation.25 | convolution fusion | flops 77316096 | bytes 2556160 | tf_op jit(solution)/shard_map/dot_general | solution.py:30
  3.6 1.3 collective-permute-start.3
  4.9 5.2 %fusion.36 = f32[512,768]{1,0:T(8,128)} fusion(f32[768,512]{1,0:T(8,128)S(1)} %copy-done, f32[768,768]{1,0:T(8,128)S(1)} %copy-done.1), kind=kOutput, calls=%fused_computation.51 | convolution fusion | flops 1811939328 | bytes 5505024 | tf_op jit(solution)/shard_map/dot_general | solution.py:73
  10.1 9.3 %all-to-all-start = ((f32[4,128,768]{2,1,0:T(8,128)}), f32[4,128,768]{2,1,0:T(8,128)S(1)}, u32[]{:S(2)}, u32[]{:S(2)}) async-start(f32[4,128,768]{2,1,0:T(8,128)} %bitcast.31), calls=%async_computation | async-start | bytes 3145728 | tf_op jit(solution)/shard_map/all_to_all | solution.py:55
  19.4 4.1 %constant_dynamic-update-slice_fusion.1 = (f32[832,768]{1,0:T(8,128)}, f32[768,768]{1,0:T(8,128)}) fusion(f32[768,768]{1,0:T(8,128)} %param.6, f32[768]{0:T(1024)S(1)} %copy-done.9), kind=kLoop, calls=%fused_computation.46 | loop fusion | flops 589823 | bytes 7080960
  23.6 2.3 %copy.16 = f32[12,125,125]{1,2,0:T(8,128)} copy(f32[12,125,125]{2,1,0:T(8,128)} %param.8) | data formatting | bytes 1500000 | tf_op args[2]
  26.6 4.7 %fusion.2 = f32[1500,768]{1,0:T(8,128)S(1)} fusion(s32[1500]{0:T(1024)S(1)} %eq.32, f32[832,768]{1,0:T(8,128)} %constant_dynamic-update-slice_fusion), kind=kOutput, calls=%fused_computation.5 | convolution fusion | flops 1920092928 | bytes 7169904 | tf_op jit(solution)/shard_map/dot_general | solution.py:30
  31.3 5.0 %fusion.8 = f32[1500,768]{1,0:T(8,128)} fusion(f32[1500,768]{1,0:T(8,128)S(1)} %fusion.2, s32[1500]{0:T(1024)S(1)} %eq.32, f32[832,768]{1,0:T(8,128)S(1)} %copy-done.4), kind=kOutput, calls=%fused_computation.12 | convolution fusion | flops 1920605952 | bytes 11777904 | tf_op jit(solution)/shard_map/dot_general | solution.py:30
  36.3 4.4 %reshape.37 = f32[12,125,768]{2,1,0:T(8,128)} reshape(f32[1500,768]{1,0:T(8,128)} %fusion.8) | data formatting | bytes 9216000 | tf_op jit(solution)/shard_map/reshape | solution.py:46
  40.7 7.2 %fusion.23 = f32[12,125,768]{2,1,0:T(8,128)} fusion(f32[12,125,768]{2,1,0:T(8,128)} %reshape.37, f32[12,125,125]{2,1,0:T(8,128)} %param.8, f32[12,125,125]{1,2,0:T(8,128)} %copy.16), kind=kOutput, calls=%fused_computation.31 | convolution fusion | flops 864375040 | bytes 10716000 | tf_op jit(solution)/shard_map/cab,cbr->car/dot_general | solution.py:48
  47.9 4.4 %reshape.38 = f32[1500,768]{1,0:T(8,128)} reshape(f32[12,125,768]{2,1,0:T(8,128)} %fusion.23) | data formatting | bytes 9216000 | tf_op jit(solution)/shard_map/reshape | solution.py:49
  53.1 10.8 %all-to-all-start.1 = ((f32[4,32,768]{2,1,0:T(8,128)}), f32[4,32,768]{2,1,0:T(8,128)S(1)}, u32[]{:S(2)}, u32[]{:S(2)}) async-start(f32[4,32,768]{2,1,0:T(8,128)} %bitcast.1), calls=%async_computation.1 | async-start | bytes 786432 | tf_op jit(solution)/shard_map/all_to_all | solution.py:55
  63.9 5.2 %fusion = f32[832,768]{1,0:T(8,128)S(1)} fusion(s32[1500]{0:T(1024)S(1)} %eq.32, f32[1500,768]{1,0:T(8,128)} %reshape.38), kind=kOutput, calls=%fused_computation.3 | convolution fusion | flops 1921632000 | bytes 7169904 | tf_op jit(solution)/shard_map/dot_general | solution.py:30
  69.2 2.8 %fusion.16 = f32[832,768]{1,0:T(8,128)S(1)} fusion(f32[832,768]{1,0:T(8,128)S(1)} %fusion, f32[1500,768]{1,0:T(8,128)S(1)} %bitcast.33, s32[1500]{0:T(1024)S(1)} %eq.32), kind=kOutput, calls=%fused_computation.24 | convolution fusion | flops 1921118976 | bytes 9725808 | tf_op jit(solution)/shard_map/dot_general | solution.py:30
  72.0 1.5 copy-done.3
  73.5 2.2 %collective-permute-start.4 = (f32[64,768]{1,0:T(8,128)S(1)}, f32[64,768]{1,0:T(8,128)S(1)}, u32[]{:S(2)}, u32[]{:S(2)}) collective-permute-start(f32[64,768]{1,0:T(8,128)S(1)} %slice.17), channel_id=1, source_target_pairs={{0,16},{16,32},{32,48},{48,64},{64,80},{80,96},{96,112},{112,128},... | collective-permute-start | bytes 589832 | tf_op jit(solution)/shard_map/ppermute | solution.py:15
  75.8 1.0 collective-permute-done.4
  76.8 2.0 %fusion.27 = f32[768,768]{1,0:T(8,128)} fusion(f32[64,768]{1,0:T(8,128)S(1)} %collective-permute-done.4, s32[64]{0:T(128)S(1)} %copy-done.8), kind=kOutput, calls=%fused_computation.40 | convolution fusion | flops 75694080 | bytes 2556160 | tf_op jit(solution)/shard_map/dot_general | solution.py:30
  78.8 6.8 %all-to-all-done.1 = f32[4,32,768]{2,1,0:T(8,128)S(1)} async-done(((f32[4,32,768]{2,1,0:T(8,128)}), f32[4,32,768]{2,1,0:T(8,128)S(1)}, u32[]{:S(2)}, u32[]{:S(2)}) %all-to-all-start.1) | async-done | bytes 393248 | tf_op jit(solution)/shard_map/all_to_all | solution.py:55
  85.7 25.7 %all-gather = f32[128,768]{1,0:T(8,128)S(1)} all-gather(f32[32,768]{1,0:T(8,128)S(1)} %reduce_sum.46), channel_id=2, replica_groups=mesh['x'=4,'zl'=4,'core'=2,'y'=4,'zh'=4] {'zh'}, dimensions={0}, use_global_device_ids=true | all-gather | bytes 491520 | tf_op jit(solution)/shard_map/all_gather | solution.py:91
  111.4 2.8 %collective-permute-start.1 = (f32[4,32,768]{2,1,0:T(8,128)S(1)}, f32[4,32,768]{2,1,0:T(8,128)S(1)}, u32[]{:S(2)}, u32[]{:S(2)}) collective-permute-start(f32[4,32,768]{2,1,0:T(8,128)S(1)} %bitcast.35), channel_id=1, source_target_pairs={{0,12},{4,0},{8,4},{12,8},{1,13},{5,1},{9,5},{13,9},{2,14},{6,2},{... | collective-permute-start | bytes 1179656 | tf_op jit(solution)/shard_map/ppermute | solution.py:20
  114.2 4.3 %collective-permute-start = (f32[4,32,768]{2,1,0:T(8,128)S(1)}, f32[4,32,768]{2,1,0:T(8,128)S(1)}, u32[]{:S(2)}, u32[]{:S(2)}) collective-permute-start(f32[4,32,768]{2,1,0:T(8,128)S(1)} %bitcast.36), channel_id=1, source_target_pairs={{0,4},{4,8},{8,12},{12,0},{1,5},{5,9},{9,13},{13,1},{2,6},{6,10},{... | collective-permute-start | bytes 1179656 | tf_op jit(solution)/shard_map/ppermute | solution.py:20
  118.5 3.0 %slice_add_fusion = f32[768,768]{1,0:T(8,128)S(1)} fusion(f32[832,768]{1,0:T(8,128)} %copy-done.3, f32[768,768]{1,0:T(8,128)} %fusion.27, f32[64,768]{1,0:T(8,128)S(1)} %collective-permute-done.4, s32[64]{0:T(128)S(1)} %copy-done.8), kind=kOutput, calls=%fused_computation.23 | convolution fusion | flops 76824576 | bytes 7274752 | tf_op jit(solution)/shard_map/dot_general | solution.py:30
  121.4 2.2 %collective-permute-start.2 = (f32[4,32,768]{2,1,0:T(8,128)S(1)}, f32[4,32,768]{2,1,0:T(8,128)S(1)}, u32[]{:S(2)}, u32[]{:S(2)}) collective-permute-start(f32[4,32,768]{2,1,0:T(8,128)S(1)} %bitcast.37), channel_id=1, source_target_pairs={{0,8},{4,12},{8,0},{12,4},{1,9},{5,13},{9,1},{13,5},{2,10},{6,14},... | collective-permute-start | bytes 1179656 | tf_op jit(solution)/shard_map/ppermute | solution.py:20
  123.8 11.5 %collective-permute-done = f32[4,32,768]{2,1,0:T(8,128)S(1)} collective-permute-done((f32[4,32,768]{2,1,0:T(8,128)S(1)}, f32[4,32,768]{2,1,0:T(8,128)S(1)}, u32[]{:S(2)}, u32[]{:S(2)}) %collective-permute-start) | collective-permute-done | bytes 393248 | tf_op jit(solution)/shard_map/ppermute | solution.py:20
  135.6 1.4 copy-done.2
  137.0 4.0 %fusion.4 = f32[2,256,1536]{2,1,0:T(8,128)S(1)} fusion(f32[2,256,768]{2,1,0:T(8,128)S(1)} %bitcast.28, f32[768,768]{1,0:T(8,128)S(1)} %copy-done.2, f32[768,768]{1,0:T(8,128)S(1)} %slice_add_fusion), kind=kOutput, calls=%fused_computation.8 | convolution fusion | flops 3625058304 | bytes 9437184 | tf_op jit(solution)/shard_map/dot_general | solution.py:94
  141.0 7.2 %all_to_all.25 = f32[2,256,1536]{2,1,0:T(8,128)} all-to-all(f32[2,256,1536]{2,1,0:T(8,128)S(1)} %fusion.4), channel_id=1, replica_groups=mesh['x'=4,'zl'=4,'core'=2,'y'=4,'zh'=4] {'core'}, dimensions={0} | all-to-all | bytes 6291456 | tf_op jit(solution)/shard_map/all_to_all | solution.py:55
  148.2 2.3 %reduce_sum.47 = f32[256,1536]{1,0:T(8,128)S(1)} reduce(f32[2,256,1536]{2,1,0:T(8,128)} %all_to_all.25, f32[]{:T(128)} %constant.31.clone.1), dimensions={0}, to_apply=%region_2.3 | reduce | flops 393216 | bytes 4718596 | tf_op jit(solution)/shard_map/reduce_sum | solution.py:55
  150.5 24.5 %all_to_all.26 = f32[4,64,1536]{2,1,0:T(8,128)} all-to-all(f32[4,64,1536]{2,1,0:T(8,128)S(1)} %bitcast.30), channel_id=1, replica_groups=mesh['x'=4,'zl'=4,'core'=2,'y'=4,'zh'=4] {'x'}, dimensions={0} | all-to-all | bytes 3145728 | tf_op jit(solution)/shard_map/all_to_all | solution.py:55
  174.9 1.5 reduce_sum.48
  176.5 14.1 %all_to_all.27 = f32[4,16,1536]{2,1,0:T(8,128)S(1)} all-to-all(f32[4,16,1536]{2,1,0:T(8,128)S(1)} %bitcast.34), channel_id=1, replica_groups=mesh['x'=4,'zl'=4,'core'=2,'y'=4,'zh'=4] {'zl'}, dimensions={0} | all-to-all | bytes 786432 | tf_op jit(solution)/shard_map/all_to_all | solution.py:55
  (41 shorter events, 3.5 us)
Async XLA Ops:
  0.6 4.2 %copy-start = (f32[768,512]{1,0:T(8,128)S(1)}, f32[768,512]{1,0:T(8,128)}, u32[]{:S(2)}) copy-start(f32[768,512]{1,0:T(8,128)} %param.7) | copy-start | bytes 4718596
  0.6 2.3 %copy-start.7 = (s32[64]{0:T(128)S(1)}, s32[64]{0:T(128)}, u32[]{:S(2)}) copy-start(s32[64]{0:T(128)} %param.10) | copy-start | bytes 772
  0.7 2.5 %copy-start.1 = (f32[768,768]{1,0:T(8,128)S(1)}, f32[768,768]{1,0:T(8,128)}, u32[]{:S(2)}) copy-start(f32[768,768]{1,0:T(8,128)} %param.6) | copy-start | bytes 7077892
  3.6 22.4 %collective-permute-start.3 = (f32[64,768]{1,0:T(8,128)S(1)}, f32[64,768]{1,0:T(8,128)S(1)}, u32[]{:S(2)}, u32[]{:S(2)}) collective-permute-start(f32[64,768]{1,0:T(8,128)S(1)} %fusion.21), channel_id=1, source_target_pairs={{16,0},{32,16},{48,32},{64,48},{80,64},{96,80},{112,96},{128,112},... | collective-permute-start | bytes 589832 | tf_op jit(solution)/shard_map/ppermute | solution.py:15
  10.1 9.3 %copy-start.9 = (f32[768]{0:T(1024)S(1)}, f32[768]{0:T(1024)}, u32[]{:S(2)}) copy-start(f32[768]{0:T(1024)} %param.11) | copy-start | bytes 9220
  10.1 42.2 %all-to-all-start = ((f32[4,128,768]{2,1,0:T(8,128)}), f32[4,128,768]{2,1,0:T(8,128)S(1)}, u32[]{:S(2)}, u32[]{:S(2)}) async-start(f32[4,128,768]{2,1,0:T(8,128)} %bitcast.31), calls=%async_computation | async-start | bytes 3145728 | tf_op jit(solution)/shard_map/all_to_all | solution.py:55
  19.4 4.1 %copy-start.6 = (s32[12,125]{1,0:T(8,128)S(1)}, s32[12,125]{1,0:T(8,128)}, u32[]{:S(2)}) copy-start(s32[12,125]{1,0:T(8,128)} %param.9) | copy-start | bytes 18004
  26.6 4.7 %copy-start.4 = (f32[832,768]{1,0:T(8,128)S(1)}, f32[832,768]{1,0:T(8,128)}, u32[]{:S(2)}) copy-start(f32[832,768]{1,0:T(8,128)} %constant_dynamic-update-slice_fusion) | copy-start | bytes 7667716
  53.1 16.0 %slice-start = ((s8[4620288]{0:T(1024)(128)(4,1)}), s8[425984]{0:T(1024)(128)(4,1)S(1)}, s32[]{:S(2)}) async-start(s8[4620288]{0:T(1024)(128)(4,1)} %bitcast.32), calls=%async_computation.5 | async-start | bytes 851968
  53.1 32.5 %all-to-all-start.1 = ((f32[4,32,768]{2,1,0:T(8,128)}), f32[4,32,768]{2,1,0:T(8,128)S(1)}, u32[]{:S(2)}, u32[]{:S(2)}) async-start(f32[4,32,768]{2,1,0:T(8,128)} %bitcast.1), calls=%async_computation.1 | async-start | bytes 786432 | tf_op jit(solution)/shard_map/all_to_all | solution.py:55
  63.9 5.2 %slice-start.1 = ((s8[4620288]{0:T(1024)(128)(4,1)}), s8[4194304]{0:T(1024)(128)(4,1)S(1)}, s32[]{:S(2)}) async-start(s8[4620288]{0:T(1024)(128)(4,1)} %bitcast.32), calls=%async_computation.6 | async-start | bytes 8388608
  69.2 7.6 %copy-start.8 = (s32[64]{0:T(128)S(1)}, s32[64]{0:T(128)}, u32[]{:S(2)}) copy-start(s32[64]{0:T(128)} %param.10) | copy-start | bytes 772
  72.0 1.5 copy-start.3
  73.5 3.3 %collective-permute-start.4 = (f32[64,768]{1,0:T(8,128)S(1)}, f32[64,768]{1,0:T(8,128)S(1)}, u32[]{:S(2)}, u32[]{:S(2)}) collective-permute-start(f32[64,768]{1,0:T(8,128)S(1)} %slice.17), channel_id=1, source_target_pairs={{0,16},{16,32},{32,48},{48,64},{64,80},{80,96},{96,112},{112,128},... | collective-permute-start | bytes 589832 | tf_op jit(solution)/shard_map/ppermute | solution.py:15
  85.7 35.8 %copy-start.5 = (f32[32,768]{1,0:T(8,128)}, f32[32,768]{1,0:T(8,128)S(1)}, u32[]{:S(2)}) copy-start(f32[32,768]{1,0:T(8,128)S(1)} %reduce_sum.46) | copy-start | bytes 294916
  111.4 23.9 %collective-permute-start.1 = (f32[4,32,768]{2,1,0:T(8,128)S(1)}, f32[4,32,768]{2,1,0:T(8,128)S(1)}, u32[]{:S(2)}, u32[]{:S(2)}) collective-permute-start(f32[4,32,768]{2,1,0:T(8,128)S(1)} %bitcast.35), channel_id=1, source_target_pairs={{0,12},{4,0},{8,4},{12,8},{1,13},{5,1},{9,5},{13,9},{2,14},{6,2},{... | collective-permute-start | bytes 1179656 | tf_op jit(solution)/shard_map/ppermute | solution.py:20
  114.2 21.1 %collective-permute-start = (f32[4,32,768]{2,1,0:T(8,128)S(1)}, f32[4,32,768]{2,1,0:T(8,128)S(1)}, u32[]{:S(2)}, u32[]{:S(2)}) collective-permute-start(f32[4,32,768]{2,1,0:T(8,128)S(1)} %bitcast.36), channel_id=1, source_target_pairs={{0,4},{4,8},{8,12},{12,0},{1,5},{5,9},{9,13},{13,1},{2,6},{6,10},{... | collective-permute-start | bytes 1179656 | tf_op jit(solution)/shard_map/ppermute | solution.py:20
  121.4 14.0 %collective-permute-start.2 = (f32[4,32,768]{2,1,0:T(8,128)S(1)}, f32[4,32,768]{2,1,0:T(8,128)S(1)}, u32[]{:S(2)}, u32[]{:S(2)}) collective-permute-start(f32[4,32,768]{2,1,0:T(8,128)S(1)} %bitcast.37), channel_id=1, source_target_pairs={{0,8},{4,12},{8,0},{12,4},{1,9},{5,13},{9,1},{13,5},{2,10},{6,14},... | collective-permute-start | bytes 1179656 | tf_op jit(solution)/shard_map/ppermute | solution.py:20
  135.3 1.7 copy-start.2

commit v2 on v1

v2 whole, which is shorter than its diff:
```python
import functools

import jax
import jax.numpy as jnp
from jax import lax
from jax.experimental import pallas as pl
from jax.experimental.pallas import tpu as pltpu
from jax.sharding import Mesh, PartitionSpec as P

FINE = ("x", "zl", "core", "y", "zh")
NODE = ("x", "zl", "core")
STATE = ("y", "zh")
VMEM = 40 * 1024 * 1024
F32 = jnp.float32
BF16 = jnp.bfloat16


def node_shift(shard, by):
    length = lax.axis_size(NODE)
    pairs = [(i, i + by) for i in range(length) if 0 <= i + by < length]
    return lax.ppermute(shard, NODE, pairs)


def ring(shard, axis, by):
    length = lax.axis_size(axis)
    return lax.ppermute(shard, axis, [(i, (i + by) % length) for i in range(length)])


def halves(value):
    top = lax.reduce_precision(value, 8, 7)
    return top.astype(BF16), (value - top).astype(BF16)


def split(value):
    top = value.astype(BF16)
    return top, (value - top.astype(F32)).astype(BF16)


def dot(left, right, dims=((1,), (0,))):
    return lax.dot_general(left, right, (dims, ((), ())), preferred_element_type=F32)


def rotate_kernel(coeffs_ref, states_ref, out_ref, top_ref, low_ref):
    @pl.when(pl.program_id(0) == 0)
    def _():
        top, low = split(coeffs_ref[...].T)
        top_ref[...] = top
        low_ref[...] = low

    top, low = split(states_ref[...])
    dims = ((1,), (1,))
    out_ref[...] = (
        dot(top_ref[...], top, dims)
        + dot(low_ref[...], top, dims)
        + dot(top_ref[...], low, dims)
    )


def rotate(coeffs, states):
    width, block = coeffs.shape
    owned = states.shape[0]
    tile = 256
    return pl.pallas_call(
        rotate_kernel,
        grid=(owned // tile,),
        in_specs=[
            pl.BlockSpec((width, block), lambda i: (0, 0)),
            pl.BlockSpec((tile, width), lambda i: (i, 0)),
        ],
        out_specs=pl.BlockSpec((block, tile), lambda i: (0, i)),
        out_shape=jax.ShapeDtypeStruct((block, owned), F32),
        scratch_shapes=[pltpu.VMEM((block, width), BF16)] * 2,
        compiler_params=pltpu.CompilerParams(vmem_limit_bytes=VMEM),
        cost_estimate=pl.CostEstimate(
            flops=6 * block * owned * width, bytes_accessed=6000000, transcendentals=0
        ),
        name="rotate",
    )(coeffs, states)


def cells_kernel(column_ref, row_ref, cell_ref, states_ref, ghost_ref, out_ref, top_ref, low_ref):
    owned = states_ref.shape[0]
    total = out_ref.shape[0]

    @pl.when(pl.program_id(0) == 0)
    def _():
        for lo, hi, ref in ((0, owned, states_ref), (owned, total, ghost_ref)):
            top, low = split(ref[...])
            top_ref[lo:hi] = top
            low_ref[lo:hi] = low
        out_ref[...] = jnp.zeros_like(out_ref)

    two = column_ref.shape[1]
    side = two // 2
    gather = (
        lax.broadcasted_iota(jnp.int32, (two, total), 1) == column_ref[0]
    ).astype(F32).astype(BF16)
    scatter = (
        lax.broadcasted_iota(jnp.int32, (total, two), 0) == row_ref[0]
    ).astype(F32).astype(BF16)
    values = dot(gather, top_ref[...]) + dot(gather, low_ref[...])
    top, low = split(values)
    results = []
    for k in range(2):
        cell = cell_ref[k]
        cell_top, cell_low = split(0.5 * (cell + cell.T))
        rows = slice(k * side, (k + 1) * side)
        results.append(
            dot(cell_top, top[rows]) + dot(cell_low, top[rows]) + dot(cell_top, low[rows])
        )
    top, low = split(jnp.concatenate(results, axis=0))
    out_ref[...] += dot(scatter, top) + dot(scatter, low)


def cells_apply(states, ghosts, cell_matrix, connect):
    owned, width = states.shape
    total = owned + ghosts.shape[0]
    cells, per_cell = connect.shape
    side = 128
    pad = side - per_cell
    cell = jnp.pad(cell_matrix, ((0, 0), (0, pad), (0, pad)))
    links = jnp.pad(connect, ((0, 0), (0, pad)), constant_values=-1)
    steps = cells // 2
    return pl.pallas_call(
        cells_kernel,
        grid=(steps,),
        in_specs=[
            pl.BlockSpec((1, 2 * side, 1), lambda i: (i, 0, 0)),
            pl.BlockSpec((1, 1, 2 * side), lambda i: (i, 0, 0)),
            pl.BlockSpec((2, side, side), lambda i: (i, 0, 0)),
            pl.BlockSpec((owned, width), lambda i: (0, 0)),
            pl.BlockSpec((total - owned, width), lambda i: (0, 0)),
        ],
        out_specs=pl.BlockSpec((total, width), lambda i: (0, 0)),
        out_shape=jax.ShapeDtypeStruct((total, width), F32),
        scratch_shapes=[pltpu.VMEM((total, width), BF16)] * 2,
        compiler_params=pltpu.CompilerParams(vmem_limit_bytes=VMEM),
        cost_estimate=pl.CostEstimate(
            flops=8 * cells * side * total * width, bytes_accessed=9000000, transcendentals=0
        ),
        name="cells",
    )(
        links.reshape(steps, 2 * side, 1),
        links.reshape(steps, 1, 2 * side),
        cell,
        states,
        ghosts,
    )


def face_pick(table, value, dims):
    top, low = halves(value)
    return dot(table, top, dims) + dot(table, low, dims)


def weights(states, cell_matrix, connect, face_list, node_mass):
    owned = states.shape[0]
    table = (face_list[:, None] == jnp.arange(owned)[None, :]).astype(BF16)
    ghosts = node_shift(face_pick(table, states, ((1,), (0,))), -1)
    assembled = cells_apply(states, ghosts, cell_matrix, connect)
    returned = node_shift(assembled[owned:], 1)
    applied = assembled[:owned] + face_pick(table, returned, ((0,), (0,)))
    return jnp.concatenate([applied, states * node_mass[:, None]], axis=1)


def panel_kernel(base_ref, p0, p1, p2, p3, top0, top1, low0, low1, out_ref, top_ref, low_ref):
    rows = p0.shape[0]
    depth = top0.shape[0]

    @pl.when(pl.program_id(0) == 0)
    def _():
        for by, piece in enumerate((p0, p1, p2, p3)):
            place = pl.ds(pl.multiple_of(lax.rem(base_ref[0] + by, 4) * rows, rows), rows)
            top, low = split(piece[...])
            top_ref[place] = top
            low_ref[place] = low

    first, second = slice(0, depth), slice(depth, 2 * depth)
    out_ref[...] = (
        dot(top_ref[:, first], top0[...])
        + dot(low_ref[:, first], top0[...])
        + dot(top_ref[:, first], low0[...])
        + dot(top_ref[:, second], top1[...])
        + dot(low_ref[:, second], top1[...])
        + dot(top_ref[:, second], low1[...])
    )


def panel_dot(base, pieces, tops, lows):
    rows, depth = pieces[0].shape
    width = tops[0].shape[1]
    tile = 256
    whole = pl.BlockSpec((rows, depth), lambda i: (0, 0))
    tall = pl.BlockSpec((depth // 2, tile), lambda i: (0, i))
    return pl.pallas_call(
        panel_kernel,
        grid=(width // tile,),
        in_specs=[pl.BlockSpec(memory_space=pltpu.SMEM)] + [whole] * 4 + [tall] * 4,
        out_specs=pl.BlockSpec((4 * rows, tile), lambda i: (0, i)),
        out_shape=jax.ShapeDtypeStruct((4 * rows, width), F32),
        scratch_shapes=[pltpu.VMEM((4 * rows, depth), BF16)] * 2,
        compiler_params=pltpu.CompilerParams(vmem_limit_bytes=VMEM),
        cost_estimate=pl.CostEstimate(
            flops=6 * 4 * rows * depth * width, bytes_accessed=12000000, transcendentals=0
        ),
        name="panel",
    )(base, *pieces, *tops, *lows)


def spread_sum(pieces, axis):
    return jnp.sum(lax.all_to_all(pieces, axis, 0, 0, tiled=True), axis=0)


def local(states, coeffs, cell_matrix, connect, face_list, node_mass):
    owned, width = states.shape
    block = coeffs.shape[1]
    partial = rotate(coeffs, states)
    over_y = spread_sum(partial.reshape(4, block // 4, owned), "y")
    rotated = spread_sum(over_y.reshape(4, block // 16, owned), "zh")

    late, _ = lax.optimization_barrier((states, partial))
    mine = weights(late, cell_matrix, connect, face_list, node_mass)
    other = ring(mine, "core", 1)
    tops, lows = zip(halves(mine), halves(other))

    core = lax.axis_index("core")
    pair = rotated.reshape(2, block // 32, owned)
    keep = lax.dynamic_index_in_dim(pair, core, 0, keepdims=False)
    send = lax.dynamic_index_in_dim(pair, 1 - core, 0, keepdims=False)
    both = jnp.concatenate([keep, ring(send, "core", 1)], axis=1)
    group = lax.all_gather(both, "zh", axis=0, tiled=False)
    here = lax.axis_index("y")
    results = []
    for half in range(2):
        rows = group[:, half * 8 : (half + 1) * 8].reshape(32, 2 * owned)
        pieces = [rows] + [ring(rows, "y", -by) for by in (1, 2, 3)]
        panel = panel_dot(here.reshape(1).astype(jnp.int32), pieces, tops, lows)
        panel = spread_sum(panel.reshape(4, 32, 2 * width), "x")
        results.append(spread_sum(panel.reshape(4, 8, 2 * width), "zl"))
    panel = jnp.concatenate(results, axis=0)
    return rotated, panel[:, :width], panel[:, width:]


def solution(mesh):
    fine = Mesh(mesh.devices.reshape(4, 4, 2, 4, 4), FINE)
    return jax.shard_map(
        local,
        mesh=fine,
        in_specs=(
            P(NODE, STATE),
            P(STATE, None),
            P(NODE, None, None),
            P(NODE, None),
            P(NODE),
            P(NODE),
        ),
        out_specs=(P(STATE, NODE), P(NODE, STATE), P(NODE, STATE)),
        check_vma=False,
    )
```

time: 194 us -> 228 us (1.18)
  matrix products: 41.7 us -> 1.95 us
  starting transfers between devices: 32.7 us -> 65.5 us
  waiting for transfers between devices: 19.3 us -> 50.9 us
  Pallas kernels: 0 us -> 29.3 us
  blocking collectives: 71.5 us -> 53.2 us
  local copies, waits for them, and re-layouts: 16.1 us -> 10.4 us
  other arithmetic: 8.82 us -> 11.6 us
    dot_general x11 -> x4, matrix products: 41.7 us -> 1.95 us  [dot(): lax.dot_general(left, right, (dims, ((), ())), preferred_element_type=F32)]
    all_to_all x2 -> x5, waiting for transfers between devices: 6.84 us -> 40.8 us  [spread_sum(): return jnp.sum(lax.all_to_all(pieces, axis, 0, 0, tiled=True), axis=0)]
    pallas_call x0 -> x4, Pallas kernels: none -> 29.3 us  [the longest x1 17.1 us: cells_apply(): pl.pallas_call(cells_kernel, grid=(steps,), in_specs=[pl.BlockSpec((1, 2...]
    all_to_all x3 -> x1, blocking collectives: 45.8 us -> 24.9 us  [spread_sum(): return jnp.sum(lax.all_to_all(pieces, axis, 0, 0, tiled=True), axis=0)]
    ppermute x3 -> x8, starting transfers between devices: 9.2 us -> 26.4 us  [ring(): lax.ppermute(shard, axis, [(i, (i + by) % length) for i in range(length)])]
    all_to_all x2 -> x5, starting transfers between devices: 20 us -> 31.8 us  [spread_sum(): return jnp.sum(lax.all_to_all(pieces, axis, 0, 0, tiled=True), axis=0)]
    reshape x2 -> x3, local copies, waits for them, and re-layouts: 8.76 us -> 0.64 us  [the longest x1 0.6 us: cells_apply(): links.reshape(steps, 2 * side, 1)]
    convert_element_type x0 -> x2, other arithmetic: none -> 6.99 us  [halves(): return (top.astype(BF16), (value - top).astype(BF16))]
  transfers between devices with their start and end apart: 7 -> 15, of which waited for: 4 -> 11; matrix products, arithmetic and copies ran while one was open for 27% -> 4% of each run, Pallas kernels for 0% -> 2%
where the time goes in v2:
time: 228 us; the launch traced here: 224 us
  starting transfers between devices  65.5 us (29%)
  blocking collectives  53.2 us (23%)
  waiting for transfers between devices  50.9 us (22%)
  Pallas kernels  29.3 us (13%)
  other arithmetic  11.6 us (5%)
  local copies, waits for them, and re-layouts  10.4 us (5%)
    all_to_all x5, waiting for transfers between devices, spread_sum(): return jnp.sum(lax.all_to_all(pieces, axis, 0, 0, tiled=True), axis=0)  40.8 us
    all_to_all x5, starting transfers between devices, spread_sum(): return jnp.sum(lax.all_to_all(pieces, axis, 0, 0, tiled=True), axis=0)  31.8 us
    all_gather x1, blocking collectives, local(): group = lax.all_gather(both, 'zh', axis=0, tiled=False)  28.2 us
    ppermute x8, starting transfers between devices, ring(): lax.ppermute(shard, axis, [(i, (i + by) % length) for i in range(length)])  26.4 us
    all_to_all x1, blocking collectives, spread_sum(): return jnp.sum(lax.all_to_all(pieces, axis, 0, 0, tiled=True), axis=0)  24.9 us
    pallas_call x1, Pallas kernels, cells_apply(): pl.pallas_call(cells_kernel, grid=(steps,), in_specs=[pl.BlockSpec((1, 2...  17.1 us
    pallas_call x2, Pallas kernels, panel_dot(): pl.pallas_call(panel_kernel, grid=(width // tile,), in_specs=[pl.BlockSpe...  9.2 us
    ppermute x8, waiting for transfers between devices, ring(): lax.ppermute(shard, axis, [(i, (i + by) % length) for i in range(length)])  9.19 us
  transfers between devices with their start and end apart: 15, of which 11 were waited for; matrix products, arithmetic and copies ran while one was open for 4% of the time, Pallas kernels for 2%

profile of v2, /device:TPU:24, one launch (start us, length us, event | category | flops | bytes accessed | tf_op | source)
XLA Modules:
  0.0 223.8 jit_solution(6137720575967722205)
XLA Ops:
  3.7 3.0 %rotate.1 = f32[512,768]{1,0:T(8,128)S(1)} custom-call(f32[768,512]{1,0:T(8,128)S(1)} %copy-done.10, f32[768,768]{1,0:T(8,128)S(1)} %copy-done), custom_call_target="tpu_custom_call" | custom-call | flops 1811939328 | bytes 6000000 | tf_op jit(solution)/shard_map/rotate/pallas_call | solution.py:63
  11.4 17.1 %cells.1 = f32[832,768]{1,0:T(8,128)S(1)} custom-call(s32[6,256,1]{2,1,0:T(8,128)S(1)} %reshape.58.column_ref, s32[6,1,256]{2,1,0:T(1,128)S(1)} %reshape.51.row_ref, f32[12,128,128]{2,1,0:T(8,128)S(1)} %pad.9.cell_ref, f32[768,768]{1,0:T(8,128)S(1)} %copy-done.1, f32[64,768]{1,0:T(8,128)S(1)} %collective-permute-done.4.ghost_ref), custom_call_target="tpu_custom_call" | custom-call | flops 7851737088 | bytes 9000000 | tf_op jit(solution)/shard_map/cells/pallas_call | solution.py:124
  28.6 5.9 %collective-permute-start.5 = (f32[64,768]{1,0:T(8,128)S(1)}, f32[64,768]{1,0:T(8,128)S(1)}, u32[]{:S(2)}, u32[]{:S(2)}) collective-permute-start(f32[64,768]{1,0:T(8,128)S(1)} %slice.26), channel_id=1, source_target_pairs={{0,16},{16,32},{32,48},{48,64},{64,80},{80,96},{96,112},{112,128},... | collective-permute-start | bytes 589832 | tf_op jit(solution)/shard_map/ppermute | solution.py:21
  36.7 3.9 %fusion = (bf16[768,1536]{1,0:T(8,128)(2,1)S(1)}, bf16[768,1536]{1,0:T(8,128)(2,1)}, f32[768,1536]{1,0:T(8,128)}) fusion(f32[768,768]{1,0:T(8,128)S(1)} %broadcast_multiply_fusion, f32[768,768]{1,0:T(8,128)S(1)} %slice_add_fusion), kind=kLoop, calls=%fused_computation.4 | loop fusion | flops 5898240 | bytes 14155776 | tf_op jit(solution)/shard_map/convert_element_type | solution.py:31
  40.6 3.5 %collective-permute-start.6 = (f32[768,1536]{1,0:T(8,128)}, f32[768,1536]{1,0:T(8,128)}, u32[]{:S(2)}, u32[]{:S(2)}) collective-permute-start(f32[768,1536]{1,0:T(8,128)} %get-tuple-element.9), channel_id=1, source_target_pairs={{0,16},{16,0},{1,17},{17,1},{2,18},{18,2},{3,19},{19,3},{4,20},{20... | collective-permute-start | bytes 14155784 | tf_op jit(solution)/shard_map/ppermute | solution.py:26
  44.1 24.9 %all_to_all.30 = f32[4,128,768]{2,1,0:T(8,128)} all-to-all(f32[4,128,768]{2,1,0:T(8,128)S(1)} %bitcast.17), channel_id=1, replica_groups=mesh['x'=4,'zl'=4,'core'=2,'y'=4,'zh'=4] {'y'}, dimensions={0} | all-to-all | bytes 3145728 | tf_op jit(solution)/shard_map/all_to_all | solution.py:211
  69.0 2.3 %reduce_sum.54 = f32[128,768]{1,0:T(8,128)} reduce(f32[4,128,768]{2,1,0:T(8,128)} %all_to_all.30, f32[]{:T(128)} %constant.19.clone.1), dimensions={0}, to_apply=%region_0.0 | reduce | flops 294912 | bytes 1966084 | tf_op jit(solution)/shard_map/reduce_sum | solution.py:211
  71.3 13.1 %all-to-all-start.1 = ((f32[4,32,768]{2,1,0:T(8,128)}), f32[4,32,768]{2,1,0:T(8,128)S(1)}, u32[]{:S(2)}, u32[]{:S(2)}) async-start(f32[4,32,768]{2,1,0:T(8,128)} %bitcast.1), calls=%async_computation.1 | async-start | bytes 786432 | tf_op jit(solution)/shard_map/all_to_all | solution.py:211
  84.4 19.1 %all-to-all-done.1 = f32[4,32,768]{2,1,0:T(8,128)S(1)} async-done(((f32[4,32,768]{2,1,0:T(8,128)}), f32[4,32,768]{2,1,0:T(8,128)S(1)}, u32[]{:S(2)}, u32[]{:S(2)}) %all-to-all-start.1) | async-done | bytes 393248 | tf_op jit(solution)/shard_map/all_to_all | solution.py:211
  103.6 1.9 collective-permute-start
  106.7 28.2 %all-gather = f32[64,1536]{1,0:T(8,128)S(1)} all-gather(f32[16,1536]{1,0:T(8,128)S(1)} %pad_maximum_fusion.1), channel_id=2, replica_groups=mesh['x'=4,'zl'=4,'core'=2,'y'=4,'zh'=4] {'zh'}, dimensions={0}, use_global_device_ids=true | all-gather | bytes 491520 | tf_op jit(solution)/shard_map/all_gather | solution.py:231
  135.0 2.8 %collective-permute-start.1 = (f32[32,1536]{1,0:T(8,128)S(1)}, f32[32,1536]{1,0:T(8,128)S(1)}, u32[]{:S(2)}, u32[]{:S(2)}) collective-permute-start(f32[32,1536]{1,0:T(8,128)S(1)} %get-tuple-element.11.p0), channel_id=1, source_target_pairs={{0,12},{4,0},{8,4},{12,8},{1,13},{5,1},{9,5},{13,9},{2,14},{6,2},{... | collective-permute-start | bytes 589832 | tf_op jit(solution)/shard_map/ppermute | solution.py:26
  137.7 4.7 %collective-permute-start.2 = (f32[32,1536]{1,0:T(8,128)S(1)}, f32[32,1536]{1,0:T(8,128)S(1)}, u32[]{:S(2)}, u32[]{:S(2)}) collective-permute-start(f32[32,1536]{1,0:T(8,128)S(1)} %get-tuple-element.11.p0), channel_id=1, source_target_pairs={{0,8},{4,12},{8,0},{12,4},{1,9},{5,13},{9,1},{13,5},{2,10},{6,14},... | collective-permute-start | bytes 589832 | tf_op jit(solution)/shard_map/ppermute | solution.py:26
  142.5 3.1 %collective-permute-start.3 = (f32[32,1536]{1,0:T(8,128)S(1)}, f32[32,1536]{1,0:T(8,128)S(1)}, u32[]{:S(2)}, u32[]{:S(2)}) collective-permute-start(f32[32,1536]{1,0:T(8,128)S(1)} %get-tuple-element.11.p0), channel_id=1, source_target_pairs={{0,4},{4,8},{8,12},{12,0},{1,5},{5,9},{9,13},{13,1},{2,6},{6,10},{... | collective-permute-start | bytes 589832 | tf_op jit(solution)/shard_map/ppermute | solution.py:26
  145.6 3.0 %fusion.1 = (bf16[768,1536]{1,0:T(8,128)(2,1)S(1)}, bf16[768,1536]{1,0:T(8,128)(2,1)S(1)}) fusion(f32[768,1536]{1,0:T(8,128)} %collective-permute-done.6), kind=kLoop, calls=%fused_computation.5 | loop fusion | flops 4718592 | bytes 9437184 | tf_op jit(solution)/shard_map/convert_element_type | solution.py:31
  149.2 2.2 collective-permute-done.3.p3
  151.4 4.6 %panel.2 = f32[128,1536]{1,0:T(8,128)} custom-call(s32[1]{0:T(128)} %bitcast.2.base_ref, f32[32,1536]{1,0:T(8,128)S(1)} %get-tuple-element.11.p0, f32[32,1536]{1,0:T(8,128)S(1)} %collective-permute-done.1.p1, f32[32,1536]{1,0:T(8,128)S(1)} %collective-permute-done.2.p2, f32[32,1536]{1,0:T(8,128)S(1)} %collective-permute-done.3.p3, ...), custom_call_target="tpu_custom_call" | custom-call | flops 1811939328 | bytes 12000000 | tf_op jit(solution)/shard_map/panel/pallas_call | solution.py:195
  156.0 7.2 %all-to-all-start.2 = ((f32[4,32,1536]{2,1,0:T(8,128)}), f32[4,32,1536]{2,1,0:T(8,128)S(1)}, u32[]{:S(2)}, u32[]{:S(2)}) async-start(f32[4,32,1536]{2,1,0:T(8,128)} %bitcast.8), calls=%async_computation.2 | async-start | bytes 1572864 | tf_op jit(solution)/shard_map/all_to_all | solution.py:211
  163.2 3.4 %collective-permute-start.7 = (f32[32,1536]{1,0:T(8,128)S(1)}, f32[32,1536]{1,0:T(8,128)S(1)}, u32[]{:S(2)}, u32[]{:S(2)}) collective-permute-start(f32[32,1536]{1,0:T(8,128)S(1)} %get-tuple-element.10.p0), channel_id=1, source_target_pairs={{0,12},{4,0},{8,4},{12,8},{1,13},{5,1},{9,5},{13,9},{2,14},{6,2},{... | collective-permute-start | bytes 589832 | tf_op jit(solution)/shard_map/ppermute | solution.py:26
  166.5 4.6 %collective-permute-start.8 = (f32[32,1536]{1,0:T(8,128)S(1)}, f32[32,1536]{1,0:T(8,128)S(1)}, u32[]{:S(2)}, u32[]{:S(2)}) collective-permute-start(f32[32,1536]{1,0:T(8,128)S(1)} %get-tuple-element.10.p0), channel_id=1, source_target_pairs={{0,8},{4,12},{8,0},{12,4},{1,9},{5,13},{9,1},{13,5},{2,10},{6,14},... | collective-permute-start | bytes 589832 | tf_op jit(solution)/shard_map/ppermute | solution.py:26
  171.1 2.5 %collective-permute-start.9 = (f32[32,1536]{1,0:T(8,128)S(1)}, f32[32,1536]{1,0:T(8,128)S(1)}, u32[]{:S(2)}, u32[]{:S(2)}) collective-permute-start(f32[32,1536]{1,0:T(8,128)S(1)} %get-tuple-element.10.p0), channel_id=1, source_target_pairs={{0,4},{4,8},{8,12},{12,0},{1,5},{5,9},{9,13},{13,1},{2,6},{6,10},{... | collective-permute-start | bytes 589832 | tf_op jit(solution)/shard_map/ppermute | solution.py:26
  173.6 3.6 %collective-permute-done.8.p2 = f32[32,1536]{1,0:T(8,128)S(1)} collective-permute-done((f32[32,1536]{1,0:T(8,128)S(1)}, f32[32,1536]{1,0:T(8,128)S(1)}, u32[]{:S(2)}, u32[]{:S(2)}) %collective-permute-start.8) | collective-permute-done | bytes 196640 | tf_op jit(solution)/shard_map/ppermute | solution.py:26
  177.2 1.7 collective-permute-done.9.p3
  178.9 1.7 copy-done.3
  180.6 1.7 copy-done.5
  183.9 4.6 %panel.3 = f32[128,1536]{1,0:T(8,128)} custom-call(s32[1]{0:T(128)} %bitcast.2.base_ref, f32[32,1536]{1,0:T(8,128)S(1)} %get-tuple-element.10.p0, f32[32,1536]{1,0:T(8,128)S(1)} %collective-permute-done.7.p1, f32[32,1536]{1,0:T(8,128)S(1)} %collective-permute-done.8.p2, f32[32,1536]{1,0:T(8,128)S(1)} %collective-permute-done.9.p3, ...), custom_call_target="tpu_custom_call" | custom-call | flops 1811939328 | bytes 12000000 | tf_op jit(solution)/shard_map/panel/pallas_call | solution.py:195
  188.5 4.8 %all-to-all-start.4 = ((f32[4,32,1536]{2,1,0:T(8,128)}), f32[4,32,1536]{2,1,0:T(8,128)S(1)}, u32[]{:S(2)}, u32[]{:S(2)}) async-start(f32[4,32,1536]{2,1,0:T(8,128)} %bitcast.11), calls=%async_computation.4 | async-start | bytes 1572864 | tf_op jit(solution)/shard_map/all_to_all | solution.py:211
  194.0 9.9 %all-to-all-done.4 = f32[4,32,1536]{2,1,0:T(8,128)S(1)} async-done(((f32[4,32,1536]{2,1,0:T(8,128)}), f32[4,32,1536]{2,1,0:T(8,128)S(1)}, u32[]{:S(2)}, u32[]{:S(2)}) %all-to-all-start.4) | async-done | bytes 786464 | tf_op jit(solution)/shard_map/all_to_all | solution.py:211
  203.9 3.4 %all-to-all-start.3 = ((f32[4,8,1536]{2,1,0:T(8,128)}), f32[4,8,1536]{2,1,0:T(8,128)S(1)}, u32[]{:S(2)}, u32[]{:S(2)}) async-start(f32[4,8,1536]{2,1,0:T(8,128)} %bitcast.9), calls=%async_computation.3 | async-start | bytes 393216 | tf_op jit(solution)/shard_map/all_to_all | solution.py:211
  208.0 5.5 %all-to-all-done.3 = f32[4,8,1536]{2,1,0:T(8,128)S(1)} async-done(((f32[4,8,1536]{2,1,0:T(8,128)}), f32[4,8,1536]{2,1,0:T(8,128)S(1)}, u32[]{:S(2)}, u32[]{:S(2)}) %all-to-all-start.3) | async-done | bytes 196640 | tf_op jit(solution)/shard_map/all_to_all | solution.py:211
  213.6 3.4 %all-to-all-start.5 = ((f32[4,8,1536]{2,1,0:T(8,128)}), f32[4,8,1536]{2,1,0:T(8,128)S(1)}, u32[]{:S(2)}, u32[]{:S(2)}) async-start(f32[4,8,1536]{2,1,0:T(8,128)} %bitcast.12), calls=%async_computation.5 | async-start | bytes 393216 | tf_op jit(solution)/shard_map/all_to_all | solution.py:211
  217.0 6.2 %all-to-all-done.5 = f32[4,8,1536]{2,1,0:T(8,128)S(1)} async-done(((f32[4,8,1536]{2,1,0:T(8,128)}), f32[4,8,1536]{2,1,0:T(8,128)S(1)}, u32[]{:S(2)}, u32[]{:S(2)}) %all-to-all-start.5) | async-done | bytes 196640 | tf_op jit(solution)/shard_map/all_to_all | solution.py:211
  (58 shorter events, 15.4 us)
Async XLA Ops:
  0.6 1.7 copy-start
  2.3 1.4 copy-start.10
  3.7 3.0 %copy-start.13 = (s32[64]{0:T(128)S(1)}, s32[64]{0:T(128)}, u32[]{:S(2)}) copy-start(s32[64]{0:T(128)} %param.10) | copy-start | bytes 772
  6.7 1.2 copy-start.8
  6.7 2.6 %copy-start.12 = (s32[12,125]{1,0:T(8,128)S(1)}, s32[12,125]{1,0:T(8,128)}, u32[]{:S(2)}) copy-start(s32[12,125]{1,0:T(8,128)} %param.9) | copy-start | bytes 18004
  7.2 4.2 %copy-start.1 = (f32[768,768]{1,0:T(8,128)S(1)}, f32[768,768]{1,0:T(8,128)}, u32[]{:S(2)}) copy-start(f32[768,768]{1,0:T(8,128)} %states_ref.2) | copy-start | bytes 7077892
  7.9 3.5 %collective-permute-start.4 = (f32[64,768]{1,0:T(8,128)S(1)}, f32[64,768]{1,0:T(8,128)S(1)}, u32[]{:S(2)}, u32[]{:S(2)}) collective-permute-start(f32[64,768]{1,0:T(8,128)S(1)} %fusion.6), channel_id=1, source_target_pairs={{16,0},{32,16},{48,32},{64,48},{80,64},{96,80},{112,96},{128,112},... | collective-permute-start | bytes 589832 | tf_op jit(solution)/shard_map/ppermute | solution.py:21
  11.2 23.2 %copy-start.15 = (f32[768]{0:T(1024)S(1)}, f32[768]{0:T(1024)}, u32[]{:S(2)}) copy-start(f32[768]{0:T(1024)} %param.11) | copy-start | bytes 9220
  28.5 6.9 %copy-start.14 = (s32[64]{0:T(128)S(1)}, s32[64]{0:T(128)}, u32[]{:S(2)}) copy-start(s32[64]{0:T(128)} %param.10) | copy-start | bytes 772
  28.6 6.9 %collective-permute-start.5 = (f32[64,768]{1,0:T(8,128)S(1)}, f32[64,768]{1,0:T(8,128)S(1)}, u32[]{:S(2)}, u32[]{:S(2)}) collective-permute-start(f32[64,768]{1,0:T(8,128)S(1)} %slice.26), channel_id=1, source_target_pairs={{0,16},{16,32},{32,48},{48,64},{64,80},{80,96},{96,112},{112,128},... | collective-permute-start | bytes 589832 | tf_op jit(solution)/shard_map/ppermute | solution.py:21
  36.7 7.4 %copy-start.9 = (f32[512,768]{1,0:T(8,128)S(1)}, f32[512,768]{1,0:T(8,128)}, u32[]{:S(2)}) copy-start(f32[512,768]{1,0:T(8,128)} %copy-done.8) | copy-start | bytes 4718596
  40.6 104.9 %collective-permute-start.6 = (f32[768,1536]{1,0:T(8,128)}, f32[768,1536]{1,0:T(8,128)}, u32[]{:S(2)}, u32[]{:S(2)}) collective-permute-start(f32[768,1536]{1,0:T(8,128)} %get-tuple-element.9), channel_id=1, source_target_pairs={{0,16},{16,0},{1,17},{17,1},{2,18},{18,2},{3,19},{19,3},{4,20},{20... | collective-permute-start | bytes 14155784 | tf_op jit(solution)/shard_map/ppermute | solution.py:26
  71.3 32.2 %all-to-all-start.1 = ((f32[4,32,768]{2,1,0:T(8,128)}), f32[4,32,768]{2,1,0:T(8,128)S(1)}, u32[]{:S(2)}, u32[]{:S(2)}) async-start(f32[4,32,768]{2,1,0:T(8,128)} %bitcast.1), calls=%async_computation.1 | async-start | bytes 786432 | tf_op jit(solution)/shard_map/all_to_all | solution.py:211
  103.5 45.1 %copy-start.11 = (f32[32,768]{1,0:T(8,128)}, f32[32,768]{1,0:T(8,128)S(1)}, u32[]{:S(2)}) copy-start(f32[32,768]{1,0:T(8,128)S(1)} %reduce_sum.55) | copy-start | bytes 294916
  103.6 3.1 %collective-permute-start = (f32[16,768]{1,0:T(8,128)S(1)}, f32[16,768]{1,0:T(8,128)S(1)}, u32[]{:S(2)}, u32[]{:S(2)}) collective-permute-start(f32[16,768]{1,0:T(8,128)S(1)} %get-tuple-element.15), channel_id=1, source_target_pairs={{0,16},{16,0},{1,17},{17,1},{2,18},{18,2},{3,19},{19,3},{4,20},{20... | collective-permute-start | bytes 147464 | tf_op jit(solution)/shard_map/ppermute | solution.py:26
  135.0 16.4 %copy-start.2 = (bf16[768,1536]{1,0:T(8,128)(2,1)S(1)}, bf16[768,1536]{1,0:T(8,128)(2,1)}, u32[]{:S(2)}) copy-start(bf16[768,1536]{1,0:T(8,128)(2,1)} %get-tuple-element.8.top0) | copy-start | bytes 7077892
  135.0 13.7 %collective-permute-start.1 = (f32[32,1536]{1,0:T(8,128)S(1)}, f32[32,1536]{1,0:T(8,128)S(1)}, u32[]{:S(2)}, u32[]{:S(2)}) collective-permute-start(f32[32,1536]{1,0:T(8,128)S(1)} %get-tuple-element.11.p0), channel_id=1, source_target_pairs={{0,12},{4,0},{8,4},{12,8},{1,13},{5,1},{9,5},{13,9},{2,14},{6,2},{... | collective-permute-start | bytes 589832 | tf_op jit(solution)/shard_map/ppermute | solution.py:26
  137.7 11.4 %collective-permute-start.2 = (f32[32,1536]{1,0:T(8,128)S(1)}, f32[32,1536]{1,0:T(8,128)S(1)}, u32[]{:S(2)}, u32[]{:S(2)}) collective-permute-start(f32[32,1536]{1,0:T(8,128)S(1)} %get-tuple-element.11.p0), channel_id=1, source_target_pairs={{0,8},{4,12},{8,0},{12,4},{1,9},{5,13},{9,1},{13,5},{2,10},{6,14},... | collective-permute-start | bytes 589832 | tf_op jit(solution)/shard_map/ppermute | solution.py:26
  142.5 8.9 %collective-permute-start.3 = (f32[32,1536]{1,0:T(8,128)S(1)}, f32[32,1536]{1,0:T(8,128)S(1)}, u32[]{:S(2)}, u32[]{:S(2)}) collective-permute-start(f32[32,1536]{1,0:T(8,128)S(1)} %get-tuple-element.11.p0), channel_id=1, source_target_pairs={{0,4},{4,8},{8,12},{12,0},{1,5},{5,9},{9,13},{13,1},{2,6},{6,10},{... | collective-permute-start | bytes 589832 | tf_op jit(solution)/shard_map/ppermute | solution.py:26
  148.6 7.3 %copy-start.4 = (bf16[768,1536]{1,0:T(8,128)(2,1)}, bf16[768,1536]{1,0:T(8,128)(2,1)S(1)}, u32[]{:S(2)}) copy-start(bf16[768,1536]{1,0:T(8,128)(2,1)S(1)} %get-tuple-element.5.low1) | copy-start | bytes 7077892
  148.6 7.3 %copy-start.6 = (bf16[768,1536]{1,0:T(8,128)(2,1)}, bf16[768,1536]{1,0:T(8,128)(2,1)S(1)}, u32[]{:S(2)}) copy-start(bf16[768,1536]{1,0:T(8,128)(2,1)S(1)} %get-tuple-element.6.top1) | copy-start | bytes 7077892
  156.0 32.5 %all-to-all-start.2 = ((f32[4,32,1536]{2,1,0:T(8,128)}), f32[4,32,1536]{2,1,0:T(8,128)S(1)}, u32[]{:S(2)}, u32[]{:S(2)}) async-start(f32[4,32,1536]{2,1,0:T(8,128)} %bitcast.8), calls=%async_computation.2 | async-start | bytes 1572864 | tf_op jit(solution)/shard_map/all_to_all | solution.py:211
  163.2 10.4 %collective-permute-start.7 = (f32[32,1536]{1,0:T(8,128)S(1)}, f32[32,1536]{1,0:T(8,128)S(1)}, u32[]{:S(2)}, u32[]{:S(2)}) collective-permute-start(f32[32,1536]{1,0:T(8,128)S(1)} %get-tuple-element.10.p0), channel_id=1, source_target_pairs={{0,12},{4,0},{8,4},{12,8},{1,13},{5,1},{9,5},{13,9},{2,14},{6,2},{... | collective-permute-start | bytes 589832 | tf_op jit(solution)/shard_map/ppermute | solution.py:26
  166.5 10.7 %collective-permute-start.8 = (f32[32,1536]{1,0:T(8,128)S(1)}, f32[32,1536]{1,0:T(8,128)S(1)}, u32[]{:S(2)}, u32[]{:S(2)}) collective-permute-start(f32[32,1536]{1,0:T(8,128)S(1)} %get-tuple-element.10.p0), channel_id=1, source_target_pairs={{0,8},{4,12},{8,0},{12,4},{1,9},{5,13},{9,1},{13,5},{2,10},{6,14},... | collective-permute-start | bytes 589832 | tf_op jit(solution)/shard_map/ppermute | solution.py:26
  171.1 7.8 %collective-permute-start.9 = (f32[32,1536]{1,0:T(8,128)S(1)}, f32[32,1536]{1,0:T(8,128)S(1)}, u32[]{:S(2)}, u32[]{:S(2)}) collective-permute-start(f32[32,1536]{1,0:T(8,128)S(1)} %get-tuple-element.10.p0), channel_id=1, source_target_pairs={{0,4},{4,8},{8,12},{12,0},{1,5},{5,9},{9,13},{13,1},{2,6},{6,10},{... | collective-permute-start | bytes 589832 | tf_op jit(solution)/shard_map/ppermute | solution.py:26
  178.9 1.7 copy-start.3
  180.6 1.7 copy-start.5
  182.3 1.7 copy-start.7
  188.5 15.4 %all-to-all-start.4 = ((f32[4,32,1536]{2,1,0:T(8,128)}), f32[4,32,1536]{2,1,0:T(8,128)S(1)}, u32[]{:S(2)}, u32[]{:S(2)}) async-start(f32[4,32,1536]{2,1,0:T(8,128)} %bitcast.11), calls=%async_computation.4 | async-start | bytes 1572864 | tf_op jit(solution)/shard_map/all_to_all | solution.py:211
  203.9 9.6 %all-to-all-start.3 = ((f32[4,8,1536]{2,1,0:T(8,128)}), f32[4,8,1536]{2,1,0:T(8,128)S(1)}, u32[]{:S(2)}, u32[]{:S(2)}) async-start(f32[4,8,1536]{2,1,0:T(8,128)} %bitcast.9), calls=%async_computation.3 | async-start | bytes 393216 | tf_op jit(solution)/shard_map/all_to_all | solution.py:211
  213.6 9.6 %all-to-all-start.5 = ((f32[4,8,1536]{2,1,0:T(8,128)}), f32[4,8,1536]{2,1,0:T(8,128)S(1)}, u32[]{:S(2)}, u32[]{:S(2)}) async-start(f32[4,8,1536]{2,1,0:T(8,128)} %bitcast.12), calls=%async_computation.5 | async-start | bytes 393216 | tf_op jit(solution)/shard_map/all_to_all | solution.py:211

commit v3 on v2

v3 whole, which is shorter than its diff:
```python
import jax
import jax.numpy as jnp
from jax import lax
from jax.experimental import pallas as pl
from jax.experimental.pallas import tpu as pltpu
from jax.sharding import Mesh, PartitionSpec as P

FINE = ("x", "zl", "core", "y", "zh")
NODE = ("x", "zl", "core")
STATE = ("y", "zh")
VMEM = 56 * 1024 * 1024
F32 = jnp.float32
BF16 = jnp.bfloat16


def node_shift(shard, by):
    length = lax.axis_size(NODE)
    pairs = [(i, i + by) for i in range(length) if 0 <= i + by < length]
    return lax.ppermute(shard, NODE, pairs)


def ring(shard, axis, by):
    length = lax.axis_size(axis)
    return lax.ppermute(shard, axis, [(i, (i + by) % length) for i in range(length)])


def halves(value):
    top = lax.reduce_precision(value, 8, 7)
    return top.astype(BF16), (value - top).astype(BF16)


def split(value):
    top = value.astype(BF16)
    return top, (value - top.astype(F32)).astype(BF16)


def dot(left, right, dims=((1,), (0,))):
    return lax.dot_general(left, right, (dims, ((), ())), preferred_element_type=F32)


def params():
    return pltpu.CompilerParams(vmem_limit_bytes=VMEM)


def cost(flops, moved):
    return pl.CostEstimate(flops=flops, bytes_accessed=moved, transcendentals=0)


ANY = pl.BlockSpec(memory_space=pl.ANY)


def rotate_kernel(coeffs_ref, states_ref, out_ref, top_ref, low_ref):
    @pl.when(pl.program_id(0) == 0)
    def _():
        top, low = split(coeffs_ref[...].T)
        for y in range(4):
            for zh in range(4):
                for core in range(2):
                    source = ((y * 4 + zh) * 2 + core) * 16
                    place = ((y * 2 + core) * 4 + zh) * 16
                    top_ref[place : place + 16] = top[source : source + 16]
                    low_ref[place : place + 16] = low[source : source + 16]

    top, low = split(states_ref[...])
    dims = ((1,), (1,))
    out_ref[...] = (
        dot(top_ref[...], top, dims)
        + dot(low_ref[...], top, dims)
        + dot(top_ref[...], low, dims)
    )


def rotate(coeffs, states):
    width, block = coeffs.shape
    owned = states.shape[0]
    tile = 256
    return pl.pallas_call(
        rotate_kernel,
        grid=(owned // tile,),
        in_specs=[
            pl.BlockSpec((width, block), lambda i: (0, 0)),
            pl.BlockSpec((tile, width), lambda i: (i, 0)),
        ],
        out_specs=pl.BlockSpec((block, tile), lambda i: (0, i)),
        out_shape=jax.ShapeDtypeStruct((block, owned), F32),
        scratch_shapes=[pltpu.VMEM((block, width), BF16)] * 2,
        compiler_params=params(),
        cost_estimate=cost(6 * block * owned * width, 6000000),
        name="rotate",
    )(coeffs, states)


def cells_kernel(column_ref, row_ref, cell_ref, states_ref, ghost_ref, _, out_ref, pair_ref):
    owned = states_ref.shape[0]
    total = out_ref.shape[0]
    depth = pair_ref.shape[0] // 2

    @pl.when(pl.program_id(0) == 0)
    def _():
        for place, ref in ((0, states_ref), (owned, ghost_ref)):
            top, low = split(ref[...])
            end = place + ref.shape[0]
            pair_ref[place:end] = top
            pair_ref[depth + place : depth + end] = low
        blank = jnp.zeros((depth - total, pair_ref.shape[1]), BF16)
        pair_ref[total:depth] = blank
        pair_ref[depth + total :] = blank
        out_ref[...] = jnp.zeros_like(out_ref)

    count, side = cell_ref.shape[0], cell_ref.shape[1]
    many = count * side
    gather = (
        lax.broadcasted_iota(jnp.int32, (many, depth), 1) == column_ref[0]
    ).astype(F32).astype(BF16)
    scatter = (
        lax.broadcasted_iota(jnp.int32, (total, many), 0) == row_ref[0]
    ).astype(F32).astype(BF16)
    top, low = split(dot(jnp.concatenate([gather, gather], axis=1), pair_ref[...]))
    results = []
    for k in range(count):
        cell = cell_ref[k]
        cell_top, cell_low = split(0.5 * (cell + cell.T))
        rows = slice(k * side, (k + 1) * side)
        results.append(
            dot(
                jnp.concatenate([cell_top, cell_low, cell_top], axis=1),
                jnp.concatenate([top[rows], top[rows], low[rows]], axis=0),
            )
        )
    top, low = split(jnp.concatenate(results, axis=0))
    out_ref[...] += dot(
        jnp.concatenate([scatter, scatter], axis=1), jnp.concatenate([top, low], axis=0)
    )


def cells_apply(states, ghosts, cell_matrix, connect, after):
    owned, width = states.shape
    total = owned + ghosts.shape[0]
    depth = -(-total // 128) * 128
    cells, per_cell = connect.shape
    side, count = 128, 4
    pad = side - per_cell
    cell = jnp.pad(cell_matrix, ((0, 0), (0, pad), (0, pad)))
    links = jnp.pad(connect, ((0, 0), (0, pad)), constant_values=-1)
    steps = cells // count
    return pl.pallas_call(
        cells_kernel,
        grid=(steps,),
        in_specs=[
            pl.BlockSpec((1, count * side, 1), lambda i: (i, 0, 0)),
            pl.BlockSpec((1, 1, count * side), lambda i: (i, 0, 0)),
            pl.BlockSpec((count, side, side), lambda i: (i, 0, 0)),
            pl.BlockSpec((owned, width), lambda i: (0, 0)),
            pl.BlockSpec((total - owned, width), lambda i: (0, 0)),
            ANY,
        ],
        out_specs=pl.BlockSpec((total, width), lambda i: (0, 0)),
        out_shape=jax.ShapeDtypeStruct((total, width), F32),
        scratch_shapes=[pltpu.VMEM((2 * depth, width), BF16)],
        compiler_params=params(),
        cost_estimate=cost(8 * cells * side * total * width, 9000000),
        name="cells",
    )(
        links.reshape(steps, count * side, 1),
        links.reshape(steps, 1, count * side),
        cell,
        states,
        ghosts,
        after,
    )


def face_pick(table, value, dims):
    top, low = halves(value)
    return dot(table, top, dims) + dot(table, low, dims)


def weights(states, cell_matrix, connect, face_list, node_mass, after):
    owned = states.shape[0]
    table = (face_list[:, None] == jnp.arange(owned)[None, :]).astype(BF16)
    ghosts = node_shift(face_pick(table, states, ((1,), (0,))), -1)
    assembled = cells_apply(states, ghosts, cell_matrix, connect, after)
    returned = node_shift(assembled[owned:], 1)
    applied = assembled[:owned] + face_pick(table, returned, ((0,), (0,)))
    return jnp.concatenate([applied, states * node_mass[:, None]], axis=1)


def panel_kernel(base_ref, p0, p1, p2, p3, mine_ref, other_ref, out_ref, top_ref, low_ref):
    rows = p0.shape[0]
    depth = mine_ref.shape[0]

    @pl.when(pl.program_id(0) == 0)
    def _():
        for by, piece in enumerate((p0, p1, p2, p3)):
            place = pl.ds(pl.multiple_of(lax.rem(base_ref[0] + by, 4) * rows, rows), rows)
            top, low = split(piece[...])
            top_ref[place] = top
            low_ref[place] = low

    total = None
    for k, ref in enumerate((mine_ref, other_ref)):
        top, low = split(ref[...])
        part = slice(k * depth, (k + 1) * depth)
        value = (
            dot(top_ref[:, part], top) + dot(low_ref[:, part], top) + dot(top_ref[:, part], low)
        )
        total = value if total is None else total + value
    out_ref[...] = total


def panel_dot(base, pieces, mine, other):
    rows, depth = pieces[0].shape
    width = mine.shape[1]
    tile = 256
    whole = pl.BlockSpec((rows, depth), lambda i: (0, 0))
    tall = pl.BlockSpec((depth // 2, tile), lambda i: (0, i))
    return pl.pallas_call(
        panel_kernel,
        grid=(width // tile,),
        in_specs=[pl.BlockSpec(memory_space=pltpu.SMEM)] + [whole] * 4 + [tall] * 2,
        out_specs=pl.BlockSpec((4 * rows, tile), lambda i: (0, i)),
        out_shape=jax.ShapeDtypeStruct((4 * rows, width), F32),
        scratch_shapes=[pltpu.VMEM((4 * rows, depth), BF16)] * 2,
        compiler_params=params(),
        cost_estimate=cost(6 * 4 * rows * depth * width, 12000000),
        name="panel",
    )(base, *pieces, mine, other)


def fold_kernel(core_ref, pieces_ref, _, out_ref):
    owned = pieces_ref.shape[3]
    for k in range(2):
        which = core_ref[0] if k == 0 else 1 - core_ref[0]
        value = pieces_ref[0, which]
        for y in range(1, 4):
            value = value + pieces_ref[y, which]
        out_ref[:, k * owned : (k + 1) * owned] = value


def fold(core, pieces, after):
    _, _, rows, owned = pieces.shape
    return pl.pallas_call(
        fold_kernel,
        in_specs=[
            pl.BlockSpec(memory_space=pltpu.SMEM),
            pl.BlockSpec(memory_space=pltpu.VMEM),
            ANY,
        ],
        out_specs=pl.BlockSpec(memory_space=pltpu.VMEM),
        out_shape=jax.ShapeDtypeStruct((rows, 2 * owned), F32),
        compiler_params=params(),
        cost_estimate=cost(8 * rows * owned, 2000000),
        name="fold",
    )(core, pieces, after)


def swap(pieces, axis):
    return lax.all_to_all(pieces, axis, 0, 0, tiled=True)


def local(states, coeffs, cell_matrix, connect, face_list, node_mass):
    owned, width = states.shape
    block = coeffs.shape[1]
    core = lax.axis_index("core").astype(jnp.int32).reshape(1)
    here = lax.axis_index("y").astype(jnp.int32).reshape(1)

    partial = rotate(coeffs, states)
    mine = weights(states, cell_matrix, connect, face_list, node_mass, partial)
    other = ring(mine, "core", 1)
    pieces = swap(partial.reshape(8, block // 8, owned), ("y", "core"))
    over_y = fold(core, pieces.reshape(4, 2, block // 8, owned), mine)
    both = jnp.sum(swap(over_y.reshape(4, block // 32, 2 * owned), "zh"), axis=0)

    own, theirs = both[:, :owned], ring(both[:, owned:], "core", 1)
    first = core[0] == 0
    rotated = jnp.concatenate(
        [jnp.where(first, own, theirs), jnp.where(first, theirs, own)], axis=0
    )

    group = lax.all_gather(both, "zh", axis=0, tiled=True)
    rows = [group] + [ring(group, "y", -by) for by in (1, 2, 3)]
    panel = panel_dot(here, rows, mine, other)
    panel = jnp.sum(swap(panel.reshape(4, block // 8, 2 * width), "x"), axis=0)
    panel = swap(panel.reshape(4, block // 32, 2 * width), "zl")
    return rotated, jnp.sum(panel[:, :, :width], axis=0), jnp.sum(panel[:, :, width:], axis=0)


def solution(mesh):
    fine = Mesh(mesh.devices.reshape(4, 4, 2, 4, 4), FINE)
    return jax.shard_map(
        local,
        mesh=fine,
        in_specs=(
            P(NODE, STATE),
            P(STATE, None),
            P(NODE, None, None),
            P(NODE, None),
            P(NODE),
            P(NODE),
        ),
        out_specs=(P(STATE, NODE), P(NODE, STATE), P(NODE, STATE)),
        check_vma=False,
    )
```

time: 228 us -> 214 us (0.939); the launches traced: 224 us -> 213 us
  blocking collectives: 53.2 us -> 92.6 us
  starting transfers between devices: 65.5 us -> 31.2 us
  waiting for transfers between devices: 50.9 us -> 38.5 us
  other arithmetic: 11.6 us -> 5.24 us
  Pallas kernels: 29.3 us -> 34.1 us
  local copies, waits for them, and re-layouts: 10.4 us -> 7.04 us
    all_to_all x1 -> x2, blocking collectives: 24.9 us -> 66.5 us  [swap(): return lax.all_to_all(pieces, axis, 0, 0, tiled=True)]
    all_to_all x5 -> x2, starting transfers between devices: 31.8 us -> 11.1 us  [swap(): return lax.all_to_all(pieces, axis, 0, 0, tiled=True)]
    all_to_all x5 -> x2, waiting for transfers between devices: 40.8 us -> 26.4 us  [swap(): return lax.all_to_all(pieces, axis, 0, 0, tiled=True)]
    ppermute x8 -> x5, starting transfers between devices: 26.4 us -> 15.8 us  [ring(): lax.ppermute(shard, axis, [(i, (i + by) % length) for i in range(length)])]
    convert_element_type x2 -> x0, other arithmetic: 6.99 us -> none  [halves(): return (top.astype(BF16), (value - top).astype(BF16))]
    unnamed x32 -> x26, local copies, waits for them, and re-layouts: 8.51 us -> 3.03 us
    ppermute x2, starting transfers between devices: 7.28 us -> 4.34 us  [node_shift(): return lax.ppermute(shard, NODE, pairs)]
    pallas_call x1, Pallas kernels: 3 us -> 5.94 us  [rotate(): pl.pallas_call(rotate_kernel, grid=(owned // tile,), in_specs=[pl.BlockSp...]
  transfers between devices with their start and end apart: 15 -> 9, of which waited for: 11 -> 7; matrix products, arithmetic and copies ran while one was open for 4% -> 2% of each run, Pallas kernels for 2% -> 4%
where the time goes in v3:
time: 214 us; the launch traced here: 213 us
  blocking collectives  92.6 us (43%)
  waiting for transfers between devices  38.5 us (18%)
  Pallas kernels  34.1 us (16%)
  starting transfers between devices  31.2 us (15%)
  local copies, waits for them, and re-layouts  7.04 us (3%)
  other arithmetic  5.24 us (2%)
  matrix products  3.8 us (2%)
    all_to_all x2, blocking collectives, swap(): return lax.all_to_all(pieces, axis, 0, 0, tiled=True)  66.5 us
    all_to_all x2, waiting for transfers between devices, swap(): return lax.all_to_all(pieces, axis, 0, 0, tiled=True)  26.4 us
    all_gather x1, blocking collectives, local(): group = lax.all_gather(both, 'zh', axis=0, tiled=True)  26.1 us
    pallas_call x1, Pallas kernels, cells_apply(): pl.pallas_call(cells_kernel, grid=(steps,), in_specs=[pl.BlockSpec((1, co...  16.8 us
    ppermute x5, starting transfers between devices, ring(): lax.ppermute(shard, axis, [(i, (i + by) % length) for i in range(length)])  15.8 us
    ppermute x5, waiting for transfers between devices, ring(): lax.ppermute(shard, axis, [(i, (i + by) % length) for i in range(length)])  11.3 us
    all_to_all x2, starting transfers between devices, swap(): return lax.all_to_all(pieces, axis, 0, 0, tiled=True)  11.1 us
    pallas_call x1, Pallas kernels, panel_dot(): pl.pallas_call(panel_kernel, grid=(width // tile,), in_specs=[pl.BlockSpe...  9.22 us
  transfers between devices with their start and end apart: 9, of which 7 were waited for; matrix products, arithmetic and copies ran while one was open for 2% of the time, Pallas kernels for 4%

profile of v3, /device:TPU:24, one launch (start us, length us, event | category | flops | bytes accessed | tf_op | source)
XLA Modules:
  0.0 213.3 jit_solution(9083327468304751166)
XLA Ops:
  0.7 2.2 %fusion.1 = f32[64,768]{1,0:T(8,128)S(1)} fusion(f32[768,768]{1,0:T(8,128)} %states_ref.3, s32[64]{0:T(128)} %param.10), kind=kOutput, calls=%fused_computation.5 | convolution fusion | flops 77316096 | bytes 2556160 | tf_op jit(solution)/shard_map/dot_general | solution.py:38
  3.4 1.3 collective-permute-start
  5.3 1.5 reshape.44.column_ref
  6.8 1.0 pad.9.cell_ref
  7.8 5.9 %rotate.1._ = f32[512,768]{1,0:T(8,128)} custom-call(f32[768,512]{1,0:T(8,128)} %coeffs_ref.1, f32[768,768]{1,0:T(8,128)} %states_ref.3), custom_call_target="tpu_custom_call" | custom-call | flops 1811939328 | bytes 6000000 | tf_op jit(solution)/shard_map/rotate/pallas_call | solution.py:77
  13.8 0.7 copy-done.12
  14.4 16.8 %cells.1 = f32[832,768]{1,0:T(8,128)} custom-call(s32[3,512,1]{2,1,0:T(8,128)} %reshape.44.column_ref, s32[3,1,512]{2,1,0:T(1,128)} %reshape.39.row_ref, f32[12,128,128]{2,1,0:T(8,128)} %pad.9.cell_ref, f32[768,768]{1,0:T(8,128)} %states_ref.3, f32[64,768]{1,0:T(8,128)} %copy-done.12, f32[512,768]{1,0:T(8,128)} %rotate.1._), custom_call_target="tpu_custom_call" | custom-call | flops 7851737088 | bytes 9000000 | tf_op jit(solution)/shard_map/cells/pallas_call | solution.py:146
  31.2 0.9 slice.25
  32.1 3.0 %collective-permute-start.1 = (f32[64,768]{1,0:T(8,128)S(1)}, f32[64,768]{1,0:T(8,128)S(1)}, u32[]{:S(2)}, u32[]{:S(2)}) collective-permute-start(f32[64,768]{1,0:T(8,128)S(1)} %slice.25), channel_id=1, source_target_pairs={{0,16},{16,32},{32,48},{48,64},{64,80},{80,96},{96,112},{112,128},... | collective-permute-start | bytes 589832 | tf_op jit(solution)/shard_map/ppermute | solution.py:19
  35.4 0.8 collective-permute-done.1
  37.8 2.8 %pad_maximum_fusion._.mine_ref = f32[768,1536]{1,0:T(8,128)} fusion(f32[768,768]{1,0:T(8,128)S(1)} %broadcast_multiply_fusion, f32[768,768]{1,0:T(8,128)S(1)} %slice_add_fusion), kind=kLoop, calls=%fused_computation | loop fusion | flops 1179648 | bytes 9437184 | tf_op jit(solution)/shard_map/concatenate | solution.py:185
  40.6 4.6 %collective-permute-start.6 = (f32[768,1536]{1,0:T(8,128)}, f32[768,1536]{1,0:T(8,128)}, u32[]{:S(2)}, u32[]{:S(2)}) collective-permute-start(f32[768,1536]{1,0:T(8,128)} %pad_maximum_fusion._.mine_ref), channel_id=1, source_target_pairs={{0,16},{16,0},{1,17},{17,1},{2,18},{18,2},{3,19},{19,3},{4,20},{20... | collective-permute-start | bytes 14155784 | tf_op jit(solution)/shard_map/ppermute | solution.py:24
  45.3 7.6 %all-to-all-start = ((f32[8,64,768]{2,1,0:T(8,128)}), f32[8,64,768]{2,1,0:T(8,128)S(1)}, u32[]{:S(2)}, u32[]{:S(2)}) async-start(f32[8,64,768]{2,1,0:T(8,128)} %bitcast.1), calls=%async_computation | async-start | bytes 3145728 | tf_op jit(solution)/shard_map/all_to_all | solution.py:258
  52.9 19.5 %all-to-all-done = f32[8,64,768]{2,1,0:T(8,128)S(1)} async-done(((f32[8,64,768]{2,1,0:T(8,128)}), f32[8,64,768]{2,1,0:T(8,128)S(1)}, u32[]{:S(2)}, u32[]{:S(2)}) %all-to-all-start) | async-done | bytes 1572896 | tf_op jit(solution)/shard_map/all_to_all | solution.py:258
  72.4 1.1 copy-done.2
  73.5 2.2 %fold.1 = f32[64,1536]{1,0:T(8,128)} custom-call(s32[1]{0:T(128)} %bitcast.core_ref, f32[4,2,64,768]{3,2,1,0:T(8,128)} %bitcast.7, f32[768,1536]{1,0:T(8,128)} %pad_maximum_fusion._.mine_ref), custom_call_target="tpu_custom_call" | custom-call | flops 393216 | bytes 2000000 | tf_op jit(solution)/shard_map/fold/pallas_call | solution.py:242
  75.7 31.8 %all_to_all.20 = f32[4,16,1536]{2,1,0:T(8,128)S(1)} all-to-all(f32[4,16,1536]{2,1,0:T(8,128)} %bitcast.9), channel_id=1, replica_groups=mesh['x'=4,'zl'=4,'core'=2,'y'=4,'zh'=4] {'zh'}, dimensions={0} | all-to-all | bytes 786432 | tf_op jit(solution)/shard_map/all_to_all | solution.py:258
  107.6 26.1 %all_gather.3.p0 = f32[64,1536]{1,0:T(8,128)S(1)} all-gather(f32[16,1536]{1,0:T(8,128)S(1)} %reduce_sum.36), channel_id=1, replica_groups=mesh['x'=4,'zl'=4,'core'=2,'y'=4,'zh'=4] {'zh'}, dimensions={0}, use_global_device_ids=true | all-gather | bytes 491520 | tf_op jit(solution)/shard_map/all_gather | solution.py:280
  133.7 4.0 %collective-permute-start.5 = (f32[64,1536]{1,0:T(8,128)S(1)}, f32[64,1536]{1,0:T(8,128)S(1)}, u32[]{:S(2)}, u32[]{:S(2)}) collective-permute-start(f32[64,1536]{1,0:T(8,128)S(1)} %all_gather.3.p0), channel_id=1, source_target_pairs={{0,4},{4,8},{8,12},{12,0},{1,5},{5,9},{9,13},{13,1},{2,6},{6,10},{... | collective-permute-start | bytes 1179656 | tf_op jit(solution)/shard_map/ppermute | solution.py:24
  137.7 1.9 collective-permute-start.4
  139.6 3.3 %collective-permute-start.3 = (f32[64,1536]{1,0:T(8,128)S(1)}, f32[64,1536]{1,0:T(8,128)S(1)}, u32[]{:S(2)}, u32[]{:S(2)}) collective-permute-start(f32[64,1536]{1,0:T(8,128)S(1)} %all_gather.3.p0), channel_id=1, source_target_pairs={{0,12},{4,0},{8,4},{12,8},{1,13},{5,1},{9,5},{13,9},{2,14},{6,2},{... | collective-permute-start | bytes 1179656 | tf_op jit(solution)/shard_map/ppermute | solution.py:24
  142.9 4.3 %collective-permute-done.5.p3 = f32[64,1536]{1,0:T(8,128)S(1)} collective-permute-done((f32[64,1536]{1,0:T(8,128)S(1)}, f32[64,1536]{1,0:T(8,128)S(1)}, u32[]{:S(2)}, u32[]{:S(2)}) %collective-permute-start.5) | collective-permute-done | bytes 393248 | tf_op jit(solution)/shard_map/ppermute | solution.py:24
  147.2 1.8 collective-permute-done.4.p2
  148.9 4.1 %collective-permute-done.3.p1 = f32[64,1536]{1,0:T(8,128)S(1)} collective-permute-done((f32[64,1536]{1,0:T(8,128)S(1)}, f32[64,1536]{1,0:T(8,128)S(1)}, u32[]{:S(2)}, u32[]{:S(2)}) %collective-permute-start.3) | collective-permute-done | bytes 393248 | tf_op jit(solution)/shard_map/ppermute | solution.py:24
  153.1 0.7 copy-done.11
  153.8 9.2 %panel.1 = f32[256,1536]{1,0:T(8,128)} custom-call(s32[1]{0:T(128)} %bitcast.4.base_ref, f32[64,1536]{1,0:T(8,128)} %copy-done.5, f32[64,1536]{1,0:T(8,128)} %copy-done.11, f32[64,1536]{1,0:T(8,128)} %copy-done.10, f32[64,1536]{1,0:T(8,128)} %copy-done.9, f32[768,1536]{1,0:T(8,128)} %pad_maximum_fusion._.mine_ref, f32[768,1536]{1,0:T(8,128)} %collective-permute-done.6.other_ref), custom_call_target="tpu_custom_call" | custom-call | flops 3623878656 | bytes 12000000 | tf_op jit(solution)/shard_map/panel/pallas_call | solution.py:217
  163.0 34.7 %all_to_all.21 = f32[4,64,1536]{2,1,0:T(8,128)S(1)} all-to-all(f32[4,64,1536]{2,1,0:T(8,128)} %bitcast.8), channel_id=1, replica_groups=mesh['x'=4,'zl'=4,'core'=2,'y'=4,'zh'=4] {'x'}, dimensions={0} | all-to-all | bytes 3145728 | tf_op jit(solution)/shard_map/all_to_all | solution.py:258
  197.7 0.8 reduce_sum.37
  198.6 3.5 %all-to-all-start.3 = ((f32[4,16,1536]{2,1,0:T(8,128)}), f32[4,16,1536]{2,1,0:T(8,128)S(1)}, u32[]{:S(2)}, u32[]{:S(2)}) async-start(f32[4,16,1536]{2,1,0:T(8,128)} %bitcast.6), calls=%async_computation.3 | async-start | bytes 786432 | tf_op jit(solution)/shard_map/all_to_all | solution.py:258
  202.0 1.9 collective-permute-start.2
  204.0 1.2 collective-permute-done.2
  205.8 6.9 %all-to-all-done.3 = f32[4,16,1536]{2,1,0:T(8,128)S(1)} async-done(((f32[4,16,1536]{2,1,0:T(8,128)}), f32[4,16,1536]{2,1,0:T(8,128)S(1)}, u32[]{:S(2)}, u32[]{:S(2)}) %all-to-all-start.3) | async-done | bytes 393248 | tf_op jit(solution)/shard_map/all_to_all | solution.py:258
  (36 shorter events, 4.2 us)
Async XLA Ops:
  0.6 2.4 %copy-start = (f32[768,768]{1,0:T(8,128)S(1)}, f32[768,768]{1,0:T(8,128)}, u32[]{:S(2)}) copy-start(f32[768,768]{1,0:T(8,128)} %states_ref.3) | copy-start | bytes 7077892
  0.6 2.4 %copy-start.7 = (s32[64]{0:T(128)S(1)}, s32[64]{0:T(128)}, u32[]{:S(2)}) copy-start(s32[64]{0:T(128)} %param.10) | copy-start | bytes 772
  0.7 4.1 %copy-start.6 = (s32[12,125]{1,0:T(8,128)S(1)}, s32[12,125]{1,0:T(8,128)}, u32[]{:S(2)}) copy-start(s32[12,125]{1,0:T(8,128)} %param.9) | copy-start | bytes 18004
  3.0 3.8 %copy-start.4 = (f32[12,125,125]{2,1,0:T(8,128)S(1)}, f32[12,125,125]{2,1,0:T(8,128)}, u32[]{:S(2)}) copy-start(f32[12,125,125]{2,1,0:T(8,128)} %param.8) | copy-start | bytes 2250004
  3.4 10.3 %collective-permute-start = (f32[64,768]{1,0:T(8,128)S(1)}, f32[64,768]{1,0:T(8,128)S(1)}, u32[]{:S(2)}, u32[]{:S(2)}) collective-permute-start(f32[64,768]{1,0:T(8,128)S(1)} %fusion.4), channel_id=1, source_target_pairs={{16,0},{32,16},{48,32},{64,48},{80,64},{96,80},{112,96},{128,112},... | collective-permute-start | bytes 589832 | tf_op jit(solution)/shard_map/ppermute | solution.py:19
  13.7 21.5 %copy-start.1 = (f32[768,768]{1,0:T(8,128)S(1)}, f32[768,768]{1,0:T(8,128)}, u32[]{:S(2)}) copy-start(f32[768,768]{1,0:T(8,128)} %states_ref.3) | copy-start | bytes 7077892
  13.7 21.5 %copy-start.8 = (f32[768]{0:T(1024)S(1)}, f32[768]{0:T(1024)}, u32[]{:S(2)}) copy-start(f32[768]{0:T(1024)} %param.11) | copy-start | bytes 9220
  13.7 0.7 copy-start.12
  32.1 4.1 %collective-permute-start.1 = (f32[64,768]{1,0:T(8,128)S(1)}, f32[64,768]{1,0:T(8,128)S(1)}, u32[]{:S(2)}, u32[]{:S(2)}) collective-permute-start(f32[64,768]{1,0:T(8,128)S(1)} %slice.25), channel_id=1, source_target_pairs={{0,16},{16,32},{32,48},{48,64},{64,80},{80,96},{96,112},{112,128},... | collective-permute-start | bytes 589832 | tf_op jit(solution)/shard_map/ppermute | solution.py:19
  35.4 1.7 copy-start.3
  40.6 112.4 %collective-permute-start.6 = (f32[768,1536]{1,0:T(8,128)}, f32[768,1536]{1,0:T(8,128)}, u32[]{:S(2)}, u32[]{:S(2)}) collective-permute-start(f32[768,1536]{1,0:T(8,128)} %pad_maximum_fusion._.mine_ref), channel_id=1, source_target_pairs={{0,16},{16,0},{1,17},{17,1},{2,18},{18,2},{3,19},{19,3},{4,20},{20... | collective-permute-start | bytes 14155784 | tf_op jit(solution)/shard_map/ppermute | solution.py:24
  45.3 27.1 %all-to-all-start = ((f32[8,64,768]{2,1,0:T(8,128)}), f32[8,64,768]{2,1,0:T(8,128)S(1)}, u32[]{:S(2)}, u32[]{:S(2)}) async-start(f32[8,64,768]{2,1,0:T(8,128)} %bitcast.1), calls=%async_computation | async-start | bytes 3145728 | tf_op jit(solution)/shard_map/all_to_all | solution.py:258
  72.4 1.1 copy-start.2
  133.7 19.4 %copy-start.5 = (f32[64,1536]{1,0:T(8,128)}, f32[64,1536]{1,0:T(8,128)S(1)}, u32[]{:S(2)}) copy-start(f32[64,1536]{1,0:T(8,128)S(1)} %all_gather.3.p0) | copy-start | bytes 1179652
  133.7 13.5 %collective-permute-start.5 = (f32[64,1536]{1,0:T(8,128)S(1)}, f32[64,1536]{1,0:T(8,128)S(1)}, u32[]{:S(2)}, u32[]{:S(2)}) collective-permute-start(f32[64,1536]{1,0:T(8,128)S(1)} %all_gather.3.p0), channel_id=1, source_target_pairs={{0,4},{4,8},{8,12},{12,0},{1,5},{5,9},{9,13},{13,1},{2,6},{6,10},{... | collective-permute-start | bytes 1179656 | tf_op jit(solution)/shard_map/ppermute | solution.py:24
  137.7 11.3 %collective-permute-start.4 = (f32[64,1536]{1,0:T(8,128)S(1)}, f32[64,1536]{1,0:T(8,128)S(1)}, u32[]{:S(2)}, u32[]{:S(2)}) collective-permute-start(f32[64,1536]{1,0:T(8,128)S(1)} %all_gather.3.p0), channel_id=1, source_target_pairs={{0,8},{4,12},{8,0},{12,4},{1,9},{5,13},{9,1},{13,5},{2,10},{6,14},... | collective-permute-start | bytes 1179656 | tf_op jit(solution)/shard_map/ppermute | solution.py:24
  139.6 13.5 %collective-permute-start.3 = (f32[64,1536]{1,0:T(8,128)S(1)}, f32[64,1536]{1,0:T(8,128)S(1)}, u32[]{:S(2)}, u32[]{:S(2)}) collective-permute-start(f32[64,1536]{1,0:T(8,128)S(1)} %all_gather.3.p0), channel_id=1, source_target_pairs={{0,12},{4,0},{8,4},{12,8},{1,13},{5,1},{9,5},{13,9},{2,14},{6,2},{... | collective-permute-start | bytes 1179656 | tf_op jit(solution)/shard_map/ppermute | solution.py:24
  147.2 5.9 %copy-start.9 = (f32[64,1536]{1,0:T(8,128)}, f32[64,1536]{1,0:T(8,128)S(1)}, u32[]{:S(2)}) copy-start(f32[64,1536]{1,0:T(8,128)S(1)} %collective-permute-done.5.p3) | copy-start | bytes 1179652
  148.9 4.1 %copy-start.10 = (f32[64,1536]{1,0:T(8,128)}, f32[64,1536]{1,0:T(8,128)S(1)}, u32[]{:S(2)}) copy-start(f32[64,1536]{1,0:T(8,128)S(1)} %collective-permute-done.4.p2) | copy-start | bytes 1179652
  153.0 0.7 copy-start.11
  198.6 14.1 %all-to-all-start.3 = ((f32[4,16,1536]{2,1,0:T(8,128)}), f32[4,16,1536]{2,1,0:T(8,128)S(1)}, u32[]{:S(2)}, u32[]{:S(2)}) async-start(f32[4,16,1536]{2,1,0:T(8,128)} %bitcast.6), calls=%async_computation.3 | async-start | bytes 786432 | tf_op jit(solution)/shard_map/all_to_all | solution.py:258
  202.0 3.1 %collective-permute-start.2 = (f32[16,768]{1,0:T(8,128)S(1)}, f32[16,768]{1,0:T(8,128)S(1)}, u32[]{:S(2)}, u32[]{:S(2)}) collective-permute-start(f32[16,768]{1,0:T(8,128)S(1)} %slice.27), channel_id=1, source_target_pairs={{0,16},{16,0},{1,17},{17,1},{2,18},{18,2},{3,19},{19,3},{4,20},{20... | collective-permute-start | bytes 147464 | tf_op jit(solution)/shard_map/ppermute | solution.py:24

commit v4 on v1

v4 whole, which is shorter than its diff:
```python
import jax
import jax.numpy as jnp
from jax import lax
from jax.experimental import pallas as pl
from jax.experimental.pallas import tpu as pltpu
from jax.sharding import Mesh, PartitionSpec as P

FINE = ("x", "zl", "core", "y", "zh")
NODE = ("x", "zl", "core")
STATE = ("y", "zh")
VMEM = 56 * 1024 * 1024
F32 = jnp.float32
BF16 = jnp.bfloat16
HIGH = lax.Precision.HIGH


def node_shift(shard, by):
    length = lax.axis_size(NODE)
    pairs = [(i, i + by) for i in range(length) if 0 <= i + by < length]
    return lax.ppermute(shard, NODE, pairs)


def ring(shard, axis, by):
    length = lax.axis_size(axis)
    return lax.ppermute(shard, axis, [(i, (i + by) % length) for i in range(length)])


def halves(value):
    top = lax.reduce_precision(value, 8, 7)
    return top.astype(BF16), (value - top).astype(BF16)


def split(value):
    top = value.astype(BF16)
    return top, (value - top.astype(F32)).astype(BF16)


def dot(left, right, dims=((1,), (0,))):
    return lax.dot_general(left, right, (dims, ((), ())), preferred_element_type=F32)


def params():
    return pltpu.CompilerParams(vmem_limit_bytes=VMEM)


def cost(flops, moved):
    return pl.CostEstimate(flops=flops, bytes_accessed=moved, transcendentals=0)


ANY = pl.BlockSpec(memory_space=pl.ANY)


def rotate_kernel(
    coeffs_ref,
    states_ref,
    connect_ref,
    face_ref,
    mass_ref,
    out_ref,
    links_ref,
    table_ref,
    scale_ref,
    top_ref,
    low_ref,
):
    @pl.when(pl.program_id(0) == 0)
    def _():
        links_ref[...] = connect_ref[...]
        table_ref[...] = face_ref[...]
        scale_ref[...] = mass_ref[...]
        top, low = split(coeffs_ref[...].T)
        for y in range(4):
            for zh in range(4):
                for core in range(2):
                    source = ((y * 4 + zh) * 2 + core) * 16
                    place = ((y * 2 + core) * 4 + zh) * 16
                    top_ref[place : place + 16] = top[source : source + 16]
                    low_ref[place : place + 16] = low[source : source + 16]

    top, low = split(states_ref[...])
    dims = ((1,), (1,))
    out_ref[...] = (
        dot(top_ref[...], top, dims)
        + dot(low_ref[...], top, dims)
        + dot(top_ref[...], low, dims)
    )


def rotate(coeffs, states, connect, face_list, node_mass):
    width, block = coeffs.shape
    owned = states.shape[0]
    tile = 256
    fixed = lambda shape: pl.BlockSpec(shape, lambda i: (0, 0))
    small = [connect, face_list.reshape(1, -1), node_mass.reshape(1, -1)]
    return pl.pallas_call(
        rotate_kernel,
        grid=(owned // tile,),
        in_specs=[
            fixed((width, block)),
            pl.BlockSpec((tile, width), lambda i: (i, 0)),
        ]
        + [fixed(a.shape) for a in small],
        out_specs=[
            pl.BlockSpec((block, tile), lambda i: (0, i)),
        ]
        + [fixed(a.shape) for a in small],
        out_shape=[
            jax.ShapeDtypeStruct((block, owned), F32),
        ]
        + [jax.ShapeDtypeStruct(a.shape, a.dtype) for a in small],
        scratch_shapes=[pltpu.VMEM((block, width), BF16)] * 2,
        compiler_params=params(),
        cost_estimate=cost(6 * block * owned * width, 6000000),
        name="rotate",
    )(coeffs, states, *small)


def cells_kernel(connect_ref, cell_ref, states_ref, ghost_ref, out_ref, pair_ref, link_ref, h_ref):
    owned = states_ref.shape[0]
    total, width = out_ref.shape
    depth = pair_ref.shape[0] // 2
    cells, per_cell = connect_ref.shape
    side, count = h_ref.shape[1], h_ref.shape[0]
    many = count * side

    for place, ref in ((0, states_ref), (owned, ghost_ref)):
        top, low = split(ref[...])
        end = place + ref.shape[0]
        pair_ref[place:end] = top
        pair_ref[depth + place : depth + end] = low
    blank = jnp.zeros((depth - total, width), BF16)
    pair_ref[total:depth] = blank
    pair_ref[depth + total :] = blank
    link_ref[...] = jnp.full(link_ref.shape, -1.0, F32)
    link_ref[:cells, :per_cell] = connect_ref[...].astype(F32)
    h_ref[...] = jnp.zeros_like(h_ref)
    links = link_ref[...]
    columns = links.T
    along = lax.broadcasted_iota(jnp.int32, (side, depth), 1).astype(F32)
    down = lax.broadcasted_iota(jnp.int32, (total, side), 0).astype(F32)

    for first in range(0, cells, count):
        group = range(first, first + count)
        gather = jnp.concatenate(
            [(along == columns[:, c : c + 1]).astype(F32).astype(BF16) for c in group], axis=0
        )
        scatter = jnp.concatenate(
            [(down == links[c : c + 1]).astype(F32).astype(BF16) for c in group], axis=1
        )
        top, low = split(dot(jnp.concatenate([gather, gather], axis=1), pair_ref[...]))
        results = []
        for k, c in enumerate(group):
            h_ref[k, :per_cell, :per_cell] = cell_ref[c]
            cell = h_ref[k]
            cell_top, cell_low = split(0.5 * (cell + cell.T))
            rows = slice(k * side, (k + 1) * side)
            results.append(
                dot(
                    jnp.concatenate([cell_top, cell_low, cell_top], axis=1),
                    jnp.concatenate([top[rows], top[rows], low[rows]], axis=0),
                )
            )
        top, low = split(jnp.concatenate(results, axis=0))
        value = dot(
            jnp.concatenate([scatter, scatter], axis=1), jnp.concatenate([top, low], axis=0)
        )
        out_ref[...] = value if first == 0 else out_ref[...] + value


def cells_apply(states, ghosts, cell_matrix, connect):
    owned, width = states.shape
    total = owned + ghosts.shape[0]
    depth = -(-total // 128) * 128
    cells = connect.shape[0]
    side, count = 128, 4
    return pl.pallas_call(
        cells_kernel,
        out_shape=jax.ShapeDtypeStruct((total, width), F32),
        in_specs=[pl.BlockSpec(memory_space=pltpu.VMEM)] * 4,
        out_specs=pl.BlockSpec(memory_space=pltpu.VMEM),
        scratch_shapes=[
            pltpu.VMEM((2 * depth, width), BF16),
            pltpu.VMEM((16, side), F32),
            pltpu.VMEM((count, side, side), F32),
        ],
        compiler_params=params(),
        cost_estimate=cost(8 * cells * side * total * width, 9000000),
        name="cells",
    )(connect, cell_matrix, states, ghosts)


def face_pick(table, value, dims):
    top, low = halves(value)
    return dot(table, top, dims) + dot(table, low, dims)


def tie_kernel(*refs):
    pass


def tie(*arrays):
    return pl.pallas_call(
        tie_kernel,
        in_specs=[ANY] * len(arrays),
        out_specs=[ANY] * len(arrays),
        out_shape=[jax.ShapeDtypeStruct(a.shape, a.dtype) for a in arrays],
        input_output_aliases={i: i for i in range(len(arrays))},
        name="tie",
    )(*arrays)


def swap(pieces, axis):
    return lax.all_to_all(pieces, axis, 0, 0, tiled=True)


def spread_sum(pieces, axis):
    length = lax.axis_size(axis)
    here = lax.axis_index(axis)
    part = lambda by: lax.dynamic_index_in_dim(pieces, (here + by) % length, 0, keepdims=False)
    return sum((ring(part(by), axis, by) for by in range(1, length)), part(0))


def gather_rows(rows, axis):
    length = lax.axis_size(axis)
    here = lax.axis_index(axis)
    out = jnp.zeros((length,) + rows.shape, rows.dtype)
    out = lax.dynamic_update_slice_in_dim(out, rows[None], here, 0)
    for by in (1, length - 1, 2):
        out = lax.dynamic_update_slice_in_dim(
            out, ring(rows, axis, by)[None], (here - by) % length, 0
        )
    return out.reshape((-1,) + rows.shape[1:])


def local(states, coeffs, cell_matrix, connect, face_list, node_mass):
    owned, width = states.shape
    block = coeffs.shape[1]
    first = lax.axis_index("core") == 0

    partial, links, faces, mass = rotate(coeffs, states, connect, face_list, node_mass)
    pieces = swap(partial.reshape(8, block // 8, owned), ("y", "core"))

    weighted = states * mass.reshape(-1, 1)
    weighted_other = ring(weighted, "core", 1)
    table = (faces.reshape(-1, 1) == jnp.arange(owned)[None, :]).astype(BF16)
    ghosts = node_shift(face_pick(table, states, ((1,), (0,))), -1)
    assembled = cells_apply(states, ghosts, cell_matrix, links)

    over_y = jnp.sum(pieces.reshape(4, 2, block // 8, owned), axis=0)
    over_y = jnp.concatenate(
        [jnp.where(first, over_y[0], over_y[1]), jnp.where(first, over_y[1], over_y[0])], axis=1
    )
    over_y, assembled = tie(over_y, assembled)
    both = jnp.sum(swap(over_y.reshape(4, block // 32, 2 * owned), "zh"), axis=0)

    returned = node_shift(assembled[owned:], 1)
    applied = assembled[:owned] + face_pick(table, returned, ((0,), (0,)))
    parts = 4
    applied_other = jnp.concatenate(
        [ring(part, "core", 1) for part in jnp.split(applied, parts, axis=0)], axis=0
    )

    own, theirs = both[:, :owned], ring(both[:, owned:], "core", 1)
    rotated = jnp.concatenate(
        [jnp.where(first, own, theirs), jnp.where(first, theirs, own)], axis=0
    )

    rows = gather_rows(lax.all_gather(both, "zh", axis=0, tiled=True), "y")

    def panel(here, there):
        return sum(
            jnp.dot(part, weight, precision=HIGH, preferred_element_type=F32)
            for part, weight in ((rows[:, :owned], here), (rows[:, owned:], there))
        ).reshape(4, block // 8, width)

    def over_x(value):
        return jnp.sum(swap(value, "x"), axis=0).reshape(4, block // 32, width)

    m_panel = spread_sum(over_x(panel(weighted, weighted_other)), "zl")
    h_panel = jnp.sum(swap(over_x(panel(applied, applied_other)), "zl"), axis=0)
    return rotated, h_panel, m_panel


def solution(mesh):
    fine = Mesh(mesh.devices.reshape(4, 4, 2, 4, 4), FINE)
    return jax.shard_map(
        local,
        mesh=fine,
        in_specs=(
            P(NODE, STATE),
            P(STATE, None),
            P(NODE, None, None),
            P(NODE, None),
            P(NODE),
            P(NODE),
        ),
        out_specs=(P(STATE, NODE), P(NODE, STATE), P(NODE, STATE)),
        check_vma=False,
    )
```

time: 194 us -> 201 us (1.036)
  starting transfers between devices: 32.7 us -> 78.8 us
  blocking collectives: 71.5 us -> 34.9 us
  matrix products: 41.7 us -> 15.5 us
  Pallas kernels: 0 us -> 20.7 us
  waiting for transfers between devices: 19.3 us -> 35.4 us
  local copies, waits for them, and re-layouts: 16.1 us -> 4.53 us
  other arithmetic: 8.82 us -> 6.69 us
    all_to_all x3 -> x0, blocking collectives: 45.8 us -> none  [spread_sum(): return jnp.sum(lax.all_to_all(pieces, axis, 0, 0, tiled=True), axis=0)]
    ppermute x3 -> x12, starting transfers between devices: 9.2 us -> 40.2 us  [ring(): lax.ppermute(shard, axis, [(i, (i + by) % length) for i in range(length)])]
    dot_general x11 -> x8, matrix products: 41.7 us -> 15.5 us  [the longest x4 11.8 us: panel(): jnp.dot(part, weight, precision=HIGH, preferred_element_type=F32)]
    pallas_call x0 -> x3, Pallas kernels: none -> 20.7 us  [the longest x1 14.7 us: cells_apply(): pl.pallas_call(cells_kernel, out_shape=jax.ShapeDtypeStruct((total, width...]
    all_to_all x2 -> x5, starting transfers between devices: 20 us -> 31.5 us  [swap(): return lax.all_to_all(pieces, axis, 0, 0, tiled=True)]
    all_gather x1, blocking collectives: 25.7 us -> 34.9 us  [local(): rows = gather_rows(lax.all_gather(both, 'zh', axis=0, tiled=True), 'y')]
    all_to_all x2 -> x5, waiting for transfers between devices: 6.84 us -> 14.5 us  [swap(): return lax.all_to_all(pieces, axis, 0, 0, tiled=True)]
    reshape x2 -> x1, local copies, waits for them, and re-layouts: 8.76 us -> 1.27 us  [rotate(): small = [connect, face_list.reshape(1, -1), node_mass.reshape(1, -1)]]
  transfers between devices with their start and end apart: 7 -> 19, of which waited for: 4 -> 8; matrix products, arithmetic and copies ran while one was open for 27% -> 11% of each run, Pallas kernels for 0% -> 7%
where the time goes in v4:
time: 201 us; the launch traced here: 198 us
  starting transfers between devices  78.8 us (39%)
  waiting for transfers between devices  35.4 us (18%)
  blocking collectives  34.9 us (17%)
  Pallas kernels  20.7 us (10%)
  matrix products  15.5 us (8%)
  other arithmetic  6.69 us (3%)
  local copies, waits for them, and re-layouts  4.53 us (2%)
    ppermute x12, starting transfers between devices, ring(): lax.ppermute(shard, axis, [(i, (i + by) % length) for i in range(length)])  40.2 us
    all_gather x1, blocking collectives, local(): rows = gather_rows(lax.all_gather(both, 'zh', axis=0, tiled=True), 'y')  34.9 us
    all_to_all x5, starting transfers between devices, swap(): return lax.all_to_all(pieces, axis, 0, 0, tiled=True)  31.5 us
    ppermute x12, waiting for transfers between devices, ring(): lax.ppermute(shard, axis, [(i, (i + by) % length) for i in range(length)])  18.9 us
    pallas_call x1, Pallas kernels, cells_apply(): pl.pallas_call(cells_kernel, out_shape=jax.ShapeDtypeStruct((total, width...  14.7 us
    all_to_all x5, waiting for transfers between devices, swap(): return lax.all_to_all(pieces, axis, 0, 0, tiled=True)  14.5 us
    dot_general x4, matrix products, panel(): jnp.dot(part, weight, precision=HIGH, preferred_element_type=F32)  11.8 us
    ppermute x2, starting transfers between devices, node_shift(): return lax.ppermute(shard, NODE, pairs)  7.06 us
  transfers between devices with their start and end apart: 19, of which 8 were waited for; matrix products, arithmetic and copies ran while one was open for 11% of the time, Pallas kernels for 7%

profile of v4, /device:TPU:24, one launch (start us, length us, event | category | flops | bytes accessed | tf_op | source)
XLA Modules:
  0.0 197.6 jit_solution(11524560657509645442)
XLA Ops:
  1.9 5.9 %rotate.1 = (f32[512,768]{1,0:T(8,128)}, s32[12,125]{1,0:T(8,128)}, s32[1,64]{1,0:T(1,128)}, f32[1,768]{1,0:T(1,128)}) custom-call(f32[768,512]{1,0:T(8,128)} %coeffs_ref.1, f32[768,768]{1,0:T(8,128)} %states_ref.3, s32[12,125]{1,0:T(8,128)} %connect_ref.1, s32[1,64]{1,0:T(1,128)} %bitcast.49, f32[1,768]{1,0:T(1,128)} %reshape.45.mass_ref), custom_call_target="tpu_custom_call" | custom-call | flops 1811939328 | bytes 6000000 | tf_op jit(solution)/shard_map/rotate/pallas_call | solution.py:95
  7.8 9.9 %all-to-all-start = ((f32[8,64,768]{2,1,0:T(8,128)}), f32[8,64,768]{2,1,0:T(8,128)}, u32[]{:S(2)}, u32[]{:S(2)}) async-start(f32[8,64,768]{2,1,0:T(8,128)} %bitcast.42), calls=%async_computation | async-start | bytes 3145728 | tf_op jit(solution)/shard_map/all_to_all | solution.py:213
  19.9 2.0 %collective-permute-done.ghost_ref = f32[64,768]{1,0:T(8,128)S(1)} collective-permute-done((f32[64,768]{1,0:T(8,128)S(1)}, f32[64,768]{1,0:T(8,128)S(1)}, u32[]{:S(2)}, u32[]{:S(2)}) %collective-permute-start) | collective-permute-done | bytes 196640 | tf_op jit(solution)/shard_map/ppermute | solution.py:20
  22.6 14.7 %cells.1.refs_1_ = f32[832,768]{1,0:T(8,128)} custom-call(s32[12,125]{1,0:T(8,128)} %get-tuple-element.10.connect_ref, f32[12,125,125]{2,1,0:T(8,128)} %cell_ref.1, f32[768,768]{1,0:T(8,128)} %states_ref.3, f32[64,768]{1,0:T(8,128)} %copy-done.7), custom_call_target="tpu_custom_call" | custom-call | flops 7851737088 | bytes 9000000 | tf_op jit(solution)/shard_map/cells/pallas_call | solution.py:176
  39.7 10.1 %all-to-all-start.1 = ((f32[4,16,1536]{2,1,0:T(8,128)}), f32[4,16,1536]{2,1,0:T(8,128)S(1)}, u32[]{:S(2)}, u32[]{:S(2)}) async-start(f32[4,16,1536]{2,1,0:T(8,128)} %bitcast.41), calls=%async_computation.1 | async-start | bytes 786432 | tf_op jit(solution)/shard_map/all_to_all | solution.py:213
  50.8 5.8 %collective-permute-start.5 = (f32[64,768]{1,0:T(8,128)S(1)}, f32[64,768]{1,0:T(8,128)S(1)}, u32[]{:S(2)}, u32[]{:S(2)}) collective-permute-start(f32[64,768]{1,0:T(8,128)S(1)} %slice.34), channel_id=1, source_target_pairs={{0,16},{16,32},{32,48},{48,64},{64,80},{80,96},{96,112},{112,128},... | collective-permute-start | bytes 589832 | tf_op jit(solution)/shard_map/ppermute | solution.py:20
  58.2 2.1 %collective-permute-start.10 = (f32[768,768]{1,0:T(8,128)}, f32[768,768]{1,0:T(8,128)}, u32[]{:S(2)}, u32[]{:S(2)}) collective-permute-start(f32[768,768]{1,0:T(8,128)} %broadcast_multiply_fusion), channel_id=1, source_target_pairs={{0,16},{16,0},{1,17},{17,1},{2,18},{18,2},{3,19},{19,3},{4,20},{20... | collective-permute-start | bytes 7077896 | tf_op jit(solution)/shard_map/ppermute | solution.py:25
  61.0 2.3 %add_add_fusion = f32[768,768]{1,0:T(8,128)S(1)} fusion(f32[768,768]{1,0:T(8,128)S(1)} %fusion.19, f32[832,768]{1,0:T(8,128)} %get-tuple-element.13, f32[64,768]{1,0:T(8,128)S(1)} %collective-permute-done.5, s32[64]{0:T(128)S(1)} %bitcast.48), kind=kOutput, calls=%fused_computation.11 | convolution fusion | flops 76824576 | bytes 7274752 | tf_op jit(solution)/shard_map/dot_general | solution.py:39
  64.6 4.6 %collective-permute-start.9 = (f32[192,768]{1,0:T(8,128)}, f32[192,768]{1,0:T(8,128)}, u32[]{:S(2)}, u32[]{:S(2)}) collective-permute-start(f32[192,768]{1,0:T(8,128)} %get-tuple-element.16), channel_id=1, source_target_pairs={{0,16},{16,0},{1,17},{17,1},{2,18},{18,2},{3,19},{19,3},{4,20},{20... | collective-permute-start | bytes 1769480 | tf_op jit(solution)/shard_map/ppermute | solution.py:25
  69.3 1.9 collective-permute-start.8
  71.3 34.9 %all_gather.3 = f32[64,1536]{1,0:T(8,128)S(1)} all-gather(f32[16,1536]{1,0:T(8,128)S(1)} %reduce_sum.46), channel_id=1, replica_groups=mesh['x'=4,'zl'=4,'core'=2,'y'=4,'zh'=4] {'zh'}, dimensions={0}, use_global_device_ids=true | all-gather | bytes 491520 | tf_op jit(solution)/shard_map/all_gather | solution.py:268
  106.1 8.9 %collective-permute-start.2 = (f32[64,1536]{1,0:T(8,128)S(1)}, f32[64,1536]{1,0:T(8,128)S(1)}, u32[]{:S(2)}, u32[]{:S(2)}) collective-permute-start(f32[64,1536]{1,0:T(8,128)S(1)} %all_gather.3), channel_id=1, source_target_pairs={{0,4},{4,8},{8,12},{12,0},{1,5},{5,9},{9,13},{13,1},{2,6},{6,10},{... | collective-permute-start | bytes 1179656 | tf_op jit(solution)/shard_map/ppermute | solution.py:25
  115.0 1.9 collective-permute-start.3
  117.2 3.1 %collective-permute-done.2 = f32[64,1536]{1,0:T(8,128)S(1)} collective-permute-done((f32[64,1536]{1,0:T(8,128)S(1)}, f32[64,1536]{1,0:T(8,128)S(1)}, u32[]{:S(2)}, u32[]{:S(2)}) %collective-permute-start.2) | collective-permute-done | bytes 393248 | tf_op jit(solution)/shard_map/ppermute | solution.py:25
  120.3 3.8 %collective-permute-start.4 = (f32[64,1536]{1,0:T(8,128)S(1)}, f32[64,1536]{1,0:T(8,128)S(1)}, u32[]{:S(2)}, u32[]{:S(2)}) collective-permute-start(f32[64,1536]{1,0:T(8,128)S(1)} %all_gather.3), channel_id=1, source_target_pairs={{0,8},{4,12},{8,0},{12,4},{1,9},{5,13},{9,1},{13,5},{2,10},{6,14},... | collective-permute-start | bytes 1179656 | tf_op jit(solution)/shard_map/ppermute | solution.py:25
  124.2 10.2 %collective-permute-done.3 = f32[64,1536]{1,0:T(8,128)S(1)} collective-permute-done((f32[64,1536]{1,0:T(8,128)S(1)}, f32[64,1536]{1,0:T(8,128)S(1)}, u32[]{:S(2)}, u32[]{:S(2)}) %collective-permute-start.3) | collective-permute-done | bytes 393248 | tf_op jit(solution)/shard_map/ppermute | solution.py:25
  134.3 1.9 collective-permute-start.7
  136.3 2.4 %collective-permute-start.6 = (f32[192,768]{1,0:T(8,128)S(1)}, f32[192,768]{1,0:T(8,128)S(1)}, u32[]{:S(2)}, u32[]{:S(2)}) collective-permute-start(f32[192,768]{1,0:T(8,128)S(1)} %get-tuple-element.15), channel_id=1, source_target_pairs={{0,16},{16,0},{1,17},{17,1},{2,18},{18,2},{3,19},{19,3},{4,20},{20... | collective-permute-start | bytes 1769480 | tf_op jit(solution)/shard_map/ppermute | solution.py:25
  140.3 2.5 %fusion.1 = f32[256,768]{1,0:T(8,128)S(1)} fusion(f32[192,768]{1,0:T(8,128)} %collective-permute-done.9, f32[192,768]{1,0:T(8,128)} %collective-permute-done.8, f32[192,768]{1,0:T(8,128)S(1)} %collective-permute-done.7, f32[192,768]{1,0:T(8,128)S(1)} %collective-permute-done.6, f32[256,1536]{1,0:T(8,128)S(1)} %bitcast.37), kind=kOutput, calls=%fused_computation.3 | convolution fusion | flops 907739136 | bytes 3932160 | tf_op jit(solution)/shard_map/dot_general | solution.py:272
  142.8 2.2 %convolution_add_fusion.1 = f32[256,768]{1,0:T(8,128)} fusion(f32[256,768]{1,0:T(8,128)S(1)} %fusion.1, f32[768,768]{1,0:T(8,128)S(1)} %add_add_fusion, f32[256,1536]{1,0:T(8,128)S(1)} %bitcast.38), kind=kOutput, calls=%fused_computation.13 | convolution fusion | flops 906166272 | bytes 4718592 | tf_op jit(solution)/shard_map/dot_general | solution.py:272
  145.1 4.6 %all-to-all-start.2 = ((f32[4,64,768]{2,1,0:T(8,128)}), f32[4,64,768]{2,1,0:T(8,128)S(1)}, u32[]{:S(2)}, u32[]{:S(2)}) async-start(f32[4,64,768]{2,1,0:T(8,128)} %bitcast.12), calls=%async_computation.2 | async-start | bytes 1572864 | tf_op jit(solution)/shard_map/all_to_all | solution.py:213
  149.7 3.3 %fusion.13 = f32[256,768]{1,0:T(8,128)S(1)} fusion(f32[768,768]{1,0:T(8,128)} %collective-permute-done.10, f32[256,1536]{1,0:T(8,128)} %bitcast.39), kind=kOutput, calls=%fused_computation.18 | convolution fusion | flops 905969664 | bytes 3932160 | tf_op jit(solution)/shard_map/dot_general | solution.py:272
  152.9 3.8 %convolution_add_fusion = f32[256,768]{1,0:T(8,128)} fusion(f32[256,768]{1,0:T(8,128)S(1)} %fusion.13, f32[768,768]{1,0:T(8,128)} %broadcast_multiply_fusion, f32[256,1536]{1,0:T(8,128)S(1)} %bitcast.40), kind=kOutput, calls=%fused_computation.12 | convolution fusion | flops 906166272 | bytes 4718592 | tf_op jit(solution)/shard_map/dot_general | solution.py:272
  156.8 5.5 %all-to-all-done.2 = f32[4,64,768]{2,1,0:T(8,128)S(1)} async-done(((f32[4,64,768]{2,1,0:T(8,128)}), f32[4,64,768]{2,1,0:T(8,128)S(1)}, u32[]{:S(2)}, u32[]{:S(2)}) %all-to-all-start.2) | async-done | bytes 786464 | tf_op jit(solution)/shard_map/all_to_all | solution.py:213
  162.3 3.5 %all-to-all-start.4 = ((f32[4,64,768]{2,1,0:T(8,128)}), f32[4,64,768]{2,1,0:T(8,128)S(1)}, u32[]{:S(2)}, u32[]{:S(2)}) async-start(f32[4,64,768]{2,1,0:T(8,128)} %bitcast.14), calls=%async_computation.4 | async-start | bytes 1572864 | tf_op jit(solution)/shard_map/all_to_all | solution.py:213
  165.8 1.9 collective-permute-start.1
  168.5 9.0 %all-to-all-done.4 = f32[4,64,768]{2,1,0:T(8,128)S(1)} async-done(((f32[4,64,768]{2,1,0:T(8,128)}), f32[4,64,768]{2,1,0:T(8,128)S(1)}, u32[]{:S(2)}, u32[]{:S(2)}) %all-to-all-start.4) | async-done | bytes 786464 | tf_op jit(solution)/shard_map/all_to_all | solution.py:213
  177.4 3.4 %all-to-all-start.3 = ((f32[4,16,768]{2,1,0:T(8,128)}), f32[4,16,768]{2,1,0:T(8,128)S(1)}, u32[]{:S(2)}, u32[]{:S(2)}) async-start(f32[4,16,768]{2,1,0:T(8,128)} %bitcast.13), calls=%async_computation.3 | async-start | bytes 393216 | tf_op jit(solution)/shard_map/all_to_all | solution.py:213
  180.9 5.7 %collective-permute-start.13 = (f32[16,768]{1,0:T(8,128)S(1)}, f32[16,768]{1,0:T(8,128)S(1)}, u32[]{:S(2)}, u32[]{:S(2)}) collective-permute-start(f32[16,768]{1,0:T(8,128)S(1)} %get-tuple-element.22), channel_id=1, source_target_pairs={{0,96},{32,0},{64,32},{96,64},{1,97},{33,1},{65,33},{97,65},{2,98}... | collective-permute-start | bytes 147464 | tf_op jit(solution)/shard_map/ppermute | solution.py:25
  186.6 1.9 collective-permute-start.12
  188.6 3.0 %collective-permute-start.11 = (f32[16,768]{1,0:T(8,128)S(1)}, f32[16,768]{1,0:T(8,128)S(1)}, u32[]{:S(2)}, u32[]{:S(2)}) collective-permute-start(f32[16,768]{1,0:T(8,128)S(1)} %get-tuple-element.21), channel_id=1, source_target_pairs={{0,32},{32,64},{64,96},{96,0},{1,33},{33,65},{65,97},{97,1},{2,34}... | collective-permute-start | bytes 147464 | tf_op jit(solution)/shard_map/ppermute | solution.py:25
  193.5 2.8 %collective-permute-done.11 = f32[16,768]{1,0:T(8,128)S(1)} collective-permute-done((f32[16,768]{1,0:T(8,128)S(1)}, f32[16,768]{1,0:T(8,128)S(1)}, u32[]{:S(2)}, u32[]{:S(2)}) %collective-permute-start.11) | collective-permute-done | bytes 49184 | tf_op jit(solution)/shard_map/ppermute | solution.py:25
  (56 shorter events, 16.7 us)
Async XLA Ops:
  7.8 9.9 %copy-start = (f32[768,768]{1,0:T(8,128)S(1)}, f32[768,768]{1,0:T(8,128)}, u32[]{:S(2)}) copy-start(f32[768,768]{1,0:T(8,128)} %states_ref.3) | copy-start | bytes 7077892
  7.8 9.9 %copy-start.5 = (s32[1,64]{1,0:T(1,128)S(1)}, s32[1,64]{1,0:T(1,128)}, u32[]{:S(2)}) copy-start(s32[1,64]{1,0:T(1,128)} %get-tuple-element.11) | copy-start | bytes 772
  7.8 29.5 %all-to-all-start = ((f32[8,64,768]{2,1,0:T(8,128)}), f32[8,64,768]{2,1,0:T(8,128)}, u32[]{:S(2)}, u32[]{:S(2)}) async-start(f32[8,64,768]{2,1,0:T(8,128)} %bitcast.42), calls=%async_computation | async-start | bytes 3145728 | tf_op jit(solution)/shard_map/all_to_all | solution.py:213
  17.8 2.1 %copy-start.6 = (f32[1,768]{1,0:T(1,128)S(1)}, f32[1,768]{1,0:T(1,128)}, u32[]{:S(2)}) copy-start(f32[1,768]{1,0:T(1,128)} %get-tuple-element.14) | copy-start | bytes 9220
  18.6 3.3 %collective-permute-start = (f32[64,768]{1,0:T(8,128)S(1)}, f32[64,768]{1,0:T(8,128)S(1)}, u32[]{:S(2)}, u32[]{:S(2)}) collective-permute-start(f32[64,768]{1,0:T(8,128)S(1)} %fusion.12), channel_id=1, source_target_pairs={{16,0},{32,16},{48,32},{64,48},{80,64},{96,80},{112,96},{128,112},... | collective-permute-start | bytes 589832 | tf_op jit(solution)/shard_map/ppermute | solution.py:20
  21.9 0.7 copy-start.7
  39.0 17.6 %copy-start.1 = (f32[768,768]{1,0:T(8,128)S(1)}, f32[768,768]{1,0:T(8,128)}, u32[]{:S(2)}) copy-start(f32[768,768]{1,0:T(8,128)} %states_ref.3) | copy-start | bytes 7077892
  39.7 31.5 %all-to-all-start.1 = ((f32[4,16,1536]{2,1,0:T(8,128)}), f32[4,16,1536]{2,1,0:T(8,128)S(1)}, u32[]{:S(2)}, u32[]{:S(2)}) async-start(f32[4,16,1536]{2,1,0:T(8,128)} %bitcast.41), calls=%async_computation.1 | async-start | bytes 786432 | tf_op jit(solution)/shard_map/all_to_all | solution.py:213
  50.8 9.6 %collective-permute-start.5 = (f32[64,768]{1,0:T(8,128)S(1)}, f32[64,768]{1,0:T(8,128)S(1)}, u32[]{:S(2)}, u32[]{:S(2)}) collective-permute-start(f32[64,768]{1,0:T(8,128)S(1)} %slice.34), channel_id=1, source_target_pairs={{0,16},{16,32},{32,48},{48,64},{64,80},{80,96},{96,112},{112,128},... | collective-permute-start | bytes 589832 | tf_op jit(solution)/shard_map/ppermute | solution.py:20
  58.2 91.4 %collective-permute-start.10 = (f32[768,768]{1,0:T(8,128)}, f32[768,768]{1,0:T(8,128)}, u32[]{:S(2)}, u32[]{:S(2)}) collective-permute-start(f32[768,768]{1,0:T(8,128)} %broadcast_multiply_fusion), channel_id=1, source_target_pairs={{0,16},{16,0},{1,17},{17,1},{2,18},{18,2},{3,19},{19,3},{4,20},{20... | collective-permute-start | bytes 7077896 | tf_op jit(solution)/shard_map/ppermute | solution.py:25
  64.6 74.1 %collective-permute-start.9 = (f32[192,768]{1,0:T(8,128)}, f32[192,768]{1,0:T(8,128)}, u32[]{:S(2)}, u32[]{:S(2)}) collective-permute-start(f32[192,768]{1,0:T(8,128)} %get-tuple-element.16), channel_id=1, source_target_pairs={{0,16},{16,0},{1,17},{17,1},{2,18},{18,2},{3,19},{19,3},{4,20},{20... | collective-permute-start | bytes 1769480 | tf_op jit(solution)/shard_map/ppermute | solution.py:25
  69.3 69.5 %collective-permute-start.8 = (f32[192,768]{1,0:T(8,128)}, f32[192,768]{1,0:T(8,128)}, u32[]{:S(2)}, u32[]{:S(2)}) collective-permute-start(f32[192,768]{1,0:T(8,128)} %get-tuple-element.17), channel_id=1, source_target_pairs={{0,16},{16,0},{1,17},{17,1},{2,18},{18,2},{3,19},{19,3},{4,20},{20... | collective-permute-start | bytes 1769480 | tf_op jit(solution)/shard_map/ppermute | solution.py:25
  71.3 63.1 %copy-start.4 = (f32[192,768]{1,0:T(8,128)S(1)}, f32[192,768]{1,0:T(8,128)}, u32[]{:S(2)}) copy-start(f32[192,768]{1,0:T(8,128)} %get-tuple-element.18) | copy-start | bytes 1769476
  106.1 14.2 %collective-permute-start.2 = (f32[64,1536]{1,0:T(8,128)S(1)}, f32[64,1536]{1,0:T(8,128)S(1)}, u32[]{:S(2)}, u32[]{:S(2)}) collective-permute-start(f32[64,1536]{1,0:T(8,128)S(1)} %all_gather.3), channel_id=1, source_target_pairs={{0,4},{4,8},{8,12},{12,0},{1,5},{5,9},{9,13},{13,1},{2,6},{6,10},{... | collective-permute-start | bytes 1179656 | tf_op jit(solution)/shard_map/ppermute | solution.py:25
  115.0 19.3 %collective-permute-start.3 = (f32[64,1536]{1,0:T(8,128)S(1)}, f32[64,1536]{1,0:T(8,128)S(1)}, u32[]{:S(2)}, u32[]{:S(2)}) collective-permute-start(f32[64,1536]{1,0:T(8,128)S(1)} %all_gather.3), channel_id=1, source_target_pairs={{0,12},{4,0},{8,4},{12,8},{1,13},{5,1},{9,5},{13,9},{2,14},{6,2},{... | collective-permute-start | bytes 1179656 | tf_op jit(solution)/shard_map/ppermute | solution.py:25
  120.3 16.0 %collective-permute-start.4 = (f32[64,1536]{1,0:T(8,128)S(1)}, f32[64,1536]{1,0:T(8,128)S(1)}, u32[]{:S(2)}, u32[]{:S(2)}) collective-permute-start(f32[64,1536]{1,0:T(8,128)S(1)} %all_gather.3), channel_id=1, source_target_pairs={{0,8},{4,12},{8,0},{12,4},{1,9},{5,13},{9,1},{13,5},{2,10},{6,14},... | collective-permute-start | bytes 1179656 | tf_op jit(solution)/shard_map/ppermute | solution.py:25
  134.3 4.5 %collective-permute-start.7 = (f32[192,768]{1,0:T(8,128)S(1)}, f32[192,768]{1,0:T(8,128)S(1)}, u32[]{:S(2)}, u32[]{:S(2)}) collective-permute-start(f32[192,768]{1,0:T(8,128)S(1)} %copy-done.4), channel_id=1, source_target_pairs={{0,16},{16,0},{1,17},{17,1},{2,18},{18,2},{3,19},{19,3},{4,20},{20... | collective-permute-start | bytes 1769480 | tf_op jit(solution)/shard_map/ppermute | solution.py:25
  136.3 4.0 %collective-permute-start.6 = (f32[192,768]{1,0:T(8,128)S(1)}, f32[192,768]{1,0:T(8,128)S(1)}, u32[]{:S(2)}, u32[]{:S(2)}) collective-permute-start(f32[192,768]{1,0:T(8,128)S(1)} %get-tuple-element.15), channel_id=1, source_target_pairs={{0,16},{16,0},{1,17},{17,1},{2,18},{18,2},{3,19},{19,3},{4,20},{20... | collective-permute-start | bytes 1769480 | tf_op jit(solution)/shard_map/ppermute | solution.py:25
  138.8 4.1 %copy-start.2 = (f32[4,64,1536]{2,1,0:T(8,128)}, f32[4,64,1536]{2,1,0:T(8,128)S(1)}, u32[]{:S(2)}) copy-start(f32[4,64,1536]{2,1,0:T(8,128)S(1)} %bitcast_dynamic-update-slice_fusion) | copy-start | bytes 4718596
  145.1 17.2 %all-to-all-start.2 = ((f32[4,64,768]{2,1,0:T(8,128)}), f32[4,64,768]{2,1,0:T(8,128)S(1)}, u32[]{:S(2)}, u32[]{:S(2)}) async-start(f32[4,64,768]{2,1,0:T(8,128)} %bitcast.12), calls=%async_computation.2 | async-start | bytes 1572864 | tf_op jit(solution)/shard_map/all_to_all | solution.py:213
  149.7 3.3 %copy-start.3 = (f32[4,64,1536]{2,1,0:T(8,128)S(1)}, f32[4,64,1536]{2,1,0:T(8,128)}, u32[]{:S(2)}) copy-start(f32[4,64,1536]{2,1,0:T(8,128)} %copy-done.2) | copy-start | bytes 4718596
  162.3 15.2 %all-to-all-start.4 = ((f32[4,64,768]{2,1,0:T(8,128)}), f32[4,64,768]{2,1,0:T(8,128)S(1)}, u32[]{:S(2)}, u32[]{:S(2)}) async-start(f32[4,64,768]{2,1,0:T(8,128)} %bitcast.14), calls=%async_computation.4 | async-start | bytes 1572864 | tf_op jit(solution)/shard_map/all_to_all | solution.py:213
  165.8 15.0 %collective-permute-start.1 = (f32[16,768]{1,0:T(8,128)S(1)}, f32[16,768]{1,0:T(8,128)S(1)}, u32[]{:S(2)}, u32[]{:S(2)}) collective-permute-start(f32[16,768]{1,0:T(8,128)S(1)} %slice.39), channel_id=1, source_target_pairs={{0,16},{16,0},{1,17},{17,1},{2,18},{18,2},{3,19},{19,3},{4,20},{20... | collective-permute-start | bytes 147464 | tf_op jit(solution)/shard_map/ppermute | solution.py:25
  177.4 19.5 %all-to-all-start.3 = ((f32[4,16,768]{2,1,0:T(8,128)}), f32[4,16,768]{2,1,0:T(8,128)S(1)}, u32[]{:S(2)}, u32[]{:S(2)}) async-start(f32[4,16,768]{2,1,0:T(8,128)} %bitcast.13), calls=%async_computation.3 | async-start | bytes 393216 | tf_op jit(solution)/shard_map/all_to_all | solution.py:213
  180.9 11.3 %collective-permute-start.13 = (f32[16,768]{1,0:T(8,128)S(1)}, f32[16,768]{1,0:T(8,128)S(1)}, u32[]{:S(2)}, u32[]{:S(2)}) collective-permute-start(f32[16,768]{1,0:T(8,128)S(1)} %get-tuple-element.22), channel_id=1, source_target_pairs={{0,96},{32,0},{64,32},{96,64},{1,97},{33,1},{65,33},{97,65},{2,98}... | collective-permute-start | bytes 147464 | tf_op jit(solution)/shard_map/ppermute | solution.py:25
  186.6 6.9 %collective-permute-start.12 = (f32[16,768]{1,0:T(8,128)S(1)}, f32[16,768]{1,0:T(8,128)S(1)}, u32[]{:S(2)}, u32[]{:S(2)}) collective-permute-start(f32[16,768]{1,0:T(8,128)S(1)} %get-tuple-element.23), channel_id=1, source_target_pairs={{0,64},{32,96},{64,0},{96,32},{1,65},{33,97},{65,1},{97,33},{2,66}... | collective-permute-start | bytes 147464 | tf_op jit(solution)/shard_map/ppermute | solution.py:25
  188.6 7.8 %collective-permute-start.11 = (f32[16,768]{1,0:T(8,128)S(1)}, f32[16,768]{1,0:T(8,128)S(1)}, u32[]{:S(2)}, u32[]{:S(2)}) collective-permute-start(f32[16,768]{1,0:T(8,128)S(1)} %get-tuple-element.21), channel_id=1, source_target_pairs={{0,32},{32,64},{64,96},{96,0},{1,33},{33,65},{65,97},{97,1},{2,34}... | collective-permute-start | bytes 147464 | tf_op jit(solution)/shard_map/ppermute | solution.py:25

commit v5 on v4

v5 whole, which is shorter than its diff:
```python
import functools

import jax
import jax.numpy as jnp
from jax import lax
from jax.experimental import pallas as pl
from jax.experimental.pallas import tpu as pltpu
from jax.sharding import Mesh, PartitionSpec as P

FINE = ("x", "zl", "core", "y", "zh")
NODE = ("x", "zl", "core")
STATE = ("y", "zh")
VMEM = 56 * 1024 * 1024
F32 = jnp.float32
BF16 = jnp.bfloat16
HIGH = lax.Precision.HIGH


def node_shift(shard, by):
    length = lax.axis_size(NODE)
    pairs = [(i, i + by) for i in range(length) if 0 <= i + by < length]
    return lax.ppermute(shard, NODE, pairs)


def ring(shard, axis, by):
    length = lax.axis_size(axis)
    return lax.ppermute(shard, axis, [(i, (i + by) % length) for i in range(length)])


def halves(value):
    top = lax.reduce_precision(value, 8, 7)
    return top.astype(BF16), (value - top).astype(BF16)


def split(value):
    top = value.astype(BF16)
    return top, (value - top.astype(F32)).astype(BF16)


def dot(left, right, dims=((1,), (0,))):
    return lax.dot_general(left, right, (dims, ((), ())), preferred_element_type=F32)


def params():
    return pltpu.CompilerParams(vmem_limit_bytes=VMEM)


def cost(flops, moved):
    return pl.CostEstimate(flops=flops, bytes_accessed=moved, transcendentals=0)


ANY = pl.BlockSpec(memory_space=pl.ANY)


def rotate_kernel(
    coeffs_ref, states_ref, face_ref, out_ref, picked_ref, top_ref, low_ref
):
    step = pl.program_id(0)
    tile = states_ref.shape[0]

    @pl.when(step == 0)
    def _():
        top, low = split(coeffs_ref[...].T)
        top_ref[...] = top
        low_ref[...] = low
        picked_ref[...] = jnp.zeros_like(picked_ref)

    top, low = split(states_ref[...])
    dims = ((1,), (1,))
    out_ref[...] = (
        dot(top_ref[...], top, dims)
        + dot(low_ref[...], top, dims)
        + dot(top_ref[...], low, dims)
    )
    nodes = lax.broadcasted_iota(jnp.int32, (face_ref.shape[0], tile), 1) + step * tile
    table = (nodes == face_ref[...]).astype(F32).astype(BF16)
    picked_ref[...] += dot(table, top) + dot(table, low)


def rotate(coeffs, states, face_list):
    width, block = coeffs.shape
    owned = states.shape[0]
    face = face_list.shape[0]
    tile = 256
    fixed = lambda shape: pl.BlockSpec(shape, lambda i: (0, 0))
    return pl.pallas_call(
        rotate_kernel,
        grid=(owned // tile,),
        in_specs=[
            fixed((width, block)),
            pl.BlockSpec((tile, width), lambda i: (i, 0)),
            fixed((face, 1)),
        ],
        out_specs=[
            pl.BlockSpec((block, tile), lambda i: (0, i)),
            fixed((face, width)),
        ],
        out_shape=[
            jax.ShapeDtypeStruct((block, owned), F32),
            jax.ShapeDtypeStruct((face, width), F32),
        ],
        scratch_shapes=[pltpu.VMEM((block, width), BF16)] * 2,
        compiler_params=params(),
        cost_estimate=cost(6 * block * owned * width, 6000000),
        name="rotate",
    )(coeffs, states, face_list.reshape(-1, 1))


def cells_kernel(some, connect_ref, cell_ref, states_ref, ghost_ref, *refs):
    before_ref = refs[0] if len(refs) == 5 else None
    out_ref, pair_ref, link_ref, h_ref = refs[-4:]
    owned = states_ref.shape[0]
    total, width = out_ref.shape
    depth = pair_ref.shape[0] // 2
    cells, per_cell = connect_ref.shape
    side, count = h_ref.shape[1], h_ref.shape[0]
    many = count * side

    for place, ref in ((0, states_ref), (owned, ghost_ref)):
        top, low = split(ref[...])
        end = place + ref.shape[0]
        pair_ref[place:end] = top
        pair_ref[depth + place : depth + end] = low
    blank = jnp.zeros((depth - total, width), BF16)
    pair_ref[total:depth] = blank
    pair_ref[depth + total :] = blank
    link_ref[...] = jnp.full(link_ref.shape, -1.0, F32)
    link_ref[:cells, :per_cell] = connect_ref[...].astype(F32)
    h_ref[...] = jnp.zeros_like(h_ref)
    links = link_ref[...]
    columns = links.T
    along = lax.broadcasted_iota(jnp.int32, (side, depth), 1).astype(F32)
    down = lax.broadcasted_iota(jnp.int32, (total, side), 0).astype(F32)

    for first in range(some.start, some.stop, count):
        group = range(first, first + count)
        gather = jnp.concatenate(
            [(along == columns[:, c : c + 1]).astype(F32).astype(BF16) for c in group], axis=0
        )
        scatter = jnp.concatenate(
            [(down == links[c : c + 1]).astype(F32).astype(BF16) for c in group], axis=1
        )
        top, low = split(dot(jnp.concatenate([gather, gather], axis=1), pair_ref[...]))
        results = []
        for k, c in enumerate(group):
            h_ref[k, :per_cell, :per_cell] = cell_ref[c]
            cell = h_ref[k]
            cell_top, cell_low = split(0.5 * (cell + cell.T))
            rows = slice(k * side, (k + 1) * side)
            results.append(
                dot(
                    jnp.concatenate([cell_top, cell_low, cell_top], axis=1),
                    jnp.concatenate([top[rows], top[rows], low[rows]], axis=0),
                )
            )
        top, low = split(jnp.concatenate(results, axis=0))
        value = dot(
            jnp.concatenate([scatter, scatter], axis=1), jnp.concatenate([top, low], axis=0)
        )
        if first > some.start:
            out_ref[...] += value
        elif before_ref is not None:
            out_ref[...] = before_ref[...] + value
        else:
            out_ref[...] = value


def cells_apply(some, states, ghosts, cell_matrix, connect, *before):
    owned, width = states.shape
    total = owned + ghosts.shape[0]
    depth = -(-total // 128) * 128
    side, count = 128, 3
    arrays = (connect, cell_matrix, states, ghosts) + before
    return pl.pallas_call(
        functools.partial(cells_kernel, some),
        out_shape=jax.ShapeDtypeStruct((total, width), F32),
        in_specs=[pl.BlockSpec(memory_space=pltpu.VMEM)] * len(arrays),
        out_specs=pl.BlockSpec(memory_space=pltpu.VMEM),
        scratch_shapes=[
            pltpu.VMEM((2 * depth, width), BF16),
            pltpu.VMEM((16, side), F32),
            pltpu.VMEM((count, side, side), F32),
        ],
        compiler_params=params(),
        cost_estimate=cost(8 * len(some) * side * total * width, 9000000),
        name="cells",
    )(*arrays)


def face_pick(table, value, dims):
    top, low = halves(value)
    return dot(table, top, dims) + dot(table, low, dims)


def tie_kernel(*refs):
    pass


def tie(*arrays):
    return pl.pallas_call(
        tie_kernel,
        in_specs=[ANY] * len(arrays),
        out_specs=[ANY] * len(arrays),
        out_shape=[jax.ShapeDtypeStruct(a.shape, a.dtype) for a in arrays],
        input_output_aliases={i: i for i in range(len(arrays))},
        name="tie",
    )(*arrays)


def swap(pieces, axis):
    return lax.all_to_all(pieces, axis, 0, 0, tiled=True)


def gather_rows(rows, axis):
    length = lax.axis_size(axis)
    here = lax.axis_index(axis)
    out = jnp.zeros((2, length) + rows.shape[1:], rows.dtype)
    out = lax.dynamic_update_slice_in_dim(out, rows[:, None], here, 1)
    for by in (1, length - 1, 2):
        out = lax.dynamic_update_slice_in_dim(
            out, ring(rows, axis, by)[:, None], (here - by) % length, 1
        )
    return out


def local(states, coeffs, cell_matrix, connect, face_list, node_mass):
    owned, width = states.shape
    block = coeffs.shape[1]
    cells = connect.shape[0]
    first = lax.axis_index("core") == 0

    partial, picked = rotate(coeffs, states, face_list)
    pieces = swap(partial.reshape(4, block // 4, owned), "y")

    ghosts = node_shift(picked, -1)
    some, rest = range(cells // 2), range(cells // 2, cells)
    assembled = cells_apply(some, states, ghosts, cell_matrix, connect)

    over_y, assembled = tie(jnp.sum(pieces, axis=0), assembled)
    rotated = jnp.sum(swap(over_y.reshape(4, block // 16, owned), "zh"), axis=0)

    assembled = cells_apply(rest, states, ghosts, cell_matrix, connect, assembled)
    returned = node_shift(assembled[owned:], 1)
    table = (face_list[:, None] == jnp.arange(owned)[None, :]).astype(BF16)
    applied = assembled[:owned] + face_pick(table, returned, ((0,), (0,)))
    weights = jnp.concatenate([applied, states * node_mass[:, None]], axis=1)

    pair = rotated.reshape(2, block // 32, owned)
    pair = jnp.concatenate(
        [jnp.where(first, pair[1], pair[0]), jnp.where(first, pair[0], pair[1])], axis=0
    )
    group = lax.all_gather(pair, "zh", axis=0, tiled=True)
    group = group.reshape(4, 2, block // 32, owned).swapaxes(0, 1)
    rows = gather_rows(group.reshape(2, block // 8, owned), "y")
    rows = rows.reshape(2, block // 2, owned)
    theirs, ours = (
        jnp.dot(rows[k], weights, precision=HIGH, preferred_element_type=F32) for k in range(2)
    )
    panel = ours + ring(theirs, "core", 1)
    panel = jnp.sum(swap(panel.reshape(4, block // 8, 2 * width), "x"), axis=0)
    panel = swap(panel.reshape(4, block // 32, 2 * width), "zl")
    return rotated, jnp.sum(panel[:, :, :width], axis=0), jnp.sum(panel[:, :, width:], axis=0)


def solution(mesh):
    fine = Mesh(mesh.devices.reshape(4, 4, 2, 4, 4), FINE)
    return jax.shard_map(
        local,
        mesh=fine,
        in_specs=(
            P(NODE, STATE),
            P(STATE, None),
            P(NODE, None, None),
            P(NODE, None),
            P(NODE),
            P(NODE),
        ),
        out_specs=(P(STATE, NODE), P(NODE, STATE), P(NODE, STATE)),
        check_vma=False,
    )
```

time: 201 us -> 172 us (0.86); the launches traced: 198 us -> 171 us
  starting transfers between devices: 78.8 us -> 38.4 us
  blocking collectives: 34.9 us -> 67.8 us
  waiting for transfers between devices: 35.4 us -> 23 us
  Pallas kernels: 20.7 us -> 26.6 us
  matrix products: 15.5 us -> 9.6 us
  other arithmetic: 6.69 us -> 1.88 us
    all_to_all x0 -> x2, blocking collectives: none -> 40.5 us  [swap(): return lax.all_to_all(pieces, axis, 0, 0, tiled=True)]
    ppermute x12 -> x4, starting transfers between devices: 40.2 us -> 11.3 us  [ring(): lax.ppermute(shard, axis, [(i, (i + by) % length) for i in range(length)])]
    all_to_all x5 -> x2, waiting for transfers between devices: 14.5 us -> 3.32 us  [swap(): return lax.all_to_all(pieces, axis, 0, 0, tiled=True)]
    all_gather x1, blocking collectives: 34.9 us -> 27.3 us  [local(): group = lax.all_gather(pair, 'zh', axis=0, tiled=True)]
    all_to_all x5 -> x2, starting transfers between devices: 31.5 us -> 24.4 us  [swap(): return lax.all_to_all(pieces, axis, 0, 0, tiled=True)]
    dot_general x4 -> x2, matrix products: 11.8 us -> 4.63 us  [local(): jnp.dot(rows[k], weights, precision=HIGH, preferred_element_type=F32)]
    pallas_call x1 -> x2, Pallas kernels: 14.7 us -> 20.3 us  [cells_apply(): pl.pallas_call(functools.partial(cells_kernel, some), out_shape=jax.Shape...]
    ppermute x2, starting transfers between devices: 7.06 us -> 2.76 us  [node_shift(): return lax.ppermute(shard, NODE, pairs)]
  transfers between devices with their start and end apart: 19 -> 8, of which waited for: 8 -> 7; matrix products, arithmetic and copies ran while one was open for 11% -> 4% of each run, Pallas kernels for 7% -> 12%
where the time goes in v5:
time: 172 us; the launch traced here: 171 us
  blocking collectives  67.8 us (39%)
  starting transfers between devices  38.4 us (22%)
  Pallas kernels  26.6 us (15%)
  waiting for transfers between devices  23 us (13%)
  matrix products  9.6 us (6%)
  local copies, waits for them, and re-layouts  3.39 us (2%)
  other arithmetic  1.88 us (1%)
    all_to_all x2, blocking collectives, swap(): return lax.all_to_all(pieces, axis, 0, 0, tiled=True)  40.5 us
    all_gather x1, blocking collectives, local(): group = lax.all_gather(pair, 'zh', axis=0, tiled=True)  27.3 us
    all_to_all x2, starting transfers between devices, swap(): return lax.all_to_all(pieces, axis, 0, 0, tiled=True)  24.4 us
    pallas_call x2, Pallas kernels, cells_apply(): pl.pallas_call(functools.partial(cells_kernel, some), out_shape=jax.Shape...  20.3 us
    ppermute x4, waiting for transfers between devices, ring(): lax.ppermute(shard, axis, [(i, (i + by) % length) for i in range(length)])  17 us
    ppermute x4, starting transfers between devices, ring(): lax.ppermute(shard, axis, [(i, (i + by) % length) for i in range(length)])  11.3 us
    pallas_call x1, Pallas kernels, rotate(): pl.pallas_call(rotate_kernel, grid=(owned // tile,), in_specs=[fixed((wid...  6.25 us
    dot_general x2, matrix products, dot(): lax.dot_general(left, right, (dims, ((), ())), preferred_element_type=F32)  4.97 us
  transfers between devices with their start and end apart: 8, of which 7 were waited for; matrix products, arithmetic and copies ran while one was open for 4% of the time, Pallas kernels for 12%

profile of v5, /device:TPU:24, one launch (start us, length us, event | category | flops | bytes accessed | tf_op | source)
XLA Modules:
  0.0 171.5 jit_solution(9983647341880374680)
XLA Ops:
  0.6 1.4 copy.24.face_ref
  2.0 6.2 %rotate.1 = (f32[512,768]{1,0:T(8,128)}, f32[64,768]{1,0:T(8,128)}) custom-call(f32[768,512]{1,0:T(8,128)} %coeffs_ref.1, f32[768,768]{1,0:T(8,128)} %states_ref.5, s32[64,1]{1,0:T(8,128)} %copy.24.face_ref), custom_call_target="tpu_custom_call" | custom-call | flops 1811939328 | bytes 6000000 | tf_op jit(solution)/shard_map/rotate/pallas_call | solution.py:86
  8.2 9.3 %all-to-all-start = ((f32[4,128,768]{2,1,0:T(8,128)}), f32[4,128,768]{2,1,0:T(8,128)S(1)}, u32[]{:S(2)}, u32[]{:S(2)}) async-start(f32[4,128,768]{2,1,0:T(8,128)} %bitcast.24), calls=%async_computation | async-start | bytes 3145728 | tf_op jit(solution)/shard_map/all_to_all | solution.py:211
  17.5 1.3 collective-permute-start
  18.8 2.0 %collective-permute-done.ghost_ref = f32[64,768]{1,0:T(8,128)S(1)} collective-permute-done((f32[64,768]{1,0:T(8,128)S(1)}, f32[64,768]{1,0:T(8,128)S(1)}, u32[]{:S(2)}, u32[]{:S(2)}) %collective-permute-start) | collective-permute-done | bytes 196640 | tf_op jit(solution)/shard_map/ppermute | solution.py:22
  20.8 0.7 copy-done.4
  21.5 9.7 %cells.2.refs_1_ = f32[832,768]{1,0:T(8,128)} custom-call(s32[12,125]{1,0:T(8,128)} %connect_ref.3, f32[12,125,125]{2,1,0:T(8,128)} %cell_ref.3, f32[768,768]{1,0:T(8,128)} %states_ref.5, f32[64,768]{1,0:T(8,128)} %copy-done.4), custom_call_target="tpu_custom_call" | custom-call | flops 3925868544 | bytes 9000000 | tf_op jit(solution)/shard_map/cells/pallas_call | solution.py:174
  31.2 0.5 all-to-all-done
  31.7 0.9 reduce_sum.45.refs_0_
  32.6 15.1 %all-to-all-start.1 = ((f32[4,32,768]{2,1,0:T(8,128)}), f32[4,32,768]{2,1,0:T(8,128)S(1)}, u32[]{:S(2)}, u32[]{:S(2)}) async-start(f32[4,32,768]{2,1,0:T(8,128)} %bitcast.21), calls=%async_computation.1 | async-start | bytes 786432 | tf_op jit(solution)/shard_map/all_to_all | solution.py:211
  47.6 10.6 %cells.3 = f32[832,768]{1,0:T(8,128)} custom-call(s32[12,125]{1,0:T(8,128)} %connect_ref.3, f32[12,125,125]{2,1,0:T(8,128)} %cell_ref.3, f32[768,768]{1,0:T(8,128)} %states_ref.5, f32[64,768]{1,0:T(8,128)} %copy-done.4, f32[832,768]{1,0:T(8,128)} %get-tuple-element.10.refs_0_), custom_call_target="tpu_custom_call" | custom-call | flops 3925868544 | bytes 9000000 | tf_op jit(solution)/shard_map/cells/pallas_call | solution.py:174
  58.3 0.9 slice.42
  59.3 1.5 collective-permute-start.4
  60.8 0.2 broadcast_multiply_fusion
  61.0 0.6 collective-permute-done.4
  61.6 2.0 %fusion.4 = f32[768,768]{1,0:T(8,128)} fusion(f32[64,768]{1,0:T(8,128)S(1)} %collective-permute-done.4, s32[64]{0:T(128)S(1)} %copy-done.2), kind=kOutput, calls=%fused_computation.15 | convolution fusion | flops 75694080 | bytes 2556160 | tf_op jit(solution)/shard_map/dot_general | solution.py:41
  63.6 2.8 %all-to-all-done.1 = f32[4,32,768]{2,1,0:T(8,128)S(1)} async-done(((f32[4,32,768]{2,1,0:T(8,128)}), f32[4,32,768]{2,1,0:T(8,128)S(1)}, u32[]{:S(2)}, u32[]{:S(2)}) %all-to-all-start.1) | async-done | bytes 393248 | tf_op jit(solution)/shard_map/all_to_all | solution.py:211
  66.5 27.3 %all_gather.3 = f32[128,768]{1,0:T(8,128)S(1)} all-gather(f32[32,768]{1,0:T(8,128)S(1)} %pad_maximum_fusion.5), channel_id=1, replica_groups=mesh['x'=4,'zl'=4,'core'=2,'y'=4,'zh'=4] {'zh'}, dimensions={0}, use_global_device_ids=true | all-gather | bytes 491520 | tf_op jit(solution)/shard_map/all_gather | solution.py:252
  93.8 3.9 %collective-permute-start.1 = (f32[2,64,768]{2,1,0:T(8,128)S(1)}, f32[2,64,768]{2,1,0:T(8,128)S(1)}, u32[]{:S(2)}, u32[]{:S(2)}) collective-permute-start(f32[2,64,768]{2,1,0:T(8,128)S(1)} %bitcast.25), channel_id=1, source_target_pairs={{0,4},{4,8},{8,12},{12,0},{1,5},{5,9},{9,13},{13,1},{2,6},{6,10},{... | collective-permute-start | bytes 1179656 | tf_op jit(solution)/shard_map/ppermute | solution.py:27
  97.7 2.0 %collective-permute-start.2 = (f32[2,64,768]{2,1,0:T(8,128)S(1)}, f32[2,64,768]{2,1,0:T(8,128)S(1)}, u32[]{:S(2)}, u32[]{:S(2)}) collective-permute-start(f32[2,64,768]{2,1,0:T(8,128)S(1)} %bitcast.26), channel_id=1, source_target_pairs={{0,12},{4,0},{8,4},{12,8},{1,13},{5,1},{9,5},{13,9},{2,14},{6,2},{... | collective-permute-start | bytes 1179656 | tf_op jit(solution)/shard_map/ppermute | solution.py:27
  99.7 3.0 %slice_add_fusion = f32[768,768]{1,0:T(8,128)S(1)} fusion(f32[832,768]{1,0:T(8,128)} %cells.3, f32[768,768]{1,0:T(8,128)} %fusion.4, f32[64,768]{1,0:T(8,128)S(1)} %collective-permute-done.4, s32[64]{0:T(128)S(1)} %copy-done.2), kind=kOutput, calls=%fused_computation.4 | convolution fusion | flops 76824576 | bytes 7274752 | tf_op jit(solution)/shard_map/dot_general | solution.py:41
  102.6 3.5 %collective-permute-start.3 = (f32[2,64,768]{2,1,0:T(8,128)S(1)}, f32[2,64,768]{2,1,0:T(8,128)S(1)}, u32[]{:S(2)}, u32[]{:S(2)}) collective-permute-start(f32[2,64,768]{2,1,0:T(8,128)S(1)} %bitcast.27), channel_id=1, source_target_pairs={{0,8},{4,12},{8,0},{12,4},{1,9},{5,13},{9,1},{13,5},{2,10},{6,14},... | collective-permute-start | bytes 1179656 | tf_op jit(solution)/shard_map/ppermute | solution.py:27
  106.2 0.1 broadcast_in_dim.15
  106.4 1.2 collective-permute-done.1
  107.6 12.5 %collective-permute-done.2 = f32[2,64,768]{2,1,0:T(8,128)S(1)} collective-permute-done((f32[2,64,768]{2,1,0:T(8,128)S(1)}, f32[2,64,768]{2,1,0:T(8,128)S(1)}, u32[]{:S(2)}, u32[]{:S(2)}) %collective-permute-start.2) | collective-permute-done | bytes 393248 | tf_op jit(solution)/shard_map/ppermute | solution.py:27
  120.3 2.3 %fusion = f32[256,1536]{1,0:T(8,128)S(1)} fusion(f32[256,768]{1,0:T(8,128)S(1)} %bitcast.23, f32[768,768]{1,0:T(8,128)S(1)} %broadcast_multiply_fusion, f32[768,768]{1,0:T(8,128)S(1)} %slice_add_fusion), kind=kOutput, calls=%fused_computation.1 | convolution fusion | flops 1813118976 | bytes 7077888 | tf_op jit(solution)/shard_map/dot_general | solution.py:257
  122.6 1.9 %collective-permute-start.5 = (f32[256,1536]{1,0:T(8,128)S(1)}, f32[256,1536]{1,0:T(8,128)S(1)}, u32[]{:S(2)}, u32[]{:S(2)}) collective-permute-start(f32[256,1536]{1,0:T(8,128)S(1)} %fusion), channel_id=1, source_target_pairs={{0,16},{16,0},{1,17},{17,1},{2,18},{18,2},{3,19},{19,3},{4,20},{20... | collective-permute-start | bytes 4718600 | tf_op jit(solution)/shard_map/ppermute | solution.py:27
  124.5 3.4 %collective-permute-done.5 = f32[256,1536]{1,0:T(8,128)S(1)} collective-permute-done((f32[256,1536]{1,0:T(8,128)S(1)}, f32[256,1536]{1,0:T(8,128)S(1)}, u32[]{:S(2)}, u32[]{:S(2)}) %collective-permute-start.5) | collective-permute-done | bytes 1572896 | tf_op jit(solution)/shard_map/ppermute | solution.py:27
  127.9 2.3 %fusion.2 = f32[256,1536]{1,0:T(8,128)S(1)} fusion(f32[256,1536]{1,0:T(8,128)S(1)} %collective-permute-done.5, f32[256,768]{1,0:T(8,128)S(1)} %bitcast.22, f32[768,768]{1,0:T(8,128)S(1)} %broadcast_multiply_fusion, f32[768,768]{1,0:T(8,128)S(1)} %slice_add_fusion), kind=kOutput, calls=%fused_computation.3 | convolution fusion | flops 1813512192 | bytes 8650752 | tf_op jit(solution)/shard_map/dot_general | solution.py:257
  130.2 26.3 %all_to_all.20 = f32[4,64,1536]{2,1,0:T(8,128)S(1)} all-to-all(f32[4,64,1536]{2,1,0:T(8,128)S(1)} %bitcast.20), channel_id=1, replica_groups=mesh['x'=4,'zl'=4,'core'=2,'y'=4,'zh'=4] {'x'}, dimensions={0} | all-to-all | bytes 3145728 | tf_op jit(solution)/shard_map/all_to_all | solution.py:211
  156.6 14.2 %all_to_all.21 = f32[4,16,1536]{2,1,0:T(8,128)S(1)} all-to-all(f32[4,16,1536]{2,1,0:T(8,128)S(1)} %bitcast.29), channel_id=1, replica_groups=mesh['x'=4,'zl'=4,'core'=2,'y'=4,'zh'=4] {'zl'}, dimensions={0} | all-to-all | bytes 786432 | tf_op jit(solution)/shard_map/all_to_all | solution.py:211
  170.8 0.7 slice_reduce_fusion
  (23 shorter events, 0.4 us)
Async XLA Ops:
  8.2 9.3 %copy-start.5 = (f32[64,768]{1,0:T(8,128)S(1)}, f32[64,768]{1,0:T(8,128)}, u32[]{:S(2)}) copy-start(f32[64,768]{1,0:T(8,128)} %get-tuple-element.8) | copy-start | bytes 589828
  8.2 23.5 %all-to-all-start = ((f32[4,128,768]{2,1,0:T(8,128)}), f32[4,128,768]{2,1,0:T(8,128)S(1)}, u32[]{:S(2)}, u32[]{:S(2)}) async-start(f32[4,128,768]{2,1,0:T(8,128)} %bitcast.24), calls=%async_computation | async-start | bytes 3145728 | tf_op jit(solution)/shard_map/all_to_all | solution.py:211
  17.5 3.3 %collective-permute-start = (f32[64,768]{1,0:T(8,128)S(1)}, f32[64,768]{1,0:T(8,128)S(1)}, u32[]{:S(2)}, u32[]{:S(2)}) collective-permute-start(f32[64,768]{1,0:T(8,128)S(1)} %copy-done.5), channel_id=1, source_target_pairs={{16,0},{32,16},{48,32},{64,48},{80,64},{96,80},{112,96},{128,112},... | collective-permute-start | bytes 589832 | tf_op jit(solution)/shard_map/ppermute | solution.py:22
  20.8 0.7 copy-start.4
  32.6 33.9 %all-to-all-start.1 = ((f32[4,32,768]{2,1,0:T(8,128)}), f32[4,32,768]{2,1,0:T(8,128)S(1)}, u32[]{:S(2)}, u32[]{:S(2)}) async-start(f32[4,32,768]{2,1,0:T(8,128)} %bitcast.21), calls=%async_computation.1 | async-start | bytes 786432 | tf_op jit(solution)/shard_map/all_to_all | solution.py:211
  47.6 13.1 %copy-start = (f32[768,768]{1,0:T(8,128)S(1)}, f32[768,768]{1,0:T(8,128)}, u32[]{:S(2)}) copy-start(f32[768,768]{1,0:T(8,128)} %states_ref.5) | copy-start | bytes 7077892
  47.6 13.1 %copy-start.3 = (f32[768]{0:T(1024)S(1)}, f32[768]{0:T(1024)}, u32[]{:S(2)}) copy-start(f32[768]{0:T(1024)} %param.11) | copy-start | bytes 9220
  59.2 2.4 %copy-start.2 = (s32[64]{0:T(128)S(1)}, s32[64]{0:T(128)}, u32[]{:S(2)}) copy-start(s32[64]{0:T(128)} %param.10) | copy-start | bytes 772
  59.3 2.4 %collective-permute-start.4 = (f32[64,768]{1,0:T(8,128)S(1)}, f32[64,768]{1,0:T(8,128)S(1)}, u32[]{:S(2)}, u32[]{:S(2)}) collective-permute-start(f32[64,768]{1,0:T(8,128)S(1)} %slice.42), channel_id=1, source_target_pairs={{0,16},{16,32},{32,48},{48,64},{64,80},{80,96},{96,112},{112,128},... | collective-permute-start | bytes 589832 | tf_op jit(solution)/shard_map/ppermute | solution.py:22
  66.4 36.2 %copy-start.1 = (f32[32,768]{1,0:T(8,128)}, f32[32,768]{1,0:T(8,128)S(1)}, u32[]{:S(2)}) copy-start(f32[32,768]{1,0:T(8,128)S(1)} %reduce_sum.46) | copy-start | bytes 294916
  93.8 13.7 %collective-permute-start.1 = (f32[2,64,768]{2,1,0:T(8,128)S(1)}, f32[2,64,768]{2,1,0:T(8,128)S(1)}, u32[]{:S(2)}, u32[]{:S(2)}) collective-permute-start(f32[2,64,768]{2,1,0:T(8,128)S(1)} %bitcast.25), channel_id=1, source_target_pairs={{0,4},{4,8},{8,12},{12,0},{1,5},{5,9},{9,13},{13,1},{2,6},{6,10},{... | collective-permute-start | bytes 1179656 | tf_op jit(solution)/shard_map/ppermute | solution.py:27
  97.7 22.4 %collective-permute-start.2 = (f32[2,64,768]{2,1,0:T(8,128)S(1)}, f32[2,64,768]{2,1,0:T(8,128)S(1)}, u32[]{:S(2)}, u32[]{:S(2)}) collective-permute-start(f32[2,64,768]{2,1,0:T(8,128)S(1)} %bitcast.26), channel_id=1, source_target_pairs={{0,12},{4,0},{8,4},{12,8},{1,13},{5,1},{9,5},{13,9},{2,14},{6,2},{... | collective-permute-start | bytes 1179656 | tf_op jit(solution)/shard_map/ppermute | solution.py:27
  102.6 17.4 %collective-permute-start.3 = (f32[2,64,768]{2,1,0:T(8,128)S(1)}, f32[2,64,768]{2,1,0:T(8,128)S(1)}, u32[]{:S(2)}, u32[]{:S(2)}) collective-permute-start(f32[2,64,768]{2,1,0:T(8,128)S(1)} %bitcast.27), channel_id=1, source_target_pairs={{0,8},{4,12},{8,0},{12,4},{1,9},{5,13},{9,1},{13,5},{2,10},{6,14},... | collective-permute-start | bytes 1179656 | tf_op jit(solution)/shard_map/ppermute | solution.py:27
  122.6 5.3 %collective-permute-start.5 = (f32[256,1536]{1,0:T(8,128)S(1)}, f32[256,1536]{1,0:T(8,128)S(1)}, u32[]{:S(2)}, u32[]{:S(2)}) collective-permute-start(f32[256,1536]{1,0:T(8,128)S(1)} %fusion), channel_id=1, source_target_pairs={{0,16},{16,0},{1,17},{17,1},{2,18},{18,2},{3,19},{19,3},{4,20},{20... | collective-permute-start | bytes 4718600 | tf_op jit(solution)/shard_map/ppermute | solution.py:27

commit v6 on v4

v6 whole, which is shorter than its diff:
```python
import jax
import jax.numpy as jnp
from jax import lax
from jax.experimental import pallas as pl
from jax.experimental.pallas import tpu as pltpu
from jax.sharding import Mesh, PartitionSpec as P

FINE = ("x", "zl", "core", "y", "zh")
NODE = ("x", "zl", "core")
STATE = ("y", "zh")
VMEM = 56 * 1024 * 1024
F32 = jnp.float32
BF16 = jnp.bfloat16
HIGH = lax.Precision.HIGH


def node_shift(shard, by):
    length = lax.axis_size(NODE)
    pairs = [(i, i + by) for i in range(length) if 0 <= i + by < length]
    return lax.ppermute(shard, NODE, pairs)


def ring(shard, axis, by):
    length = lax.axis_size(axis)
    return lax.ppermute(shard, axis, [(i, (i + by) % length) for i in range(length)])


def split(value):
    top = value.astype(BF16)
    return top, (value - top.astype(F32)).astype(BF16)


def dot(left, right, dims=((1,), (0,))):
    return lax.dot_general(left, right, (dims, ((), ())), preferred_element_type=F32)


def params():
    return pltpu.CompilerParams(vmem_limit_bytes=VMEM)


def cost(flops, moved):
    return pl.CostEstimate(flops=flops, bytes_accessed=moved, transcendentals=0)


ANY = pl.BlockSpec(memory_space=pl.ANY)


def face_table(face_ref, start, rows):
    nodes = lax.broadcasted_iota(jnp.int32, (rows, face_ref.shape[1]), 0) + start
    return (nodes == face_ref[...]).astype(F32).astype(BF16)


def rotate_kernel(coeffs_ref, states_ref, face_ref, out_ref, picked_ref, top_ref, low_ref):
    step = pl.program_id(0)
    tile = states_ref.shape[0]

    @pl.when(step == 0)
    def _():
        top, low = split(coeffs_ref[...].T)
        for y in range(4):
            for zh in range(4):
                for core in range(2):
                    source = ((y * 4 + zh) * 2 + core) * 16
                    place = ((y * 2 + core) * 4 + zh) * 16
                    top_ref[place : place + 16] = top[source : source + 16]
                    low_ref[place : place + 16] = low[source : source + 16]
        picked_ref[...] = jnp.zeros_like(picked_ref)

    top, low = split(states_ref[...])
    dims = ((1,), (1,))
    out_ref[...] = (
        dot(top_ref[...], top, dims)
        + dot(low_ref[...], top, dims)
        + dot(top_ref[...], low, dims)
    )
    table = face_table(face_ref, step * tile, tile)
    dims = ((0,), (0,))
    picked_ref[...] += dot(table, top, dims) + dot(table, low, dims)


def rotate(coeffs, states, faces):
    width, block = coeffs.shape
    owned = states.shape[0]
    face = faces.shape[1]
    tile = 256
    fixed = lambda shape: pl.BlockSpec(shape, lambda i: (0, 0))
    return pl.pallas_call(
        rotate_kernel,
        grid=(owned // tile,),
        in_specs=[
            fixed((width, block)),
            pl.BlockSpec((tile, width), lambda i: (i, 0)),
            fixed((1, face)),
        ],
        out_specs=[
            pl.BlockSpec((block, tile), lambda i: (0, i)),
            fixed((face, width)),
        ],
        out_shape=[
            jax.ShapeDtypeStruct((block, owned), F32),
            jax.ShapeDtypeStruct((face, width), F32),
        ],
        scratch_shapes=[pltpu.VMEM((block, width), BF16)] * 2,
        compiler_params=params(),
        cost_estimate=cost(6 * block * owned * width, 6000000),
        name="rotate",
    )(coeffs, states, faces)


def assemble_kernel(connect_ref, cell_ref, _, top_ref, low_ref, sum_ref, link_ref, h_ref):
    total, depth = top_ref.shape
    cells, per_cell = connect_ref.shape
    count, side = h_ref.shape[0], h_ref.shape[1]

    link_ref[...] = jnp.full(link_ref.shape, -1.0, F32)
    link_ref[:cells, :per_cell] = connect_ref[...].astype(F32)
    h_ref[...] = jnp.zeros_like(h_ref)
    links = link_ref[...]
    columns = links.T
    along = lax.broadcasted_iota(jnp.int32, (side, depth), 1).astype(F32)
    down = lax.broadcasted_iota(jnp.int32, (total, side), 0).astype(F32)

    for first in range(0, cells, count):
        scatter, tops, lows = [], [], []
        for k in range(count):
            c = first + k
            gather = (along == columns[:, c : c + 1]).astype(F32).astype(BF16)
            scatter.append((down == links[c : c + 1]).astype(F32).astype(BF16))
            h_ref[k, :per_cell, :per_cell] = cell_ref[c]
            cell = h_ref[k]
            top, low = split(0.5 * (cell + cell.T))
            top, low = split(dot(top, gather) + dot(low, gather))
            tops.append(top)
            lows.append(low)
        value = dot(
            jnp.concatenate(scatter + scatter, axis=1), jnp.concatenate(tops + lows, axis=0)
        )
        if first + count < cells:
            sum_ref[...] = value if first == 0 else sum_ref[...] + value
        else:
            top_ref[...], low_ref[...] = split(sum_ref[...] + value)


def assemble(connect, cell_matrix, total, after):
    depth = -(-total // 128) * 128
    cells = connect.shape[0]
    side, count = 128, 4
    whole = pl.BlockSpec(memory_space=pltpu.VMEM)
    return pl.pallas_call(
        assemble_kernel,
        out_shape=[jax.ShapeDtypeStruct((total, depth), BF16)] * 2,
        in_specs=[whole, whole, ANY],
        out_specs=[whole] * 2,
        scratch_shapes=[
            pltpu.VMEM((total, depth), F32),
            pltpu.VMEM((16, side), F32),
            pltpu.VMEM((count, side, side), F32),
        ],
        compiler_params=params(),
        cost_estimate=cost(8000000000, 4000000),
        name="assemble",
    )(connect, cell_matrix, after)


def extend(states_ref, ghost_ref, depth):
    states, ghosts = states_ref[...], ghost_ref[...]
    rest = depth - states.shape[0] - ghosts.shape[0]
    blank = jnp.zeros((rest, states.shape[1]), BF16)
    pair = split(states), split(ghosts)
    return [jnp.concatenate([pair[0][k], pair[1][k], blank], axis=0) for k in range(2)]


def product(top_ref, low_ref, top, low):
    return dot(top_ref[...], top) + dot(low_ref[...], top) + dot(top_ref[...], low)


def back_kernel(top_ref, low_ref, states_ref, ghost_ref, out_ref):
    out_ref[...] = product(top_ref, low_ref, *extend(states_ref, ghost_ref, top_ref.shape[1]))


def apply_back(matrix, states, ghosts):
    owned, width = states.shape
    face, depth = ghosts.shape[0], matrix[0].shape[1]
    fixed = lambda shape: pl.BlockSpec(shape, lambda i: (0, 0))
    rows = pl.BlockSpec((face, depth), lambda i: (owned // face, 0))
    return pl.pallas_call(
        back_kernel,
        grid=(1,),
        in_specs=[rows, rows, fixed(states.shape), fixed(ghosts.shape)],
        out_specs=fixed(ghosts.shape),
        out_shape=jax.ShapeDtypeStruct(ghosts.shape, F32),
        compiler_params=params(),
        cost_estimate=cost(600000000, 4000000),
        name="back",
    )(*matrix, states, ghosts)


def apply_kernel(
    top_ref, low_ref, states_ref, ghost_ref, mass_ref, back_ref, face_ref, out_ref, scaled_ref
):
    owned = states_ref.shape[0]
    value = product(top_ref, low_ref, *extend(states_ref, ghost_ref, top_ref.shape[1]))
    table = face_table(face_ref, 0, owned)
    top, low = split(back_ref[...])
    out_ref[...] = value + dot(table, top) + dot(table, low)
    side = mass_ref.shape[1]
    for k in range(owned // side):
        column = jnp.broadcast_to(mass_ref[k : k + 1, :], (8, side)).T[:, :1]
        rows = slice(k * side, (k + 1) * side)
        scaled_ref[rows] = states_ref[rows] * column


def apply_cells(matrix, states, ghosts, returned, faces, mass):
    owned, width = states.shape
    depth = matrix[0].shape[1]
    tile, side = 256, 128
    fixed = lambda shape: pl.BlockSpec(shape, lambda i: (0, 0))
    tall = pl.BlockSpec((owned, tile), lambda i: (0, i))
    low = pl.BlockSpec((ghosts.shape[0], tile), lambda i: (0, i))
    return pl.pallas_call(
        apply_kernel,
        grid=(width // tile,),
        in_specs=[fixed((owned, depth))] * 2
        + [tall, low, fixed((owned // side, side)), low, fixed(faces.shape)],
        out_specs=[tall] * 2,
        out_shape=[jax.ShapeDtypeStruct((owned, width), F32)] * 2,
        compiler_params=params(),
        cost_estimate=cost(7000000000, 11000000),
        name="apply",
    )(*matrix, states, ghosts, mass.reshape(-1, side), returned, faces)


def tie_kernel(*refs):
    pass


def tie(*arrays):
    return pl.pallas_call(
        tie_kernel,
        in_specs=[ANY] * len(arrays),
        out_specs=[ANY] * len(arrays),
        out_shape=[jax.ShapeDtypeStruct(a.shape, a.dtype) for a in arrays],
        input_output_aliases={i: i for i in range(len(arrays))},
        name="tie",
    )(*arrays)


def swap(pieces, axis):
    return lax.all_to_all(pieces, axis, 0, 0, tiled=True)


def gather_rows(rows, axis):
    length = lax.axis_size(axis)
    here = lax.axis_index(axis)
    out = jnp.zeros((length,) + rows.shape, rows.dtype)
    out = lax.dynamic_update_slice_in_dim(out, rows[None], here, 0)
    for by in (1, length - 1, 2):
        out = lax.dynamic_update_slice_in_dim(
            out, ring(rows, axis, by)[None], (here - by) % length, 0
        )
    return out.reshape((-1,) + rows.shape[1:])


def local(states, coeffs, cell_matrix, connect, face_list, node_mass):
    owned, width = states.shape
    block = coeffs.shape[1]
    first = lax.axis_index("core") == 0
    faces = face_list.reshape(1, -1)

    partial, picked = rotate(coeffs, states, faces)
    pieces = swap(partial.reshape(8, block // 8, owned), ("y", "core"))
    ghosts = node_shift(picked, -1)
    matrix = assemble(connect, cell_matrix, owned + faces.shape[1], partial)
    returned = node_shift(apply_back(matrix, states, ghosts), 1)

    over_y = jnp.sum(pieces.reshape(4, 2, block // 8, owned), axis=0)
    over_y = jnp.concatenate(
        [jnp.where(first, over_y[0], over_y[1]), jnp.where(first, over_y[1], over_y[0])], axis=1
    )
    over_y, returned, *matrix = tie(over_y, returned, *matrix)
    both = jnp.sum(swap(over_y.reshape(4, block // 32, 2 * owned), "zh"), axis=0)

    mine = apply_cells(matrix, states, ghosts, returned, faces, node_mass)
    other = [ring(weight, "core", 1) for weight in mine]

    own, theirs = both[:, :owned], ring(both[:, owned:], "core", 1)
    rotated = jnp.concatenate(
        [jnp.where(first, own, theirs), jnp.where(first, theirs, own)], axis=0
    )

    rows = gather_rows(lax.all_gather(both, "zh", axis=0, tiled=True), "y")
    panel = jnp.concatenate(
        [
            sum(
                jnp.dot(part, weight, precision=HIGH, preferred_element_type=F32)
                for part, weight in ((rows[:, :owned], here), (rows[:, owned:], there))
            )
            for here, there in zip(mine, other)
        ],
        axis=1,
    )
    panel = jnp.sum(swap(panel.reshape(4, block // 8, 2 * width), "x"), axis=0)
    panel = swap(panel.reshape(4, block // 32, 2 * width), "zl")
    return rotated, jnp.sum(panel[:, :, :width], axis=0), jnp.sum(panel[:, :, width:], axis=0)


def solution(mesh):
    fine = Mesh(mesh.devices.reshape(4, 4, 2, 4, 4), FINE)
    return jax.shard_map(
        local,
        mesh=fine,
        in_specs=(
            P(NODE, STATE),
            P(STATE, None),
            P(NODE, None, None),
            P(NODE, None),
            P(NODE),
            P(NODE),
        ),
        out_specs=(P(STATE, NODE), P(NODE, STATE), P(NODE, STATE)),
        check_vma=False,
    )
```

time: 201 us -> 168 us (0.84)
  starting transfers between devices: 78.8 us -> 53.1 us
  blocking collectives: 34.9 us -> 50.6 us
  waiting for transfers between devices: 35.4 us -> 21.6 us
  matrix products: 15.5 us -> 7.07 us
  Pallas kernels: 20.7 us -> 27.7 us
  other arithmetic: 6.69 us -> 3.29 us
  local copies, waits for them, and re-layouts: 4.53 us -> 2.09 us
    all_to_all x0 -> x1, blocking collectives: none -> 23.6 us  [swap(): return lax.all_to_all(pieces, axis, 0, 0, tiled=True)]
    ppermute x12 -> x6, starting transfers between devices: 40.2 us -> 21 us  [ring(): lax.ppermute(shard, axis, [(i, (i + by) % length) for i in range(length)])]
    dot_general x8 -> x4, matrix products: 15.5 us -> 7.07 us  [local(): jnp.dot(part, weight, precision=HIGH, preferred_element_type=F32)]
    all_gather x1, blocking collectives: 34.9 us -> 26.9 us  [local(): rows = gather_rows(lax.all_gather(both, 'zh', axis=0, tiled=True), 'y')]
    ppermute x12 -> x6, waiting for transfers between devices: 18.9 us -> 11.4 us  [ring(): lax.ppermute(shard, axis, [(i, (i + by) % length) for i in range(length)])]
    pallas_call x1 -> x3, Pallas kernels: 14.7 us -> 21.4 us  [the longest x1 10 us: assemble(): pl.pallas_call(assemble_kernel, out_shape=[jax.ShapeDtypeStruct((total, d...]
    all_to_all x5 -> x3, waiting for transfers between devices: 14.5 us -> 10.1 us  [swap(): return lax.all_to_all(pieces, axis, 0, 0, tiled=True)]
    all_to_all x5 -> x3, starting transfers between devices: 31.5 us -> 27.8 us  [swap(): return lax.all_to_all(pieces, axis, 0, 0, tiled=True)]
  transfers between devices with their start and end apart: 19 -> 11, of which waited for: 8 -> 6; matrix products, arithmetic and copies ran while one was open for 11% -> 3% of each run, Pallas kernels for 7% -> 13%
where the time goes in v6:
time: 168 us; the launch traced here: 166 us
  starting transfers between devices  53.1 us (32%)
  blocking collectives  50.6 us (30%)
  Pallas kernels  27.7 us (16%)
  waiting for transfers between devices  21.6 us (13%)
  matrix products  7.07 us (4%)
  other arithmetic  3.29 us (2%)
  local copies, waits for them, and re-layouts  2.09 us (1%)
    all_to_all x3, starting transfers between devices, swap(): return lax.all_to_all(pieces, axis, 0, 0, tiled=True)  27.8 us
    all_gather x1, blocking collectives, local(): rows = gather_rows(lax.all_gather(both, 'zh', axis=0, tiled=True), 'y')  26.9 us
    all_to_all x1, blocking collectives, swap(): return lax.all_to_all(pieces, axis, 0, 0, tiled=True)  23.6 us
    ppermute x6, starting transfers between devices, ring(): lax.ppermute(shard, axis, [(i, (i + by) % length) for i in range(length)])  21 us
    ppermute x6, waiting for transfers between devices, ring(): lax.ppermute(shard, axis, [(i, (i + by) % length) for i in range(length)])  11.4 us
    all_to_all x3, waiting for transfers between devices, swap(): return lax.all_to_all(pieces, axis, 0, 0, tiled=True)  10.1 us
    pallas_call x1, Pallas kernels, assemble(): pl.pallas_call(assemble_kernel, out_shape=[jax.ShapeDtypeStruct((total, d...  10 us
    pallas_call x1, Pallas kernels, apply_cells(): pl.pallas_call(apply_kernel, grid=(width // tile,), in_specs=[fixed((owne...  8.14 us
  transfers between devices with their start and end apart: 11, of which 6 were waited for; matrix products, arithmetic and copies ran while one was open for 3% of the time, Pallas kernels for 13%

profile of v6, /device:TPU:24, one launch (start us, length us, event | category | flops | bytes accessed | tf_op | source)
XLA Modules:
  0.0 166.3 jit_solution(375356838472814838)
XLA Ops:
  0.6 6.2 %rotate.1 = (f32[512,768]{1,0:T(8,128)}, f32[64,768]{1,0:T(8,128)}) custom-call(f32[768,512]{1,0:T(8,128)} %coeffs_ref.1, f32[768,768]{1,0:T(8,128)} %states_ref.5, s32[1,64]{1,0:T(1,128)} %bitcast.33), custom_call_target="tpu_custom_call" | custom-call | flops 1811939328 | bytes 6000000 | tf_op jit(solution)/shard_map/rotate/pallas_call | solution.py:87
  6.9 9.3 %all-to-all-start = ((f32[8,64,768]{2,1,0:T(8,128)}), f32[8,64,768]{2,1,0:T(8,128)S(1)}, u32[]{:S(2)}, u32[]{:S(2)}) async-start(f32[8,64,768]{2,1,0:T(8,128)} %bitcast.31), calls=%async_computation | async-start | bytes 3145728 | tf_op jit(solution)/shard_map/all_to_all | solution.py:249
  16.1 1.3 collective-permute-start
  17.4 10.0 %assemble.1 = (bf16[832,896]{1,0:T(8,128)(2,1)}, bf16[832,896]{1,0:T(8,128)(2,1)}) custom-call(s32[12,125]{1,0:T(8,128)} %connect_ref.1, f32[12,125,125]{2,1,0:T(8,128)} %cell_ref.1, f32[512,768]{1,0:T(8,128)} %get-tuple-element.13._), custom_call_target="tpu_custom_call" | custom-call | flops 8000000000 | bytes 4000000 | tf_op jit(solution)/shard_map/assemble/pallas_call | solution.py:149
  27.4 0.7 copy-done.2
  28.2 3.3 %back.1 = f32[64,768]{1,0:T(8,128)} custom-call(bf16[832,896]{1,0:T(8,128)(2,1)} %get-tuple-element.14.top_ref.refs_2_, bf16[832,896]{1,0:T(8,128)(2,1)} %get-tuple-element.15.low_ref.refs_3_, f32[768,768]{1,0:T(8,128)} %states_ref.5, f32[64,768]{1,0:T(8,128)} %copy-done.2), custom_call_target="tpu_custom_call" | custom-call | flops 600000000 | bytes 4000000 | tf_op jit(solution)/shard_map/back/pallas_call | solution.py:186
  31.4 3.0 %collective-permute-start.1 = (f32[64,768]{1,0:T(8,128)}, f32[64,768]{1,0:T(8,128)S(1)}, u32[]{:S(2)}, u32[]{:S(2)}) collective-permute-start(f32[64,768]{1,0:T(8,128)} %back.1), channel_id=1, source_target_pairs={{0,16},{16,32},{32,48},{48,64},{64,80},{80,96},{96,112},{112,128},... | collective-permute-start | bytes 589832 | tf_op jit(solution)/shard_map/ppermute | solution.py:20
  34.5 1.2 all-to-all-done
  35.8 0.8 pad_maximum_fusion.1.refs_0_
  36.6 0.7 copy-done.3
  37.2 10.7 %all-to-all-start.1 = ((f32[4,16,1536]{2,1,0:T(8,128)}), f32[4,16,1536]{2,1,0:T(8,128)S(1)}, u32[]{:S(2)}, u32[]{:S(2)}) async-start(f32[4,16,1536]{2,1,0:T(8,128)} %bitcast.30), calls=%async_computation.1 | async-start | bytes 786432 | tf_op jit(solution)/shard_map/all_to_all | solution.py:249
  47.9 8.1 %apply.1 = (f32[768,768]{1,0:T(8,128)}, f32[768,768]{1,0:T(8,128)}) custom-call(bf16[832,896]{1,0:T(8,128)(2,1)} %get-tuple-element.18.top_ref, bf16[832,896]{1,0:T(8,128)(2,1)} %get-tuple-element.19.low_ref, f32[768,768]{1,0:T(8,128)} %states_ref.5, f32[64,768]{1,0:T(8,128)} %copy-done.2, f32[6,128]{1,0:T(8,128)} %bitcast.32, ...), custom_call_target="tpu_custom_call" | custom-call | flops 7000000000 | bytes 11000000 | tf_op jit(solution)/shard_map/apply/pallas_call | solution.py:220
  56.1 3.8 %collective-permute-start.6 = (f32[768,768]{1,0:T(8,128)}, f32[768,768]{1,0:T(8,128)S(1)}, u32[]{:S(2)}, u32[]{:S(2)}) collective-permute-start(f32[768,768]{1,0:T(8,128)} %get-tuple-element.21), channel_id=1, source_target_pairs={{0,16},{16,0},{1,17},{17,1},{2,18},{18,2},{3,19},{19,3},{4,20},{20... | collective-permute-start | bytes 7077896 | tf_op jit(solution)/shard_map/ppermute | solution.py:25
  59.9 1.9 %collective-permute-start.7 = (f32[768,768]{1,0:T(8,128)}, f32[768,768]{1,0:T(8,128)}, u32[]{:S(2)}, u32[]{:S(2)}) collective-permute-start(f32[768,768]{1,0:T(8,128)} %get-tuple-element.22), channel_id=1, source_target_pairs={{0,16},{16,0},{1,17},{17,1},{2,18},{18,2},{3,19},{19,3},{4,20},{20... | collective-permute-start | bytes 7077896 | tf_op jit(solution)/shard_map/ppermute | solution.py:25
  61.9 2.3 %all-to-all-done.1 = f32[4,16,1536]{2,1,0:T(8,128)S(1)} async-done(((f32[4,16,1536]{2,1,0:T(8,128)}), f32[4,16,1536]{2,1,0:T(8,128)S(1)}, u32[]{:S(2)}, u32[]{:S(2)}) %all-to-all-start.1) | async-done | bytes 393248 | tf_op jit(solution)/shard_map/all_to_all | solution.py:249
  64.2 26.9 %all_gather.3 = f32[64,1536]{1,0:T(8,128)S(1)} all-gather(f32[16,1536]{1,0:T(8,128)S(1)} %reduce_sum.46), channel_id=1, replica_groups=mesh['x'=4,'zl'=4,'core'=2,'y'=4,'zh'=4] {'zh'}, dimensions={0}, use_global_device_ids=true | all-gather | bytes 491520 | tf_op jit(solution)/shard_map/all_gather | solution.py:291
  91.2 6.1 %collective-permute-start.5 = (f32[64,1536]{1,0:T(8,128)S(1)}, f32[64,1536]{1,0:T(8,128)S(1)}, u32[]{:S(2)}, u32[]{:S(2)}) collective-permute-start(f32[64,1536]{1,0:T(8,128)S(1)} %all_gather.3), channel_id=1, source_target_pairs={{0,8},{4,12},{8,0},{12,4},{1,9},{5,13},{9,1},{13,5},{2,10},{6,14},... | collective-permute-start | bytes 1179656 | tf_op jit(solution)/shard_map/ppermute | solution.py:25
  97.3 1.9 %collective-permute-start.4 = (f32[64,1536]{1,0:T(8,128)S(1)}, f32[64,1536]{1,0:T(8,128)S(1)}, u32[]{:S(2)}, u32[]{:S(2)}) collective-permute-start(f32[64,1536]{1,0:T(8,128)S(1)} %all_gather.3), channel_id=1, source_target_pairs={{0,12},{4,0},{8,4},{12,8},{1,13},{5,1},{9,5},{13,9},{2,14},{6,2},{... | collective-permute-start | bytes 1179656 | tf_op jit(solution)/shard_map/ppermute | solution.py:25
  99.2 5.3 %collective-permute-start.3 = (f32[64,1536]{1,0:T(8,128)S(1)}, f32[64,1536]{1,0:T(8,128)S(1)}, u32[]{:S(2)}, u32[]{:S(2)}) collective-permute-start(f32[64,1536]{1,0:T(8,128)S(1)} %all_gather.3), channel_id=1, source_target_pairs={{0,4},{4,8},{8,12},{12,0},{1,5},{5,9},{9,13},{13,1},{2,6},{6,10},{... | collective-permute-start | bytes 1179656 | tf_op jit(solution)/shard_map/ppermute | solution.py:25
  104.8 8.8 %collective-permute-done.3 = f32[64,1536]{1,0:T(8,128)S(1)} collective-permute-done((f32[64,1536]{1,0:T(8,128)S(1)}, f32[64,1536]{1,0:T(8,128)S(1)}, u32[]{:S(2)}, u32[]{:S(2)}) %collective-permute-start.3) | collective-permute-done | bytes 393248 | tf_op jit(solution)/shard_map/ppermute | solution.py:25
  113.6 1.4 collective-permute-done.4
  115.1 1.3 fusion.2
  116.8 1.4 convolution_add_fusion.1
  118.2 3.1 %fusion = f32[256,768]{1,0:T(8,128)S(1)} fusion(f32[768,768]{1,0:T(8,128)} %collective-permute-done.7, f32[256,1536]{1,0:T(8,128)S(1)} %bitcast.26), kind=kOutput, calls=%fused_computation.3 | convolution fusion | flops 905969664 | bytes 3932160 | tf_op jit(solution)/shard_map/dot_general | solution.py:295
  121.3 1.4 convolution_add_fusion
  122.9 23.6 %all_to_all.20 = f32[4,64,1536]{2,1,0:T(8,128)S(1)} all-to-all(f32[4,64,1536]{2,1,0:T(8,128)S(1)} %bitcast.29), channel_id=1, replica_groups=mesh['x'=4,'zl'=4,'core'=2,'y'=4,'zh'=4] {'x'}, dimensions={0} | all-to-all | bytes 3145728 | tf_op jit(solution)/shard_map/all_to_all | solution.py:249
  146.5 0.9 reduce_sum.47
  147.3 7.9 %all-to-all-start.3 = ((f32[4,16,1536]{2,1,0:T(8,128)}), f32[4,16,1536]{2,1,0:T(8,128)S(1)}, u32[]{:S(2)}, u32[]{:S(2)}) async-start(f32[4,16,1536]{2,1,0:T(8,128)} %bitcast.13), calls=%async_computation.3 | async-start | bytes 786432 | tf_op jit(solution)/shard_map/all_to_all | solution.py:249
  155.2 1.9 %collective-permute-start.2 = (f32[16,768]{1,0:T(8,128)S(1)}, f32[16,768]{1,0:T(8,128)S(1)}, u32[]{:S(2)}, u32[]{:S(2)}) collective-permute-start(f32[16,768]{1,0:T(8,128)S(1)} %slice.39), channel_id=1, source_target_pairs={{0,16},{16,0},{1,17},{17,1},{2,18},{18,2},{3,19},{19,3},{4,20},{20... | collective-permute-start | bytes 147464 | tf_op jit(solution)/shard_map/ppermute | solution.py:25
  157.1 1.2 collective-permute-done.2
  159.0 6.6 %all-to-all-done.3 = f32[4,16,1536]{2,1,0:T(8,128)S(1)} async-done(((f32[4,16,1536]{2,1,0:T(8,128)}), f32[4,16,1536]{2,1,0:T(8,128)S(1)}, u32[]{:S(2)}, u32[]{:S(2)}) %all-to-all-start.3) | async-done | bytes 393248 | tf_op jit(solution)/shard_map/all_to_all | solution.py:249
  165.6 0.7 slice_reduce_fusion
  (26 shorter events, 1.7 us)
Async XLA Ops:
  6.9 9.3 %copy-start.4 = (f32[64,768]{1,0:T(8,128)S(1)}, f32[64,768]{1,0:T(8,128)}, u32[]{:S(2)}) copy-start(f32[64,768]{1,0:T(8,128)} %get-tuple-element.16) | copy-start | bytes 589828
  6.9 28.7 %all-to-all-start = ((f32[8,64,768]{2,1,0:T(8,128)}), f32[8,64,768]{2,1,0:T(8,128)S(1)}, u32[]{:S(2)}, u32[]{:S(2)}) async-start(f32[8,64,768]{2,1,0:T(8,128)} %bitcast.31), calls=%async_computation | async-start | bytes 3145728 | tf_op jit(solution)/shard_map/all_to_all | solution.py:249
  16.1 11.3 %collective-permute-start = (f32[64,768]{1,0:T(8,128)S(1)}, f32[64,768]{1,0:T(8,128)S(1)}, u32[]{:S(2)}, u32[]{:S(2)}) collective-permute-start(f32[64,768]{1,0:T(8,128)S(1)} %copy-done.4), channel_id=1, source_target_pairs={{16,0},{32,16},{48,32},{64,48},{80,64},{96,80},{112,96},{128,112},... | collective-permute-start | bytes 589832 | tf_op jit(solution)/shard_map/ppermute | solution.py:20
  27.4 0.7 copy-start.2
  31.4 5.1 %collective-permute-start.1 = (f32[64,768]{1,0:T(8,128)}, f32[64,768]{1,0:T(8,128)S(1)}, u32[]{:S(2)}, u32[]{:S(2)}) collective-permute-start(f32[64,768]{1,0:T(8,128)} %back.1), channel_id=1, source_target_pairs={{0,16},{16,32},{32,48},{48,64},{64,80},{80,96},{96,112},{112,128},... | collective-permute-start | bytes 589832 | tf_op jit(solution)/shard_map/ppermute | solution.py:20
  36.6 0.7 copy-start.3
  37.2 26.9 %all-to-all-start.1 = ((f32[4,16,1536]{2,1,0:T(8,128)}), f32[4,16,1536]{2,1,0:T(8,128)S(1)}, u32[]{:S(2)}, u32[]{:S(2)}) async-start(f32[4,16,1536]{2,1,0:T(8,128)} %bitcast.30), calls=%async_computation.1 | async-start | bytes 786432 | tf_op jit(solution)/shard_map/all_to_all | solution.py:249
  56.1 59.1 %collective-permute-start.6 = (f32[768,768]{1,0:T(8,128)}, f32[768,768]{1,0:T(8,128)S(1)}, u32[]{:S(2)}, u32[]{:S(2)}) collective-permute-start(f32[768,768]{1,0:T(8,128)} %get-tuple-element.21), channel_id=1, source_target_pairs={{0,16},{16,0},{1,17},{17,1},{2,18},{18,2},{3,19},{19,3},{4,20},{20... | collective-permute-start | bytes 7077896 | tf_op jit(solution)/shard_map/ppermute | solution.py:25
  59.9 58.3 %collective-permute-start.7 = (f32[768,768]{1,0:T(8,128)}, f32[768,768]{1,0:T(8,128)}, u32[]{:S(2)}, u32[]{:S(2)}) collective-permute-start(f32[768,768]{1,0:T(8,128)} %get-tuple-element.22), channel_id=1, source_target_pairs={{0,16},{16,0},{1,17},{17,1},{2,18},{18,2},{3,19},{19,3},{4,20},{20... | collective-permute-start | bytes 7077896 | tf_op jit(solution)/shard_map/ppermute | solution.py:25
  91.2 23.9 %collective-permute-start.5 = (f32[64,1536]{1,0:T(8,128)S(1)}, f32[64,1536]{1,0:T(8,128)S(1)}, u32[]{:S(2)}, u32[]{:S(2)}) collective-permute-start(f32[64,1536]{1,0:T(8,128)S(1)} %all_gather.3), channel_id=1, source_target_pairs={{0,8},{4,12},{8,0},{12,4},{1,9},{5,13},{9,1},{13,5},{2,10},{6,14},... | collective-permute-start | bytes 1179656 | tf_op jit(solution)/shard_map/ppermute | solution.py:25
  97.3 17.7 %collective-permute-start.4 = (f32[64,1536]{1,0:T(8,128)S(1)}, f32[64,1536]{1,0:T(8,128)S(1)}, u32[]{:S(2)}, u32[]{:S(2)}) collective-permute-start(f32[64,1536]{1,0:T(8,128)S(1)} %all_gather.3), channel_id=1, source_target_pairs={{0,12},{4,0},{8,4},{12,8},{1,13},{5,1},{9,5},{13,9},{2,14},{6,2},{... | collective-permute-start | bytes 1179656 | tf_op jit(solution)/shard_map/ppermute | solution.py:25
  99.2 14.4 %collective-permute-start.3 = (f32[64,1536]{1,0:T(8,128)S(1)}, f32[64,1536]{1,0:T(8,128)S(1)}, u32[]{:S(2)}, u32[]{:S(2)}) collective-permute-start(f32[64,1536]{1,0:T(8,128)S(1)} %all_gather.3), channel_id=1, source_target_pairs={{0,4},{4,8},{8,12},{12,0},{1,5},{5,9},{9,13},{13,1},{2,6},{6,10},{... | collective-permute-start | bytes 1179656 | tf_op jit(solution)/shard_map/ppermute | solution.py:25
  115.1 1.7 %copy-start.1 = (f32[768,768]{1,0:T(8,128)S(1)}, f32[768,768]{1,0:T(8,128)}, u32[]{:S(2)}) copy-start(f32[768,768]{1,0:T(8,128)} %get-tuple-element.21) | copy-start | bytes 7077892
  118.2 3.1 %copy-start = (f32[768,768]{1,0:T(8,128)S(1)}, f32[768,768]{1,0:T(8,128)}, u32[]{:S(2)}) copy-start(f32[768,768]{1,0:T(8,128)} %get-tuple-element.22) | copy-start | bytes 7077892
  147.3 18.3 %all-to-all-start.3 = ((f32[4,16,1536]{2,1,0:T(8,128)}), f32[4,16,1536]{2,1,0:T(8,128)S(1)}, u32[]{:S(2)}, u32[]{:S(2)}) async-start(f32[4,16,1536]{2,1,0:T(8,128)} %bitcast.13), calls=%async_computation.3 | async-start | bytes 786432 | tf_op jit(solution)/shard_map/all_to_all | solution.py:249
  155.2 3.1 %collective-permute-start.2 = (f32[16,768]{1,0:T(8,128)S(1)}, f32[16,768]{1,0:T(8,128)S(1)}, u32[]{:S(2)}, u32[]{:S(2)}) collective-permute-start(f32[16,768]{1,0:T(8,128)S(1)} %slice.39), channel_id=1, source_target_pairs={{0,16},{16,0},{1,17},{17,1},{2,18},{18,2},{3,19},{19,3},{4,20},{20... | collective-permute-start | bytes 147464 | tf_op jit(solution)/shard_map/ppermute | solution.py:25

commit v7 on v6

--- a/solution.py
+++ b/solution.py
@@ -249,18 +249,6 @@
     return lax.all_to_all(pieces, axis, 0, 0, tiled=True)
 
 
-def gather_rows(rows, axis):
-    length = lax.axis_size(axis)
-    here = lax.axis_index(axis)
-    out = jnp.zeros((length,) + rows.shape, rows.dtype)
-    out = lax.dynamic_update_slice_in_dim(out, rows[None], here, 0)
-    for by in (1, length - 1, 2):
-        out = lax.dynamic_update_slice_in_dim(
-            out, ring(rows, axis, by)[None], (here - by) % length, 0
-        )
-    return out.reshape((-1,) + rows.shape[1:])
-
-
 def local(states, coeffs, cell_matrix, connect, face_list, node_mass):
     owned, width = states.shape
     block = coeffs.shape[1]
@@ -288,7 +276,9 @@
         [jnp.where(first, own, theirs), jnp.where(first, theirs, own)], axis=0
     )
 
-    rows = gather_rows(lax.all_gather(both, "zh", axis=0, tiled=True), "y")
+    group = lax.all_gather(both, "zh", axis=0, tiled=True)
+    rows = swap(jnp.broadcast_to(group[None], (4,) + group.shape), "y")
+    rows = rows.reshape(block // 2, 2 * owned)
     panel = jnp.concatenate(
         [
             sum(

time: 168 us -> 166 us (0.988)
  blocking collectives: 50.6 us -> 75.6 us
  starting transfers between devices: 53.1 us -> 37.9 us
  waiting for transfers between devices: 21.6 us -> 9.83 us
    all_to_all x1 -> x2, blocking collectives: 23.6 us -> 48.5 us  [swap(): return lax.all_to_all(pieces, axis, 0, 0, tiled=True)]
    ppermute x6 -> x3, starting transfers between devices: 21 us -> 7.63 us  [ring(): lax.ppermute(shard, axis, [(i, (i + by) % length) for i in range(length)])]
    ppermute x6 -> x3, waiting for transfers between devices: 11.4 us -> 1.2 us  [ring(): lax.ppermute(shard, axis, [(i, (i + by) % length) for i in range(length)])]
    all_to_all x3, starting transfers between devices: 27.8 us -> 25.9 us  [swap(): return lax.all_to_all(pieces, axis, 0, 0, tiled=True)]
  transfers between devices with their start and end apart: 11 -> 8, of which waited for: 6 -> 4; matrix products, arithmetic and copies ran while one was open for 3% -> 4% of each run, Pallas kernels for 13% -> 13%
where the time goes in v7:
time: 166 us; the launch traced here: 164 us
  blocking collectives  75.6 us (46%)
  starting transfers between devices  37.9 us (23%)
  Pallas kernels  27.7 us (17%)
  waiting for transfers between devices  9.83 us (6%)
  matrix products  7.07 us (4%)
  other arithmetic  3.29 us (2%)
  local copies, waits for them, and re-layouts  1.94 us (1%)
    all_to_all x2, blocking collectives, swap(): return lax.all_to_all(pieces, axis, 0, 0, tiled=True)  48.5 us
    all_gather x1, blocking collectives, local(): group = lax.all_gather(both, 'zh', axis=0, tiled=True)  27.1 us
    all_to_all x3, starting transfers between devices, swap(): return lax.all_to_all(pieces, axis, 0, 0, tiled=True)  25.9 us
    pallas_call x1, Pallas kernels, assemble(): pl.pallas_call(assemble_kernel, out_shape=[jax.ShapeDtypeStruct((total, d...  9.99 us
    all_to_all x3, waiting for transfers between devices, swap(): return lax.all_to_all(pieces, axis, 0, 0, tiled=True)  8.62 us
    pallas_call x1, Pallas kernels, apply_cells(): pl.pallas_call(apply_kernel, grid=(width // tile,), in_specs=[fixed((owne...  8.17 us
    ppermute x3, starting transfers between devices, ring(): lax.ppermute(shard, axis, [(i, (i + by) % length) for i in range(length)])  7.63 us
    dot_general x4, matrix products, local(): jnp.dot(part, weight, precision=HIGH, preferred_element_type=F32)  7.07 us
  transfers between devices with their start and end apart: 8, of which 4 were waited for; matrix products, arithmetic and copies ran while one was open for 4% of the time, Pallas kernels for 13%

profile of v7, /device:TPU:24, one launch (start us, length us, event | category | flops | bytes accessed | tf_op | source)
XLA Modules:
  0.0 164.1 jit_solution(13764346469960756171)
XLA Ops:
  0.6 6.3 %rotate.1 = (f32[512,768]{1,0:T(8,128)}, f32[64,768]{1,0:T(8,128)}) custom-call(f32[768,512]{1,0:T(8,128)} %coeffs_ref.1, f32[768,768]{1,0:T(8,128)} %states_ref.5, s32[1,64]{1,0:T(1,128)} %bitcast.25), custom_call_target="tpu_custom_call" | custom-call | flops 1811939328 | bytes 6000000 | tf_op jit(solution)/shard_map/rotate/pallas_call | solution.py:87
  6.9 9.3 %all-to-all-start = ((f32[8,64,768]{2,1,0:T(8,128)}), f32[8,64,768]{2,1,0:T(8,128)S(1)}, u32[]{:S(2)}, u32[]{:S(2)}) async-start(f32[8,64,768]{2,1,0:T(8,128)} %bitcast.23), calls=%async_computation | async-start | bytes 3145728 | tf_op jit(solution)/shard_map/all_to_all | solution.py:249
  16.1 1.3 collective-permute-start
  17.4 10.0 %assemble.1 = (bf16[832,896]{1,0:T(8,128)(2,1)}, bf16[832,896]{1,0:T(8,128)(2,1)}) custom-call(s32[12,125]{1,0:T(8,128)} %connect_ref.1, f32[12,125,125]{2,1,0:T(8,128)} %cell_ref.1, f32[512,768]{1,0:T(8,128)} %get-tuple-element.13._), custom_call_target="tpu_custom_call" | custom-call | flops 8000000000 | bytes 4000000 | tf_op jit(solution)/shard_map/assemble/pallas_call | solution.py:149
  27.4 0.7 copy-done.2
  28.1 3.3 %back.1 = f32[64,768]{1,0:T(8,128)} custom-call(bf16[832,896]{1,0:T(8,128)(2,1)} %get-tuple-element.14.top_ref.refs_2_, bf16[832,896]{1,0:T(8,128)(2,1)} %get-tuple-element.15.low_ref.refs_3_, f32[768,768]{1,0:T(8,128)} %states_ref.5, f32[64,768]{1,0:T(8,128)} %copy-done.2), custom_call_target="tpu_custom_call" | custom-call | flops 600000000 | bytes 4000000 | tf_op jit(solution)/shard_map/back/pallas_call | solution.py:186
  31.4 3.0 %collective-permute-start.1 = (f32[64,768]{1,0:T(8,128)}, f32[64,768]{1,0:T(8,128)S(1)}, u32[]{:S(2)}, u32[]{:S(2)}) collective-permute-start(f32[64,768]{1,0:T(8,128)} %back.1), channel_id=1, source_target_pairs={{0,16},{16,32},{32,48},{48,64},{64,80},{80,96},{96,112},{112,128},... | collective-permute-start | bytes 589832 | tf_op jit(solution)/shard_map/ppermute | solution.py:20
  34.5 1.2 all-to-all-done
  35.8 0.8 pad_maximum_fusion.1.refs_0_
  36.6 0.7 copy-done.3
  37.2 10.7 %all-to-all-start.1 = ((f32[4,16,1536]{2,1,0:T(8,128)}), f32[4,16,1536]{2,1,0:T(8,128)S(1)}, u32[]{:S(2)}, u32[]{:S(2)}) async-start(f32[4,16,1536]{2,1,0:T(8,128)} %bitcast.22), calls=%async_computation.1 | async-start | bytes 786432 | tf_op jit(solution)/shard_map/all_to_all | solution.py:249
  47.9 8.2 %apply.1 = (f32[768,768]{1,0:T(8,128)}, f32[768,768]{1,0:T(8,128)}) custom-call(bf16[832,896]{1,0:T(8,128)(2,1)} %get-tuple-element.18.top_ref, bf16[832,896]{1,0:T(8,128)(2,1)} %get-tuple-element.19.low_ref, f32[768,768]{1,0:T(8,128)} %states_ref.5, f32[64,768]{1,0:T(8,128)} %copy-done.2, f32[6,128]{1,0:T(8,128)} %bitcast.24, ...), custom_call_target="tpu_custom_call" | custom-call | flops 7000000000 | bytes 11000000 | tf_op jit(solution)/shard_map/apply/pallas_call | solution.py:220
  56.1 3.8 %collective-permute-start.3 = (f32[768,768]{1,0:T(8,128)}, f32[768,768]{1,0:T(8,128)}, u32[]{:S(2)}, u32[]{:S(2)}) collective-permute-start(f32[768,768]{1,0:T(8,128)} %get-tuple-element.21), channel_id=1, source_target_pairs={{0,16},{16,0},{1,17},{17,1},{2,18},{18,2},{3,19},{19,3},{4,20},{20... | collective-permute-start | bytes 7077896 | tf_op jit(solution)/shard_map/ppermute | solution.py:25
  59.9 1.9 %collective-permute-start.4 = (f32[768,768]{1,0:T(8,128)}, f32[768,768]{1,0:T(8,128)S(1)}, u32[]{:S(2)}, u32[]{:S(2)}) collective-permute-start(f32[768,768]{1,0:T(8,128)} %get-tuple-element.22), channel_id=1, source_target_pairs={{0,16},{16,0},{1,17},{17,1},{2,18},{18,2},{3,19},{19,3},{4,20},{20... | collective-permute-start | bytes 7077896 | tf_op jit(solution)/shard_map/ppermute | solution.py:25
  61.8 2.4 %all-to-all-done.1 = f32[4,16,1536]{2,1,0:T(8,128)S(1)} async-done(((f32[4,16,1536]{2,1,0:T(8,128)}), f32[4,16,1536]{2,1,0:T(8,128)S(1)}, u32[]{:S(2)}, u32[]{:S(2)}) %all-to-all-start.1) | async-done | bytes 393248 | tf_op jit(solution)/shard_map/all_to_all | solution.py:249
  64.2 27.1 %all_gather.3 = f32[64,1536]{1,0:T(8,128)S(1)} all-gather(f32[16,1536]{1,0:T(8,128)S(1)} %reduce_sum.46), channel_id=1, replica_groups=mesh['x'=4,'zl'=4,'core'=2,'y'=4,'zh'=4] {'zh'}, dimensions={0}, use_global_device_ids=true | all-gather | bytes 491520 | tf_op jit(solution)/shard_map/all_gather | solution.py:279
  91.3 0.2 broadcast_in_dim.2
  91.5 25.4 %all_to_all.25 = f32[4,64,1536]{2,1,0:T(8,128)S(1)} all-to-all(f32[4,64,1536]{2,1,0:T(8,128)S(1)} %broadcast_in_dim.2), channel_id=1, replica_groups=mesh['x'=4,'zl'=4,'core'=2,'y'=4,'zh'=4] {'y'}, dimensions={0} | all-to-all | bytes 3145728 | tf_op jit(solution)/shard_map/all_to_all | solution.py:249
  117.0 3.1 %fusion.2 = f32[256,768]{1,0:T(8,128)S(1)} fusion(f32[768,768]{1,0:T(8,128)} %collective-permute-done.3, f32[256,1536]{1,0:T(8,128)S(1)} %bitcast.16), kind=kOutput, calls=%fused_computation.5 | convolution fusion | flops 905969664 | bytes 3932160 | tf_op jit(solution)/shard_map/dot_general | solution.py:285
  120.0 1.4 convolution_add_fusion.1
  121.4 1.3 fusion
  122.7 0.4 copy-done
  123.1 1.4 convolution_add_fusion
  124.5 0.2 pad_maximum_fusion
  124.7 23.0 %all_to_all.26 = f32[4,64,1536]{2,1,0:T(8,128)S(1)} all-to-all(f32[4,64,1536]{2,1,0:T(8,128)S(1)} %bitcast.21), channel_id=1, replica_groups=mesh['x'=4,'zl'=4,'core'=2,'y'=4,'zh'=4] {'x'}, dimensions={0} | all-to-all | bytes 3145728 | tf_op jit(solution)/shard_map/all_to_all | solution.py:249
  147.7 0.8 reduce_sum.47
  148.5 6.0 %all-to-all-start.4 = ((f32[4,16,1536]{2,1,0:T(8,128)}), f32[4,16,1536]{2,1,0:T(8,128)S(1)}, u32[]{:S(2)}, u32[]{:S(2)}) async-start(f32[4,16,1536]{2,1,0:T(8,128)} %bitcast.9), calls=%async_computation.4 | async-start | bytes 786432 | tf_op jit(solution)/shard_map/all_to_all | solution.py:249
  154.5 1.9 %collective-permute-start.2 = (f32[16,768]{1,0:T(8,128)S(1)}, f32[16,768]{1,0:T(8,128)S(1)}, u32[]{:S(2)}, u32[]{:S(2)}) collective-permute-start(f32[16,768]{1,0:T(8,128)S(1)} %slice.39), channel_id=1, source_target_pairs={{0,16},{16,0},{1,17},{17,1},{2,18},{18,2},{3,19},{19,3},{4,20},{20... | collective-permute-start | bytes 147464 | tf_op jit(solution)/shard_map/ppermute | solution.py:25
  156.5 1.2 collective-permute-done.2
  157.7 0.6 pad_maximum_fusion.2
  158.3 5.1 %all-to-all-done.4 = f32[4,16,1536]{2,1,0:T(8,128)S(1)} async-done(((f32[4,16,1536]{2,1,0:T(8,128)}), f32[4,16,1536]{2,1,0:T(8,128)S(1)}, u32[]{:S(2)}, u32[]{:S(2)}) %all-to-all-start.4) | async-done | bytes 393248 | tf_op jit(solution)/shard_map/all_to_all | solution.py:249
  163.4 0.7 slice_reduce_fusion
  (17 shorter events, 0.2 us)
Async XLA Ops:
  6.9 9.3 %copy-start.4 = (f32[64,768]{1,0:T(8,128)S(1)}, f32[64,768]{1,0:T(8,128)}, u32[]{:S(2)}) copy-start(f32[64,768]{1,0:T(8,128)} %get-tuple-element.16) | copy-start | bytes 589828
  6.9 28.7 %all-to-all-start = ((f32[8,64,768]{2,1,0:T(8,128)}), f32[8,64,768]{2,1,0:T(8,128)S(1)}, u32[]{:S(2)}, u32[]{:S(2)}) async-start(f32[8,64,768]{2,1,0:T(8,128)} %bitcast.23), calls=%async_computation | async-start | bytes 3145728 | tf_op jit(solution)/shard_map/all_to_all | solution.py:249
  16.1 11.3 %collective-permute-start = (f32[64,768]{1,0:T(8,128)S(1)}, f32[64,768]{1,0:T(8,128)S(1)}, u32[]{:S(2)}, u32[]{:S(2)}) collective-permute-start(f32[64,768]{1,0:T(8,128)S(1)} %copy-done.4), channel_id=1, source_target_pairs={{16,0},{32,16},{48,32},{64,48},{80,64},{96,80},{112,96},{128,112},... | collective-permute-start | bytes 589832 | tf_op jit(solution)/shard_map/ppermute | solution.py:20
  27.4 0.7 copy-start.2
  31.4 5.1 %collective-permute-start.1 = (f32[64,768]{1,0:T(8,128)}, f32[64,768]{1,0:T(8,128)S(1)}, u32[]{:S(2)}, u32[]{:S(2)}) collective-permute-start(f32[64,768]{1,0:T(8,128)} %back.1), channel_id=1, source_target_pairs={{0,16},{16,32},{32,48},{48,64},{64,80},{80,96},{96,112},{112,128},... | collective-permute-start | bytes 589832 | tf_op jit(solution)/shard_map/ppermute | solution.py:20
  36.6 0.7 copy-start.3
  37.2 26.9 %all-to-all-start.1 = ((f32[4,16,1536]{2,1,0:T(8,128)}), f32[4,16,1536]{2,1,0:T(8,128)S(1)}, u32[]{:S(2)}, u32[]{:S(2)}) async-start(f32[4,16,1536]{2,1,0:T(8,128)} %bitcast.22), calls=%async_computation.1 | async-start | bytes 786432 | tf_op jit(solution)/shard_map/all_to_all | solution.py:249
  56.1 60.9 %collective-permute-start.3 = (f32[768,768]{1,0:T(8,128)}, f32[768,768]{1,0:T(8,128)}, u32[]{:S(2)}, u32[]{:S(2)}) collective-permute-start(f32[768,768]{1,0:T(8,128)} %get-tuple-element.21), channel_id=1, source_target_pairs={{0,16},{16,0},{1,17},{17,1},{2,18},{18,2},{3,19},{19,3},{4,20},{20... | collective-permute-start | bytes 7077896 | tf_op jit(solution)/shard_map/ppermute | solution.py:25
  59.9 61.5 %collective-permute-start.4 = (f32[768,768]{1,0:T(8,128)}, f32[768,768]{1,0:T(8,128)S(1)}, u32[]{:S(2)}, u32[]{:S(2)}) collective-permute-start(f32[768,768]{1,0:T(8,128)} %get-tuple-element.22), channel_id=1, source_target_pairs={{0,16},{16,0},{1,17},{17,1},{2,18},{18,2},{3,19},{19,3},{4,20},{20... | collective-permute-start | bytes 7077896 | tf_op jit(solution)/shard_map/ppermute | solution.py:25
  117.0 3.1 %copy-start.1 = (f32[768,768]{1,0:T(8,128)S(1)}, f32[768,768]{1,0:T(8,128)}, u32[]{:S(2)}) copy-start(f32[768,768]{1,0:T(8,128)} %get-tuple-element.21) | copy-start | bytes 7077892
  121.4 1.7 %copy-start = (f32[768,768]{1,0:T(8,128)S(1)}, f32[768,768]{1,0:T(8,128)}, u32[]{:S(2)}) copy-start(f32[768,768]{1,0:T(8,128)} %get-tuple-element.22) | copy-start | bytes 7077892
  148.5 14.9 %all-to-all-start.4 = ((f32[4,16,1536]{2,1,0:T(8,128)}), f32[4,16,1536]{2,1,0:T(8,128)S(1)}, u32[]{:S(2)}, u32[]{:S(2)}) async-start(f32[4,16,1536]{2,1,0:T(8,128)} %bitcast.9), calls=%async_computation.4 | async-start | bytes 786432 | tf_op jit(solution)/shard_map/all_to_all | solution.py:249
  154.5 3.1 %collective-permute-start.2 = (f32[16,768]{1,0:T(8,128)S(1)}, f32[16,768]{1,0:T(8,128)S(1)}, u32[]{:S(2)}, u32[]{:S(2)}) collective-permute-start(f32[16,768]{1,0:T(8,128)S(1)} %slice.39), channel_id=1, source_target_pairs={{0,16},{16,0},{1,17},{17,1},{2,18},{18,2},{3,19},{19,3},{4,20},{20... | collective-permute-start | bytes 147464 | tf_op jit(solution)/shard_map/ppermute | solution.py:25

commit v8 on v7

--- a/solution.py
+++ b/solution.py
@@ -181,13 +181,15 @@
 def apply_back(matrix, states, ghosts):
     owned, width = states.shape
     face, depth = ghosts.shape[0], matrix[0].shape[1]
-    fixed = lambda shape: pl.BlockSpec(shape, lambda i: (0, 0))
+    tile = 384
     rows = pl.BlockSpec((face, depth), lambda i: (owned // face, 0))
+    tall = pl.BlockSpec((owned, tile), lambda i: (0, i))
+    low = pl.BlockSpec((face, tile), lambda i: (0, i))
     return pl.pallas_call(
         back_kernel,
-        grid=(1,),
-        in_specs=[rows, rows, fixed(states.shape), fixed(ghosts.shape)],
-        out_specs=fixed(ghosts.shape),
+        grid=(width // tile,),
+        in_specs=[rows, rows, tall, low],
+        out_specs=low,
         out_shape=jax.ShapeDtypeStruct(ghosts.shape, F32),
         compiler_params=params(),
         cost_estimate=cost(600000000, 4000000),

time: 166 us -> 165 us (level)
  blocking collectives: 75.6 us -> 70.8 us
  waiting for transfers between devices: 9.83 us -> 14 us
    all_to_all x3, waiting for transfers between devices: 8.62 us -> 12.8 us  [swap(): return lax.all_to_all(pieces, axis, 0, 0, tiled=True)]
    all_gather x1, blocking collectives: 27.1 us -> 23.4 us  [local(): group = lax.all_gather(both, 'zh', axis=0, tiled=True)]
where the time goes in v8:
time: 165 us; the launch traced here: 164 us
  blocking collectives  70.8 us (43%)
  starting transfers between devices  38.4 us (23%)
  Pallas kernels  27.3 us (17%)
  waiting for transfers between devices  14 us (8%)
  matrix products  7.08 us (4%)
  other arithmetic  3.29 us (2%)
  local copies, waits for them, and re-layouts  1.94 us (1%)
    all_to_all x2, blocking collectives, swap(): return lax.all_to_all(pieces, axis, 0, 0, tiled=True)  47.4 us
    all_to_all x3, starting transfers between devices, swap(): return lax.all_to_all(pieces, axis, 0, 0, tiled=True)  26.9 us
    all_gather x1, blocking collectives, local(): group = lax.all_gather(both, 'zh', axis=0, tiled=True)  23.4 us
    all_to_all x3, waiting for transfers between devices, swap(): return lax.all_to_all(pieces, axis, 0, 0, tiled=True)  12.8 us
    pallas_call x1, Pallas kernels, assemble(): pl.pallas_call(assemble_kernel, out_shape=[jax.ShapeDtypeStruct((total, d...  9.99 us
    pallas_call x1, Pallas kernels, apply_cells(): pl.pallas_call(apply_kernel, grid=(width // tile,), in_specs=[fixed((owne...  8.17 us
    ppermute x3, starting transfers between devices, ring(): lax.ppermute(shard, axis, [(i, (i + by) % length) for i in range(length)])  7.2 us
    dot_general x4, matrix products, local(): jnp.dot(part, weight, precision=HIGH, preferred_element_type=F32)  7.08 us
  transfers between devices with their start and end apart: 8, of which 4 were waited for; matrix products, arithmetic and copies ran while one was open for 4% of the time, Pallas kernels for 13%

profile of v8, /device:TPU:24, one launch (start us, length us, event | category | flops | bytes accessed | tf_op | source)
XLA Modules:
  0.0 163.6 jit_solution(2659398636632889002)
XLA Ops:
  0.6 6.3 %rotate.1 = (f32[512,768]{1,0:T(8,128)}, f32[64,768]{1,0:T(8,128)}) custom-call(f32[768,512]{1,0:T(8,128)} %coeffs_ref.1, f32[768,768]{1,0:T(8,128)} %states_ref.5, s32[1,64]{1,0:T(1,128)} %bitcast.25), custom_call_target="tpu_custom_call" | custom-call | flops 1811939328 | bytes 6000000 | tf_op jit(solution)/shard_map/rotate/pallas_call | solution.py:87
  6.9 9.3 %all-to-all-start = ((f32[8,64,768]{2,1,0:T(8,128)}), f32[8,64,768]{2,1,0:T(8,128)S(1)}, u32[]{:S(2)}, u32[]{:S(2)}) async-start(f32[8,64,768]{2,1,0:T(8,128)} %bitcast.23), calls=%async_computation | async-start | bytes 3145728 | tf_op jit(solution)/shard_map/all_to_all | solution.py:251
  16.1 1.3 collective-permute-start
  17.4 10.0 %assemble.1 = (bf16[832,896]{1,0:T(8,128)(2,1)}, bf16[832,896]{1,0:T(8,128)(2,1)}) custom-call(s32[12,125]{1,0:T(8,128)} %connect_ref.1, f32[12,125,125]{2,1,0:T(8,128)} %cell_ref.1, f32[512,768]{1,0:T(8,128)} %get-tuple-element.13._), custom_call_target="tpu_custom_call" | custom-call | flops 8000000000 | bytes 4000000 | tf_op jit(solution)/shard_map/assemble/pallas_call | solution.py:149
  27.4 0.7 copy-done.2
  28.1 2.9 %back.1 = f32[64,768]{1,0:T(8,128)} custom-call(bf16[832,896]{1,0:T(8,128)(2,1)} %get-tuple-element.14.top_ref.refs_2_, bf16[832,896]{1,0:T(8,128)(2,1)} %get-tuple-element.15.low_ref.refs_3_, f32[768,768]{1,0:T(8,128)} %states_ref.5, f32[64,768]{1,0:T(8,128)} %copy-done.2), custom_call_target="tpu_custom_call" | custom-call | flops 600000000 | bytes 4000000 | tf_op jit(solution)/shard_map/back/pallas_call | solution.py:188
  31.0 3.0 %collective-permute-start.1 = (f32[64,768]{1,0:T(8,128)}, f32[64,768]{1,0:T(8,128)S(1)}, u32[]{:S(2)}, u32[]{:S(2)}) collective-permute-start(f32[64,768]{1,0:T(8,128)} %back.1), channel_id=1, source_target_pairs={{0,16},{16,32},{32,48},{48,64},{64,80},{80,96},{96,112},{112,128},... | collective-permute-start | bytes 589832 | tf_op jit(solution)/shard_map/ppermute | solution.py:20
  34.1 1.6 all-to-all-done
  35.8 0.8 pad_maximum_fusion.1.refs_0_
  36.6 0.7 copy-done.3
  37.2 10.7 %all-to-all-start.1 = ((f32[4,16,1536]{2,1,0:T(8,128)}), f32[4,16,1536]{2,1,0:T(8,128)S(1)}, u32[]{:S(2)}, u32[]{:S(2)}) async-start(f32[4,16,1536]{2,1,0:T(8,128)} %bitcast.22), calls=%async_computation.1 | async-start | bytes 786432 | tf_op jit(solution)/shard_map/all_to_all | solution.py:251
  47.9 8.2 %apply.1 = (f32[768,768]{1,0:T(8,128)}, f32[768,768]{1,0:T(8,128)}) custom-call(bf16[832,896]{1,0:T(8,128)(2,1)} %get-tuple-element.18.top_ref, bf16[832,896]{1,0:T(8,128)(2,1)} %get-tuple-element.19.low_ref, f32[768,768]{1,0:T(8,128)} %states_ref.5, f32[64,768]{1,0:T(8,128)} %copy-done.2, f32[6,128]{1,0:T(8,128)} %bitcast.24, ...), custom_call_target="tpu_custom_call" | custom-call | flops 7000000000 | bytes 11000000 | tf_op jit(solution)/shard_map/apply/pallas_call | solution.py:222
  56.1 3.4 %collective-permute-start.3 = (f32[768,768]{1,0:T(8,128)}, f32[768,768]{1,0:T(8,128)}, u32[]{:S(2)}, u32[]{:S(2)}) collective-permute-start(f32[768,768]{1,0:T(8,128)} %get-tuple-element.21), channel_id=1, source_target_pairs={{0,16},{16,0},{1,17},{17,1},{2,18},{18,2},{3,19},{19,3},{4,20},{20... | collective-permute-start | bytes 7077896 | tf_op jit(solution)/shard_map/ppermute | solution.py:25
  59.5 1.9 %collective-permute-start.4 = (f32[768,768]{1,0:T(8,128)}, f32[768,768]{1,0:T(8,128)S(1)}, u32[]{:S(2)}, u32[]{:S(2)}) collective-permute-start(f32[768,768]{1,0:T(8,128)} %get-tuple-element.22), channel_id=1, source_target_pairs={{0,16},{16,0},{1,17},{17,1},{2,18},{18,2},{3,19},{19,3},{4,20},{20... | collective-permute-start | bytes 7077896 | tf_op jit(solution)/shard_map/ppermute | solution.py:25
  61.4 6.2 %all-to-all-done.1 = f32[4,16,1536]{2,1,0:T(8,128)S(1)} async-done(((f32[4,16,1536]{2,1,0:T(8,128)}), f32[4,16,1536]{2,1,0:T(8,128)S(1)}, u32[]{:S(2)}, u32[]{:S(2)}) %all-to-all-start.1) | async-done | bytes 393248 | tf_op jit(solution)/shard_map/all_to_all | solution.py:251
  67.6 23.4 %all_gather.3 = f32[64,1536]{1,0:T(8,128)S(1)} all-gather(f32[16,1536]{1,0:T(8,128)S(1)} %reduce_sum.46), channel_id=1, replica_groups=mesh['x'=4,'zl'=4,'core'=2,'y'=4,'zh'=4] {'zh'}, dimensions={0}, use_global_device_ids=true | all-gather | bytes 491520 | tf_op jit(solution)/shard_map/all_gather | solution.py:281
  91.0 0.2 broadcast_in_dim.2
  91.1 25.2 %all_to_all.25 = f32[4,64,1536]{2,1,0:T(8,128)S(1)} all-to-all(f32[4,64,1536]{2,1,0:T(8,128)S(1)} %broadcast_in_dim.2), channel_id=1, replica_groups=mesh['x'=4,'zl'=4,'core'=2,'y'=4,'zh'=4] {'y'}, dimensions={0} | all-to-all | bytes 3145728 | tf_op jit(solution)/shard_map/all_to_all | solution.py:251
  116.3 3.1 %fusion.2 = f32[256,768]{1,0:T(8,128)S(1)} fusion(f32[768,768]{1,0:T(8,128)} %collective-permute-done.3, f32[256,1536]{1,0:T(8,128)S(1)} %bitcast.16), kind=kOutput, calls=%fused_computation.5 | convolution fusion | flops 905969664 | bytes 3932160 | tf_op jit(solution)/shard_map/dot_general | solution.py:287
  119.4 1.4 convolution_add_fusion.1
  120.8 1.3 fusion
  122.1 0.4 copy-done
  122.5 1.4 convolution_add_fusion
  123.8 0.2 pad_maximum_fusion
  124.0 22.2 %all_to_all.26 = f32[4,64,1536]{2,1,0:T(8,128)S(1)} all-to-all(f32[4,64,1536]{2,1,0:T(8,128)S(1)} %bitcast.21), channel_id=1, replica_groups=mesh['x'=4,'zl'=4,'core'=2,'y'=4,'zh'=4] {'x'}, dimensions={0} | all-to-all | bytes 3145728 | tf_op jit(solution)/shard_map/all_to_all | solution.py:251
  146.3 0.8 reduce_sum.47
  147.1 7.0 %all-to-all-start.4 = ((f32[4,16,1536]{2,1,0:T(8,128)}), f32[4,16,1536]{2,1,0:T(8,128)S(1)}, u32[]{:S(2)}, u32[]{:S(2)}) async-start(f32[4,16,1536]{2,1,0:T(8,128)} %bitcast.9), calls=%async_computation.4 | async-start | bytes 786432 | tf_op jit(solution)/shard_map/all_to_all | solution.py:251
  154.1 1.9 %collective-permute-start.2 = (f32[16,768]{1,0:T(8,128)S(1)}, f32[16,768]{1,0:T(8,128)S(1)}, u32[]{:S(2)}, u32[]{:S(2)}) collective-permute-start(f32[16,768]{1,0:T(8,128)S(1)} %slice.39), channel_id=1, source_target_pairs={{0,16},{16,0},{1,17},{17,1},{2,18},{18,2},{3,19},{19,3},{4,20},{20... | collective-permute-start | bytes 147464 | tf_op jit(solution)/shard_map/ppermute | solution.py:25
  156.0 1.2 collective-permute-done.2
  157.2 0.6 pad_maximum_fusion.2
  157.9 5.1 %all-to-all-done.4 = f32[4,16,1536]{2,1,0:T(8,128)S(1)} async-done(((f32[4,16,1536]{2,1,0:T(8,128)}), f32[4,16,1536]{2,1,0:T(8,128)S(1)}, u32[]{:S(2)}, u32[]{:S(2)}) %all-to-all-start.4) | async-done | bytes 393248 | tf_op jit(solution)/shard_map/all_to_all | solution.py:251
  163.0 0.7 slice_reduce_fusion
  (17 shorter events, 0.2 us)
Async XLA Ops:
  6.9 9.3 %copy-start.4 = (f32[64,768]{1,0:T(8,128)S(1)}, f32[64,768]{1,0:T(8,128)}, u32[]{:S(2)}) copy-start(f32[64,768]{1,0:T(8,128)} %get-tuple-element.16) | copy-start | bytes 589828
  6.9 28.7 %all-to-all-start = ((f32[8,64,768]{2,1,0:T(8,128)}), f32[8,64,768]{2,1,0:T(8,128)S(1)}, u32[]{:S(2)}, u32[]{:S(2)}) async-start(f32[8,64,768]{2,1,0:T(8,128)} %bitcast.23), calls=%async_computation | async-start | bytes 3145728 | tf_op jit(solution)/shard_map/all_to_all | solution.py:251
  16.1 11.3 %collective-permute-start = (f32[64,768]{1,0:T(8,128)S(1)}, f32[64,768]{1,0:T(8,128)S(1)}, u32[]{:S(2)}, u32[]{:S(2)}) collective-permute-start(f32[64,768]{1,0:T(8,128)S(1)} %copy-done.4), channel_id=1, source_target_pairs={{16,0},{32,16},{48,32},{64,48},{80,64},{96,80},{112,96},{128,112},... | collective-permute-start | bytes 589832 | tf_op jit(solution)/shard_map/ppermute | solution.py:20
  27.4 0.7 copy-start.2
  31.0 5.5 %collective-permute-start.1 = (f32[64,768]{1,0:T(8,128)}, f32[64,768]{1,0:T(8,128)S(1)}, u32[]{:S(2)}, u32[]{:S(2)}) collective-permute-start(f32[64,768]{1,0:T(8,128)} %back.1), channel_id=1, source_target_pairs={{0,16},{16,32},{32,48},{48,64},{64,80},{80,96},{96,112},{112,128},... | collective-permute-start | bytes 589832 | tf_op jit(solution)/shard_map/ppermute | solution.py:20
  36.6 0.7 copy-start.3
  37.2 30.3 %all-to-all-start.1 = ((f32[4,16,1536]{2,1,0:T(8,128)}), f32[4,16,1536]{2,1,0:T(8,128)S(1)}, u32[]{:S(2)}, u32[]{:S(2)}) async-start(f32[4,16,1536]{2,1,0:T(8,128)} %bitcast.22), calls=%async_computation.1 | async-start | bytes 786432 | tf_op jit(solution)/shard_map/all_to_all | solution.py:251
  56.1 60.2 %collective-permute-start.3 = (f32[768,768]{1,0:T(8,128)}, f32[768,768]{1,0:T(8,128)}, u32[]{:S(2)}, u32[]{:S(2)}) collective-permute-start(f32[768,768]{1,0:T(8,128)} %get-tuple-element.21), channel_id=1, source_target_pairs={{0,16},{16,0},{1,17},{17,1},{2,18},{18,2},{3,19},{19,3},{4,20},{20... | collective-permute-start | bytes 7077896 | tf_op jit(solution)/shard_map/ppermute | solution.py:25
  59.5 61.3 %collective-permute-start.4 = (f32[768,768]{1,0:T(8,128)}, f32[768,768]{1,0:T(8,128)S(1)}, u32[]{:S(2)}, u32[]{:S(2)}) collective-permute-start(f32[768,768]{1,0:T(8,128)} %get-tuple-element.22), channel_id=1, source_target_pairs={{0,16},{16,0},{1,17},{17,1},{2,18},{18,2},{3,19},{19,3},{4,20},{20... | collective-permute-start | bytes 7077896 | tf_op jit(solution)/shard_map/ppermute | solution.py:25
  116.3 3.1 %copy-start.1 = (f32[768,768]{1,0:T(8,128)S(1)}, f32[768,768]{1,0:T(8,128)}, u32[]{:S(2)}) copy-start(f32[768,768]{1,0:T(8,128)} %get-tuple-element.21) | copy-start | bytes 7077892
  120.8 1.7 %copy-start = (f32[768,768]{1,0:T(8,128)S(1)}, f32[768,768]{1,0:T(8,128)}, u32[]{:S(2)}) copy-start(f32[768,768]{1,0:T(8,128)} %get-tuple-element.22) | copy-start | bytes 7077892
  147.1 15.9 %all-to-all-start.4 = ((f32[4,16,1536]{2,1,0:T(8,128)}), f32[4,16,1536]{2,1,0:T(8,128)S(1)}, u32[]{:S(2)}, u32[]{:S(2)}) async-start(f32[4,16,1536]{2,1,0:T(8,128)} %bitcast.9), calls=%async_computation.4 | async-start | bytes 786432 | tf_op jit(solution)/shard_map/all_to_all | solution.py:251
  154.1 3.1 %collective-permute-start.2 = (f32[16,768]{1,0:T(8,128)S(1)}, f32[16,768]{1,0:T(8,128)S(1)}, u32[]{:S(2)}, u32[]{:S(2)}) collective-permute-start(f32[16,768]{1,0:T(8,128)S(1)} %slice.39), channel_id=1, source_target_pairs={{0,16},{16,0},{1,17},{17,1},{2,18},{18,2},{3,19},{19,3},{4,20},{20... | collective-permute-start | bytes 147464 | tf_op jit(solution)/shard_map/ppermute | solution.py:25

commit v9 on v8

--- a/solution.py
+++ b/solution.py
@@ -82,7 +82,7 @@
     width, block = coeffs.shape
     owned = states.shape[0]
     face = faces.shape[1]
-    tile = 256
+    tile = 768
     fixed = lambda shape: pl.BlockSpec(shape, lambda i: (0, 0))
     return pl.pallas_call(
         rotate_kernel,

time: 165 us -> 164 us (level)
  waiting for transfers between devices: 14 us -> 11.1 us
  blocking collectives: 70.8 us -> 73.2 us
    all_to_all x3, waiting for transfers between devices: 12.8 us -> 9.92 us  [swap(): return lax.all_to_all(pieces, axis, 0, 0, tiled=True)]
    all_to_all x2, blocking collectives: 47.4 us -> 49.2 us  [swap(): return lax.all_to_all(pieces, axis, 0, 0, tiled=True)]
where the time goes in v9:
time: 164 us; the launch traced here: 162 us
  blocking collectives  73.2 us (45%)
  starting transfers between devices  37.7 us (23%)
  Pallas kernels  27 us (16%)
  waiting for transfers between devices  11.1 us (7%)
  matrix products  7.08 us (4%)
  other arithmetic  3.29 us (2%)
  local copies, waits for them, and re-layouts  1.94 us (1%)
    all_to_all x2, blocking collectives, swap(): return lax.all_to_all(pieces, axis, 0, 0, tiled=True)  49.2 us
    all_to_all x3, starting transfers between devices, swap(): return lax.all_to_all(pieces, axis, 0, 0, tiled=True)  26.2 us
    all_gather x1, blocking collectives, local(): group = lax.all_gather(both, 'zh', axis=0, tiled=True)  24 us
    pallas_call x1, Pallas kernels, assemble(): pl.pallas_call(assemble_kernel, out_shape=[jax.ShapeDtypeStruct((total, d...  9.99 us
    all_to_all x3, waiting for transfers between devices, swap(): return lax.all_to_all(pieces, axis, 0, 0, tiled=True)  9.92 us
    pallas_call x1, Pallas kernels, apply_cells(): pl.pallas_call(apply_kernel, grid=(width // tile,), in_specs=[fixed((owne...  8.17 us
    ppermute x3, starting transfers between devices, ring(): lax.ppermute(shard, axis, [(i, (i + by) % length) for i in range(length)])  7.2 us
    dot_general x4, matrix products, local(): jnp.dot(part, weight, precision=HIGH, preferred_element_type=F32)  7.08 us
  transfers between devices with their start and end apart: 8, of which 4 were waited for; matrix products, arithmetic and copies ran while one was open for 4% of the time, Pallas kernels for 13%

profile of v9, /device:TPU:24, one launch (start us, length us, event | category | flops | bytes accessed | tf_op | source)
XLA Modules:
  0.0 162.1 jit_solution(2519099188940520843)
XLA Ops:
  0.6 6.0 %rotate.1 = (f32[512,768]{1,0:T(8,128)}, f32[64,768]{1,0:T(8,128)}) custom-call(f32[768,512]{1,0:T(8,128)} %coeffs_ref.1, f32[768,768]{1,0:T(8,128)} %states_ref.5, s32[1,64]{1,0:T(1,128)} %bitcast.25), custom_call_target="tpu_custom_call" | custom-call | flops 1811939328 | bytes 6000000 | tf_op jit(solution)/shard_map/rotate/pallas_call | solution.py:87
  6.6 9.2 %all-to-all-start = ((f32[8,64,768]{2,1,0:T(8,128)}), f32[8,64,768]{2,1,0:T(8,128)S(1)}, u32[]{:S(2)}, u32[]{:S(2)}) async-start(f32[8,64,768]{2,1,0:T(8,128)} %bitcast.23), calls=%async_computation | async-start | bytes 3145728 | tf_op jit(solution)/shard_map/all_to_all | solution.py:251
  15.9 1.3 collective-permute-start
  17.2 10.0 %assemble.1 = (bf16[832,896]{1,0:T(8,128)(2,1)}, bf16[832,896]{1,0:T(8,128)(2,1)}) custom-call(s32[12,125]{1,0:T(8,128)} %connect_ref.1, f32[12,125,125]{2,1,0:T(8,128)} %cell_ref.1, f32[512,768]{1,0:T(8,128)} %get-tuple-element.13._), custom_call_target="tpu_custom_call" | custom-call | flops 8000000000 | bytes 4000000 | tf_op jit(solution)/shard_map/assemble/pallas_call | solution.py:149
  27.2 0.7 copy-done.2
  27.9 2.9 %back.1 = f32[64,768]{1,0:T(8,128)} custom-call(bf16[832,896]{1,0:T(8,128)(2,1)} %get-tuple-element.14.top_ref.refs_2_, bf16[832,896]{1,0:T(8,128)(2,1)} %get-tuple-element.15.low_ref.refs_3_, f32[768,768]{1,0:T(8,128)} %states_ref.5, f32[64,768]{1,0:T(8,128)} %copy-done.2), custom_call_target="tpu_custom_call" | custom-call | flops 600000000 | bytes 4000000 | tf_op jit(solution)/shard_map/back/pallas_call | solution.py:188
  30.7 3.0 %collective-permute-start.1 = (f32[64,768]{1,0:T(8,128)}, f32[64,768]{1,0:T(8,128)S(1)}, u32[]{:S(2)}, u32[]{:S(2)}) collective-permute-start(f32[64,768]{1,0:T(8,128)} %back.1), channel_id=1, source_target_pairs={{0,16},{16,32},{32,48},{48,64},{64,80},{80,96},{96,112},{112,128},... | collective-permute-start | bytes 589832 | tf_op jit(solution)/shard_map/ppermute | solution.py:20
  33.8 1.6 all-to-all-done
  35.5 0.8 pad_maximum_fusion.1.refs_0_
  36.3 0.7 copy-done.3
  37.0 10.7 %all-to-all-start.1 = ((f32[4,16,1536]{2,1,0:T(8,128)}), f32[4,16,1536]{2,1,0:T(8,128)S(1)}, u32[]{:S(2)}, u32[]{:S(2)}) async-start(f32[4,16,1536]{2,1,0:T(8,128)} %bitcast.22), calls=%async_computation.1 | async-start | bytes 786432 | tf_op jit(solution)/shard_map/all_to_all | solution.py:251
  47.7 8.2 %apply.1 = (f32[768,768]{1,0:T(8,128)}, f32[768,768]{1,0:T(8,128)}) custom-call(bf16[832,896]{1,0:T(8,128)(2,1)} %get-tuple-element.18.top_ref, bf16[832,896]{1,0:T(8,128)(2,1)} %get-tuple-element.19.low_ref, f32[768,768]{1,0:T(8,128)} %states_ref.5, f32[64,768]{1,0:T(8,128)} %copy-done.2, f32[6,128]{1,0:T(8,128)} %bitcast.24, ...), custom_call_target="tpu_custom_call" | custom-call | flops 7000000000 | bytes 11000000 | tf_op jit(solution)/shard_map/apply/pallas_call | solution.py:222
  55.8 3.4 %collective-permute-start.3 = (f32[768,768]{1,0:T(8,128)}, f32[768,768]{1,0:T(8,128)}, u32[]{:S(2)}, u32[]{:S(2)}) collective-permute-start(f32[768,768]{1,0:T(8,128)} %get-tuple-element.21), channel_id=1, source_target_pairs={{0,16},{16,0},{1,17},{17,1},{2,18},{18,2},{3,19},{19,3},{4,20},{20... | collective-permute-start | bytes 7077896 | tf_op jit(solution)/shard_map/ppermute | solution.py:25
  59.2 1.9 %collective-permute-start.4 = (f32[768,768]{1,0:T(8,128)}, f32[768,768]{1,0:T(8,128)S(1)}, u32[]{:S(2)}, u32[]{:S(2)}) collective-permute-start(f32[768,768]{1,0:T(8,128)} %get-tuple-element.22), channel_id=1, source_target_pairs={{0,16},{16,0},{1,17},{17,1},{2,18},{18,2},{3,19},{19,3},{4,20},{20... | collective-permute-start | bytes 7077896 | tf_op jit(solution)/shard_map/ppermute | solution.py:25
  61.2 3.2 %all-to-all-done.1 = f32[4,16,1536]{2,1,0:T(8,128)S(1)} async-done(((f32[4,16,1536]{2,1,0:T(8,128)}), f32[4,16,1536]{2,1,0:T(8,128)S(1)}, u32[]{:S(2)}, u32[]{:S(2)}) %all-to-all-start.1) | async-done | bytes 393248 | tf_op jit(solution)/shard_map/all_to_all | solution.py:251
  64.4 24.0 %all_gather.3 = f32[64,1536]{1,0:T(8,128)S(1)} all-gather(f32[16,1536]{1,0:T(8,128)S(1)} %reduce_sum.46), channel_id=1, replica_groups=mesh['x'=4,'zl'=4,'core'=2,'y'=4,'zh'=4] {'zh'}, dimensions={0}, use_global_device_ids=true | all-gather | bytes 491520 | tf_op jit(solution)/shard_map/all_gather | solution.py:281
  88.5 0.2 broadcast_in_dim.2
  88.6 27.5 %all_to_all.25 = f32[4,64,1536]{2,1,0:T(8,128)S(1)} all-to-all(f32[4,64,1536]{2,1,0:T(8,128)S(1)} %broadcast_in_dim.2), channel_id=1, replica_groups=mesh['x'=4,'zl'=4,'core'=2,'y'=4,'zh'=4] {'y'}, dimensions={0} | all-to-all | bytes 3145728 | tf_op jit(solution)/shard_map/all_to_all | solution.py:251
  116.1 3.1 %fusion.2 = f32[256,768]{1,0:T(8,128)S(1)} fusion(f32[768,768]{1,0:T(8,128)} %collective-permute-done.3, f32[256,1536]{1,0:T(8,128)S(1)} %bitcast.16), kind=kOutput, calls=%fused_computation.5 | convolution fusion | flops 905969664 | bytes 3932160 | tf_op jit(solution)/shard_map/dot_general | solution.py:287
  119.2 1.4 convolution_add_fusion.1
  120.6 1.3 fusion
  121.9 0.4 copy-done
  122.3 1.4 convolution_add_fusion
  123.6 0.2 pad_maximum_fusion
  123.8 21.7 %all_to_all.26 = f32[4,64,1536]{2,1,0:T(8,128)S(1)} all-to-all(f32[4,64,1536]{2,1,0:T(8,128)S(1)} %bitcast.21), channel_id=1, replica_groups=mesh['x'=4,'zl'=4,'core'=2,'y'=4,'zh'=4] {'x'}, dimensions={0} | all-to-all | bytes 3145728 | tf_op jit(solution)/shard_map/all_to_all | solution.py:251
  145.5 0.8 reduce_sum.47
  146.4 6.2 %all-to-all-start.4 = ((f32[4,16,1536]{2,1,0:T(8,128)}), f32[4,16,1536]{2,1,0:T(8,128)S(1)}, u32[]{:S(2)}, u32[]{:S(2)}) async-start(f32[4,16,1536]{2,1,0:T(8,128)} %bitcast.9), calls=%async_computation.4 | async-start | bytes 786432 | tf_op jit(solution)/shard_map/all_to_all | solution.py:251
  152.6 1.9 %collective-permute-start.2 = (f32[16,768]{1,0:T(8,128)S(1)}, f32[16,768]{1,0:T(8,128)S(1)}, u32[]{:S(2)}, u32[]{:S(2)}) collective-permute-start(f32[16,768]{1,0:T(8,128)S(1)} %slice.39), channel_id=1, source_target_pairs={{0,16},{16,0},{1,17},{17,1},{2,18},{18,2},{3,19},{19,3},{4,20},{20... | collective-permute-start | bytes 147464 | tf_op jit(solution)/shard_map/ppermute | solution.py:25
  154.5 1.2 collective-permute-done.2
  155.7 0.6 pad_maximum_fusion.2
  156.4 5.1 %all-to-all-done.4 = f32[4,16,1536]{2,1,0:T(8,128)S(1)} async-done(((f32[4,16,1536]{2,1,0:T(8,128)}), f32[4,16,1536]{2,1,0:T(8,128)S(1)}, u32[]{:S(2)}, u32[]{:S(2)}) %all-to-all-start.4) | async-done | bytes 393248 | tf_op jit(solution)/shard_map/all_to_all | solution.py:251
  161.5 0.7 slice_reduce_fusion
  (17 shorter events, 0.2 us)
Async XLA Ops:
  6.6 9.2 %copy-start.4 = (f32[64,768]{1,0:T(8,128)S(1)}, f32[64,768]{1,0:T(8,128)}, u32[]{:S(2)}) copy-start(f32[64,768]{1,0:T(8,128)} %get-tuple-element.16) | copy-start | bytes 589828
  6.6 28.7 %all-to-all-start = ((f32[8,64,768]{2,1,0:T(8,128)}), f32[8,64,768]{2,1,0:T(8,128)S(1)}, u32[]{:S(2)}, u32[]{:S(2)}) async-start(f32[8,64,768]{2,1,0:T(8,128)} %bitcast.23), calls=%async_computation | async-start | bytes 3145728 | tf_op jit(solution)/shard_map/all_to_all | solution.py:251
  15.9 11.3 %collective-permute-start = (f32[64,768]{1,0:T(8,128)S(1)}, f32[64,768]{1,0:T(8,128)S(1)}, u32[]{:S(2)}, u32[]{:S(2)}) collective-permute-start(f32[64,768]{1,0:T(8,128)S(1)} %copy-done.4), channel_id=1, source_target_pairs={{16,0},{32,16},{48,32},{64,48},{80,64},{96,80},{112,96},{128,112},... | collective-permute-start | bytes 589832 | tf_op jit(solution)/shard_map/ppermute | solution.py:20
  27.2 0.7 copy-start.2
  30.7 5.5 %collective-permute-start.1 = (f32[64,768]{1,0:T(8,128)}, f32[64,768]{1,0:T(8,128)S(1)}, u32[]{:S(2)}, u32[]{:S(2)}) collective-permute-start(f32[64,768]{1,0:T(8,128)} %back.1), channel_id=1, source_target_pairs={{0,16},{16,32},{32,48},{48,64},{64,80},{80,96},{96,112},{112,128},... | collective-permute-start | bytes 589832 | tf_op jit(solution)/shard_map/ppermute | solution.py:20
  36.3 0.7 copy-start.3
  37.0 27.4 %all-to-all-start.1 = ((f32[4,16,1536]{2,1,0:T(8,128)}), f32[4,16,1536]{2,1,0:T(8,128)S(1)}, u32[]{:S(2)}, u32[]{:S(2)}) async-start(f32[4,16,1536]{2,1,0:T(8,128)} %bitcast.22), calls=%async_computation.1 | async-start | bytes 786432 | tf_op jit(solution)/shard_map/all_to_all | solution.py:251
  55.8 60.3 %collective-permute-start.3 = (f32[768,768]{1,0:T(8,128)}, f32[768,768]{1,0:T(8,128)}, u32[]{:S(2)}, u32[]{:S(2)}) collective-permute-start(f32[768,768]{1,0:T(8,128)} %get-tuple-element.21), channel_id=1, source_target_pairs={{0,16},{16,0},{1,17},{17,1},{2,18},{18,2},{3,19},{19,3},{4,20},{20... | collective-permute-start | bytes 7077896 | tf_op jit(solution)/shard_map/ppermute | solution.py:25
  59.2 61.4 %collective-permute-start.4 = (f32[768,768]{1,0:T(8,128)}, f32[768,768]{1,0:T(8,128)S(1)}, u32[]{:S(2)}, u32[]{:S(2)}) collective-permute-start(f32[768,768]{1,0:T(8,128)} %get-tuple-element.22), channel_id=1, source_target_pairs={{0,16},{16,0},{1,17},{17,1},{2,18},{18,2},{3,19},{19,3},{4,20},{20... | collective-permute-start | bytes 7077896 | tf_op jit(solution)/shard_map/ppermute | solution.py:25
  116.1 3.1 %copy-start.1 = (f32[768,768]{1,0:T(8,128)S(1)}, f32[768,768]{1,0:T(8,128)}, u32[]{:S(2)}) copy-start(f32[768,768]{1,0:T(8,128)} %get-tuple-element.21) | copy-start | bytes 7077892
  120.6 1.7 %copy-start = (f32[768,768]{1,0:T(8,128)S(1)}, f32[768,768]{1,0:T(8,128)}, u32[]{:S(2)}) copy-start(f32[768,768]{1,0:T(8,128)} %get-tuple-element.22) | copy-start | bytes 7077892
  146.4 15.1 %all-to-all-start.4 = ((f32[4,16,1536]{2,1,0:T(8,128)}), f32[4,16,1536]{2,1,0:T(8,128)S(1)}, u32[]{:S(2)}, u32[]{:S(2)}) async-start(f32[4,16,1536]{2,1,0:T(8,128)} %bitcast.9), calls=%async_computation.4 | async-start | bytes 786432 | tf_op jit(solution)/shard_map/all_to_all | solution.py:251
  152.6 3.1 %collective-permute-start.2 = (f32[16,768]{1,0:T(8,128)S(1)}, f32[16,768]{1,0:T(8,128)S(1)}, u32[]{:S(2)}, u32[]{:S(2)}) collective-permute-start(f32[16,768]{1,0:T(8,128)S(1)} %slice.39), channel_id=1, source_target_pairs={{0,16},{16,0},{1,17},{17,1},{2,18},{18,2},{3,19},{19,3},{4,20},{20... | collective-permute-start | bytes 147464 | tf_op jit(solution)/shard_map/ppermute | solution.py:25
